TPU v7x, 512 devices: a whole 4x8x8 slice. The times are simulated.
512 devices in a mesh: expert: 128 (over z, y, core), tensor: 4 (over x).
Axes of the slice: x: 4, y: 8, z: 8, core: 2. Of those that a mesh axis runs over, the one named last changes fastest.
Arguments:
- cotangent: bfloat16 [16384, 2560], P('expert', 'tensor'), may hold values from -6 to 6
- route_first: int32 [16384, 6], P('expert'), may hold values from 0 to 127, all different within a row; in each aligned block of 128 rows (0 to 127, 128 to 255, ...) at most 9 rows name the same one
- gates_first: float32 [16384, 6], P('expert'), may hold values from 0.05 to 0.4
- hidden_first: bfloat16 [128, 1152, 768], P('expert', None, 'tensor'), may hold values from -6 to 6
- route_second: int32 [16384, 6], P('expert'), may hold values from 0 to 127, all different within a row; in each aligned block of 128 rows (0 to 127, 128 to 255, ...) at most 9 rows name the same one
- gates_second: float32 [16384, 6], P('expert'), may hold values from 0.05 to 0.4
- hidden_second: bfloat16 [128, 1152, 768], P('expert', None, 'tensor'), may hold values from -6 to 6
- master: float32 [128, 768, 2560], P('expert', None, 'tensor'), may hold values from -0.21875 to 0.21875
- moment_one: bfloat16 [128, 768, 2560], P('expert', None, 'tensor'), may hold values from -6 to 6
- moment_two: bfloat16 [128, 768, 2560], P('expert', None, 'tensor'), may hold values from 0.5 to 8
- old_plan: int32 [128], replicated, may hold values from 0 to 127, as said below
- new_plan: int32 [128], replicated, may hold values from 0 to 127, as said below
Outputs:
- layer_output: bfloat16 [16384, 2560], P('expert', 'tensor')
Inputs may be any that keep to these rules, and one draw needn't show every extreme that they name: `route_first`: in the rows of one device no expert is named by more than 9 rows. `route_second`: in the rows of one device no expert is named by more than 9 rows. `old_plan`: a permutation: every expert stands in exactly one slot. `new_plan`: a permutation equal to old_plan except in 8 slots, whose experts trade places along one cycle.
All inputs are finite; a program needn't handle non-finite values.
Results may differ from a plain program's by a relative error of at most 0.0011.
The roundings to bfloat16 on the way count: a program that leaves them out, or rounds other values in their place, can miss the bound.
Values may be sent and summed in bfloat16 or wider, within the bound.
No kernel may reach another device: no remote copies, remote signals or barrier semaphores. Data moves between devices by JAX's collectives and lax.ppermute only.
A program may use at most 64 MiB of HBM per device.

v0:
```python
import jax
import jax.numpy as jnp
from jax import lax
from jax.sharding import PartitionSpec as P

BETA_ONE = 0.9
BETA_TWO = 0.95
CORRECT_ONE = 1.0 - 0.9**10
CORRECT_TWO = 1.0 - 0.95**10
LEARN_RATE = 0.04
WEIGHT_DECAY = 0.1
EPSILON = 1e-08


def lookup(lookup_table, lookup_keys, labels):
    return jnp.sum(
        jnp.where(lookup_keys[:, None] == labels[None, :], lookup_table[None, :], 0), axis=1
    )


def inverse(placement_plan, labels):
    return jnp.sum(
        jnp.where(placement_plan[None, :] == labels[:, None], labels[None, :], 0), axis=1
    )


def buffer_index(routing, placement_plan, capacity):
    labels = jnp.arange(placement_plan.shape[0], dtype=jnp.int32)
    flattened = routing.reshape(-1)
    onehot = (flattened[:, None] == labels[None, :]).astype(jnp.int32)
    before = jnp.cumsum(onehot, axis=0) - onehot
    ranking = jnp.sum(before * onehot, axis=1)
    slot_ids = jnp.sum(onehot * inverse(placement_plan, labels)[None, :], axis=1)
    return slot_ids * capacity + ranking


def adam_weight(master, moment_one, moment_two, gradient):
    moment_new = BETA_ONE * moment_one.astype(jnp.float32) + (1.0 - BETA_ONE) * gradient
    second = BETA_TWO * moment_two.astype(jnp.float32) + (1.0 - BETA_TWO) * gradient * gradient
    ratio = moment_new / CORRECT_ONE / (jnp.sqrt(second / CORRECT_TWO) + EPSILON)
    updated = master - LEARN_RATE * (ratio + WEIGHT_DECAY * master)
    return updated.astype(jnp.bfloat16)


def shards(
    cotangent,
    route_first,
    gates_first,
    hidden_first,
    route_second,
    gates_second,
    hidden_second,
    master,
    moment_one,
    moment_two,
    old_plan,
    new_plan,
):
    expert_count = lax.axis_size("expert")
    rows_total = hidden_first.shape[1]
    capacity = rows_total // expert_count
    columns = cotangent.shape[1]
    labels = jnp.arange(old_plan.shape[0], dtype=jnp.int32)
    pair_count = route_first.shape[0] * route_first.shape[1]
    scaled = (gates_first[:, :, None] * cotangent[:, None, :].astype(jnp.float32)).astype(
        jnp.bfloat16
    )
    scaled = scaled.reshape(pair_count, columns)
    target = buffer_index(route_first, old_plan, capacity)
    outgoing = jnp.zeros((rows_total, columns), jnp.bfloat16).at[target].set(scaled)
    outgoing = outgoing.reshape(expert_count, capacity, columns)
    arrived = lax.all_to_all(outgoing, "expert", split_axis=0, concat_axis=0, tiled=True).reshape(
        rows_total, columns
    )
    local_second = hidden_second[0]
    full_first, full_second = (
        lax.all_gather(hidden_first[0], "tensor", axis=1, tiled=True),
        lax.all_gather(local_second, "tensor", axis=1, tiled=True),
    )
    gradient = lax.dot_general(
        full_first, arrived, (((0,), (0,)), ((), ())), preferred_element_type=jnp.float32
    )
    weight = adam_weight(master[0], moment_one[0], moment_two[0], gradient)
    source_slot = lookup(inverse(old_plan, labels), new_plan, labels)
    pieces = weight.reshape(expert_count, -1)
    spread = lax.all_to_all(pieces, "expert", split_axis=0, concat_axis=0, tiled=True)
    spread = jnp.take(spread, source_slot, axis=0)
    weight = lax.all_to_all(spread, "expert", split_axis=0, concat_axis=0, tiled=True).reshape(
        master.shape[1:]
    )
    produced = jnp.dot(full_second, weight, preferred_element_type=jnp.float32).astype(jnp.bfloat16)
    produced = produced.reshape(expert_count, capacity, columns)
    returned = lax.all_to_all(produced, "expert", split_axis=0, concat_axis=0, tiled=True).reshape(
        rows_total, columns
    )
    positions = buffer_index(route_second, new_plan, capacity)
    picked = jnp.take(returned, positions, axis=0).reshape(
        route_second.shape[0], route_second.shape[1], columns
    )
    summed = jnp.zeros((route_second.shape[0], columns), jnp.float32)
    for column in range(route_second.shape[1]):
        summed = summed + gates_second[:, column, None] * picked[:, column, :].astype(jnp.float32)
    return summed.astype(jnp.bfloat16)


def solution(mesh):
    placed = (
        P("expert", "tensor"),
        P("expert", None),
        P("expert", None),
        P("expert", None, "tensor"),
        P("expert", None),
        P("expert", None),
        P("expert", None, "tensor"),
        P("expert", None, "tensor"),
        P("expert", None, "tensor"),
        P("expert", None, "tensor"),
        P(),
        P(),
    )
    return jax.shard_map(
        shards, mesh=mesh, in_specs=placed, out_specs=P("expert", "tensor"), check_vma=False
    )
```

profile of v0, /device:TPU:12, one launch (start us, length us, event | category | flops | bytes accessed | tf_op | source)
XLA Modules:
  0.0 307.8 jit_solution(8022781108929787953)
XLA Ops:
  6.5 0.8 copy.85
  8.9 1.4 mul.181
  10.6 9.8 %scatter_custom_fusion = bf16[1152,640]{1,0:T(8,128)(2,1)S(1)} fusion(s32[768]{0:T(1024)S(1)} %fusion.34, f32[768,640]{1,0:T(8,128)} %mul.181, f32[768]{0:T(1024)S(1)} %mul.178, bf16[]{:T(256)} %constant.54.clone.1), kind=kCustom, calls=%fused_computation.23 | custom fusion | flops 983040 | bytes 3444738 | tf_op jit(solution)/shard_map/scatter | solution.py:70
  20.4 1.8 reshape.198
  22.2 17.4 %all-to-all-start = ((bf16[128,9,640]{2,1,0:T(8,128)(2,1)}), bf16[128,9,640]{2,1,0:T(8,128)(2,1)S(1)}, u32[]{:S(2)}, u32[]{:S(2)}) async-start(bf16[128,9,640]{2,1,0:T(8,128)(2,1)} %reshape.198), calls=%async_computation | async-start | bytes 5242880 | tf_op jit(solution)/shard_map/all_to_all | solution.py:72
  40.3 2.9 copy.83
  43.2 2.3 copy.84
  45.5 2.3 copy.90
  47.8 57.1 %all-to-all-done = bf16[128,9,640]{2,1,0:T(8,128)(2,1)S(1)} async-done(((bf16[128,9,640]{2,1,0:T(8,128)(2,1)}), bf16[128,9,640]{2,1,0:T(8,128)(2,1)S(1)}, u32[]{:S(2)}, u32[]{:S(2)}) %all-to-all-start) | async-done | bytes 1474592 | tf_op jit(solution)/shard_map/all_to_all | solution.py:72
  104.9 1.5 reshape.199
  106.4 5.9 %fusion.9 = bf16[768,640]{0,1:T(8,128)(2,1)S(1)} fusion(f32[1,768,640]{1,2,0:T(8,128)} %copy.83, bf16[1,768,640]{1,2,0:T(8,128)(2,1)} %copy.90, bf16[1,768,640]{1,2,0:T(8,128)(2,1)} %copy.84, bf16[1152,640]{1,0:T(8,128)(2,1)} %reshape.199, bf16[1,1152,768]{1,2,0:T(8,128)(2,1)} %all-gather.5.cloned.1.call-done), kind=kOutput, calls=%fused_computation.17 | convolution fusion | flops 1141309440 | bytes 8159232 | tf_op jit(solution)/shard_map/dot_general | solution.py:80
  113.9 6.6 %reduce.5 = bf16[128,3840]{1,0:T(8,128)(2,1)S(1)} reduce(bf16[128,1,3840]{2,1,0:T(2,128)(2,1)S(1)} %all_to_all.24, bf16[]{:T(256)} %broadcast.186), dimensions={1}, to_apply=%all_to_all.24.reduce_sub_computation | reduce | bytes 1966082 | tf_op jit(solution)/shard_map/all_to_all | solution.py:86
  120.5 1.2 reshape.240
  121.7 16.7 %all-to-all-start.1 = ((bf16[128,2,1920]{2,1,0:T(2,128)(2,1)}), bf16[128,2,1920]{2,1,0:T(2,128)(2,1)S(1)}, u32[]{:S(2)}, u32[]{:S(2)}) async-start(bf16[128,2,1920]{2,1,0:T(2,128)(2,1)} %reshape.240), calls=%async_computation.1 | async-start | bytes 1966080 | tf_op jit(solution)/shard_map/all_to_all | solution.py:86
  138.5 0.7 all-gather.7.cloned.1.call-update
  139.4 28.0 %all-to-all-done.1 = bf16[128,2,1920]{2,1,0:T(2,128)(2,1)S(1)} async-done(((bf16[128,2,1920]{2,1,0:T(2,128)(2,1)}), bf16[128,2,1920]{2,1,0:T(2,128)(2,1)S(1)}, u32[]{:S(2)}, u32[]{:S(2)}) %all-to-all-start.1) | async-done | bytes 983072 | tf_op jit(solution)/shard_map/all_to_all | solution.py:86
  167.5 0.8 reshape.241
  168.4 1.2 gather_fusion
  169.7 1.4 reduce.6
  171.4 35.7 %all_to_all.29 = bf16[128,2,1920]{2,1,0:T(2,128)(2,1)S(1)} all-to-all(bf16[128,2,1920]{2,1,0:T(2,128)(2,1)S(1)} %reshape.242), channel_id=1, replica_groups=mesh['expert'=128,'tensor'=4] {'expert'}, dimensions={0} | all-to-all | bytes 1966080 | tf_op jit(solution)/shard_map/all_to_all | solution.py:88
  207.1 0.8 reshape.243
  208.0 6.0 %reduce.1 = bf16[128,3840]{1,0:T(8,128)(2,1)S(1)} reduce(bf16[128,1,3840]{2,1,0:T(2,128)(2,1)S(1)} %reshape.243, bf16[]{:T(256)} %constant.69), dimensions={1}, to_apply=%all_to_all.22.reduce_sub_computation | reduce | bytes 1966082 | tf_op jit(solution)/shard_map/all_to_all | solution.py:88
  213.9 0.9 reshape.200
  214.9 2.9 fusion
  217.8 0.9 copy.94
  218.8 1.8 reshape.201
  220.6 6.8 %all-to-all-start.3 = ((bf16[128,9,640]{2,1,0:T(8,128)(2,1)}), bf16[128,9,640]{2,1,0:T(8,128)(2,1)}, u32[]{:S(2)}, u32[]{:S(2)}) async-start(bf16[128,9,640]{2,1,0:T(8,128)(2,1)} %reshape.201), calls=%async_computation.3 | async-start | bytes 5242880 | tf_op jit(solution)/shard_map/all_to_all | solution.py:93
  228.9 63.2 %all-to-all-done.3 = bf16[128,9,640]{2,1,0:T(8,128)(2,1)} async-done(((bf16[128,9,640]{2,1,0:T(8,128)(2,1)}), bf16[128,9,640]{2,1,0:T(8,128)(2,1)}, u32[]{:S(2)}, u32[]{:S(2)}) %all-to-all-start.3) | async-done | bytes 1474592 | tf_op jit(solution)/shard_map/all_to_all | solution.py:93
  292.2 2.8 reshape.202
  295.0 2.8 gather_fusion.1
  298.4 1.5 fusion.37
  299.9 0.9 fusion.27
  (60 shorter events, 6.9 us)
Async XLA Ops:
  6.5 1.6 copy-start.5
  6.5 2.2 copy-start
  8.9 1.5 copy-start.1
  22.2 82.6 %all-to-all-start = ((bf16[128,9,640]{2,1,0:T(8,128)(2,1)}), bf16[128,9,640]{2,1,0:T(8,128)(2,1)S(1)}, u32[]{:S(2)}, u32[]{:S(2)}) async-start(bf16[128,9,640]{2,1,0:T(8,128)(2,1)} %reshape.198), calls=%async_computation | async-start | bytes 5242880 | tf_op jit(solution)/shard_map/all_to_all | solution.py:72
  39.6 66.8 %all-gather.5.cloned.1.call-start = ((), (), s32[]{:S(2)}) async-start(), calls=%async_computation.4 | async-start | bytes 2211840 | tf_op jit(solution)/shard_map/all_gather | solution.py:77
  120.5 18.7 %copy-start.4 = (s32[128]{0:T(128)S(1)}, s32[128]{0:T(128)}, u32[]{:S(2)}) copy-start(s32[128]{0:T(128)} %param.23) | copy-start | bytes 1540
  121.7 45.7 %all-to-all-start.1 = ((bf16[128,2,1920]{2,1,0:T(2,128)(2,1)}), bf16[128,2,1920]{2,1,0:T(2,128)(2,1)S(1)}, u32[]{:S(2)}, u32[]{:S(2)}) async-start(bf16[128,2,1920]{2,1,0:T(2,128)(2,1)} %reshape.240), calls=%async_computation.1 | async-start | bytes 1966080 | tf_op jit(solution)/shard_map/all_to_all | solution.py:86
  138.5 76.4 %all-gather.7.cloned.1.call-start = ((), (), s32[]{:S(2)}) async-start(), calls=%async_computation.5 | async-start | bytes 2211840 | tf_op jit(solution)/shard_map/all_gather | solution.py:78
  220.6 6.8 %copy-start.2 = (s32[128,6]{0,1:T(8,128)S(1)}, s32[128,6]{0,1:T(8,128)}, u32[]{:S(2)}) copy-start(s32[128,6]{0,1:T(8,128)} %param.16) | copy-start | bytes 9220
  220.6 71.6 %all-to-all-start.3 = ((bf16[128,9,640]{2,1,0:T(8,128)(2,1)}), bf16[128,9,640]{2,1,0:T(8,128)(2,1)}, u32[]{:S(2)}, u32[]{:S(2)}) async-start(bf16[128,9,640]{2,1,0:T(8,128)(2,1)} %reshape.201), calls=%async_computation.3 | async-start | bytes 5242880 | tf_op jit(solution)/shard_map/all_to_all | solution.py:93
  227.4 1.5 copy-start.3
Sparse Core Ops, SparseCore 0:
  42.5 33.0 all-gather.4
  141.4 31.9 all-gather.6
where the time goes:
time: 310 us; the launch traced here: 308 us
  waiting for transfers between devices  149 us (48%)
  starting transfers between devices  41.2 us (13%)
  blocking collectives  35.7 us (12%)
  local copies, waits for them, and re-layouts  30.2 us (10%)
  other arithmetic  28.3 us (9%)
  between operations  14.1 us (5%)
  matrix products  8.83 us (3%)
    all_to_all x1, waiting for transfers between devices, shards(): lax.all_to_all(produced, 'expert', split_axis=0, concat_axis=0, tiled=True)  63.2 us
    all_to_all x1, waiting for transfers between devices, shards(): lax.all_to_all(outgoing, 'expert', split_axis=0, concat_axis=0, tiled=True)  57.1 us
    all_to_all x1, blocking collectives, shards(): lax.all_to_all(spread, 'expert', split_axis=0, concat_axis=0, tiled=True)  35.7 us
    all_to_all x1, waiting for transfers between devices, shards(): lax.all_to_all(pieces, 'expert', split_axis=0, concat_axis=0, tiled=True)  28 us
    all_to_all x1, starting transfers between devices, shards(): lax.all_to_all(outgoing, 'expert', split_axis=0, concat_axis=0, tiled=True)  17.4 us
    all_to_all x1, starting transfers between devices, shards(): lax.all_to_all(pieces, 'expert', split_axis=0, concat_axis=0, tiled=True)  16.7 us
    unnamed x23, local copies, waits for them, and re-layouts  11.7 us
    scatter x1, other arithmetic, shards(): jnp.zeros((rows_total, columns), jnp.bfloat16).at[target].set(scaled)  9.82 us
  transfers between devices with their start and end apart: 5, of which 3 were waited for; matrix products, arithmetic and copies ran while one was open for 7% of the time, Pallas kernels for 0%

commit v1 on v0

v1 whole, which is shorter than its diff:
```python
import jax
import jax.numpy as jnp
from jax import lax
from jax.experimental import pallas as pl
from jax.experimental.pallas import tpu as pltpu
from jax.sharding import PartitionSpec as P

BETA_ONE = 0.9
BETA_TWO = 0.95
CORRECT_ONE = 1.0 - 0.9**10
CORRECT_TWO = 1.0 - 0.95**10
LEARN_RATE = 0.04
WEIGHT_DECAY = 0.1
EPSILON = 1e-08

EXP = 128
TOK = 128
TOP = 6
CAP = 9
ROWS = EXP * CAP
MAIN = EXP * 8
HID = 768
HPART = 192
COLS = 640
WIDE = 768
PIECES = 108
PROWS = PIECES * 16
NONE = 99.0
VMEM_LIMIT = 48 * 1024 * 1024
F32 = jnp.float32
BF16 = jnp.bfloat16

NN = (((1,), (0,)), ((), ()))
NT = (((1,), (1,)), ((), ()))


def params():
    return pltpu.CompilerParams(vmem_limit_bytes=VMEM_LIMIT)


def iota(shape, dim):
    return lax.broadcasted_iota(jnp.int32, shape, dim)


def mm(a, b, dims=NN):
    return lax.dot_general(a, b, dims, preferred_element_type=F32)


def thirds(x):
    high = x.astype(BF16)
    rest = x - high.astype(F32)
    mid = rest.astype(BF16)
    low = (rest - mid.astype(F32)).astype(BF16)
    return high, mid, low


def routed(route, gates, plan):
    diag = iota((EXP, EXP), 0) == iota((EXP, EXP), 1)
    column = jnp.sum(jnp.where(diag, plan.astype(F32), 0.0), axis=1, keepdims=True)
    named = route.astype(F32)
    member = jnp.zeros((EXP, TOK), F32)
    gate = jnp.zeros((EXP, TOK), F32)
    for k in range(TOP):
        same = named[k : k + 1, :] == column
        member = jnp.where(same, 1.0, member)
        gate = jnp.where(same, gates[k : k + 1, :], gate)
    earlier = (iota((TOK, TOK), 0) < iota((TOK, TOK), 1)).astype(F32).astype(BF16)
    rank = mm(member.astype(BF16), earlier)
    return jnp.where(member > 0.0, rank, NONE), gate


def onehot(mask):
    return jnp.where(mask, 1.0, 0.0).astype(BF16)


def main_pick(block):
    r = iota((128, 256), 0)
    return onehot(iota((128, 256), 1) == 16 * block + (r // 8) * 9 + r % 8)


def last_pick():
    return onehot(iota((EXP, ROWS), 1) == iota((EXP, ROWS), 0) * 9 + 8)


def prepare_second(h_ref, out_ref):
    first = h_ref[0:128, :]
    second = h_ref[128:192, :]
    blank = jnp.zeros_like(second)
    low = jnp.concatenate([second, blank], axis=0)
    high = jnp.concatenate([blank, second], axis=0)
    pick = [main_pick(b) for b in range(8)]
    last = last_pick()
    for b in range(8):
        win = slice(128 * b, 128 * b + 256)
        out_ref[128 * b : 128 * b + 128, :] = mm(pick[b], first[:, win], NT).astype(BF16)
    out_ref[MAIN:ROWS, :] = mm(last, first, NT).astype(BF16)
    for b in range(4):
        win_low = slice(128 * b, 128 * b + 256)
        win_high = slice(128 * b + 512, 128 * b + 768)
        both = mm(pick[b], low[:, win_low], NT) + mm(pick[b + 4], high[:, win_high], NT)
        out_ref[ROWS + 128 * b : ROWS + 128 * b + 128, :] = both.astype(BF16)
    both = mm(last[0:64], low, NT) + mm(last[64:128], high, NT)
    out_ref[ROWS + 512 : PROWS, :] = both.astype(BF16)
    out_ref[PROWS:, :] = jnp.zeros((128 * 16 - PROWS, 128), BF16)


def prepare_first(h_ref, out_ref):
    for b in range(8):
        win = slice(128 * b, 128 * b + 256)
        out_ref[:, 128 * b : 128 * b + 128] = mm(h_ref[:, win], main_pick(b), NT).astype(BF16)
    out_ref[:, MAIN:ROWS] = mm(h_ref[...], last_pick(), NT).astype(BF16)


def build_rows(route_ref, gates_ref, plan_ref, tokens_ref, out_ref, extra):
    rank, gate = routed(route_ref[...], gates_ref[...], plan_ref[...])
    tokens = tokens_ref[...]
    high, mid, low = thirds(gate)
    code = rank.astype(BF16)
    for b in range(4):
        r = iota((256, EXP), 0)
        spread = onehot(iota((256, EXP), 1) == 32 * b + r // 8)
        here = mm(spread, code) == (r % 8).astype(F32)
        gates_here = (mm(spread, high) + mm(spread, mid)) + mm(spread, low)
        scale = jnp.sum(jnp.where(here, gates_here, 0.0), axis=1, keepdims=True)
        rows = mm(onehot(here), tokens)
        out_ref[256 * b : 256 * b + 256, 0:COLS] = (scale * rows).astype(BF16)
    here = rank == 8.0
    scale = jnp.sum(jnp.where(here, gate, 0.0), axis=1, keepdims=True)
    rows = (scale * mm(onehot(here), tokens)).astype(BF16).astype(F32)
    extra[...] = jnp.zeros_like(extra)
    for q in range(5):
        extra[pl.ds(q, EXP, stride=8), :] = rows[:, 128 * q : 128 * q + 128]
    out_ref[:, COLS:WIDE] = extra[...].astype(BF16)


def choose(source_ref, in_ref, out_ref):
    def body(slot, carry):
        out_ref[slot] = in_ref[source_ref[slot]]
        return carry

    lax.fori_loop(0, EXP, body, 0, unroll=8)


def last_rows(payload_ref, extra):
    extra[...] = payload_ref[:, COLS:WIDE].astype(F32)
    return jnp.concatenate(
        [extra[pl.ds(q, EXP, stride=8), :] for q in range(5)], axis=1
    ).astype(BF16)


def update(hidden_ref, payload_ref, master_ref, one_ref, two_ref, out_ref, extra, last):
    @pl.when(pl.program_id(0) == 0)
    def _():
        last[...] = last_rows(payload_ref, extra)

    gradient = mm(hidden_ref[:, 0:MAIN], payload_ref[:, 0:COLS]) + mm(
        hidden_ref[:, MAIN:ROWS], last[...]
    )
    master = master_ref[...]
    moment_new = BETA_ONE * one_ref[...].astype(F32) + (1.0 - BETA_ONE) * gradient
    second = BETA_TWO * two_ref[...].astype(F32) + (1.0 - BETA_TWO) * gradient * gradient
    ratio = moment_new / CORRECT_ONE / (jnp.sqrt(second / CORRECT_TWO) + EPSILON)
    updated = master - LEARN_RATE * (ratio + WEIGHT_DECAY * master)
    out_ref[...] = updated.astype(BF16)


def forward(hidden_ref, weight_ref, out_ref, extra):
    def part(t, low, high):
        return weight_ref[t * HPART + low : t * HPART + high, :]

    blank = jnp.zeros((64, COLS), BF16)
    pairs = [jnp.concatenate([part(t, 0, 128), part(t + 1, 0, 128)], axis=0) for t in (0, 2)]
    lows = [
        jnp.concatenate([part(t, 128, 192), blank, part(t + 1, 128, 192), blank], axis=0)
        for t in (0, 2)
    ]
    highs = [
        jnp.concatenate([blank, part(t, 128, 192), blank, part(t + 1, 128, 192)], axis=0)
        for t in (0, 2)
    ]

    def rows(at, count, packed_at, weights):
        total = None
        for n, t in enumerate((0, 2)):
            one = jnp.concatenate(
                [hidden_ref[t, at : at + count, :], hidden_ref[t + 1, at : at + count, :]], axis=1
            )
            two = jnp.concatenate(
                [
                    hidden_ref[t, packed_at : packed_at + count, :],
                    hidden_ref[t + 1, packed_at : packed_at + count, :],
                ],
                axis=1,
            )
            term = mm(one, pairs[n]) + mm(two, weights[n])
            total = term if total is None else total + term
        return total.astype(BF16)

    for b in range(4):
        for half, weights in ((0, lows), (512, highs)):
            at = half + 128 * b
            out_ref[at : at + 128, 0:COLS] = rows(at, 128, ROWS + 128 * b, weights)
    last = jnp.concatenate(
        [
            rows(MAIN, 64, ROWS + 512, lows),
            rows(MAIN + 64, 64, ROWS + 512, highs),
        ],
        axis=0,
    ).astype(F32)
    extra[...] = jnp.zeros_like(extra)
    for q in range(5):
        extra[pl.ds(q, EXP, stride=8), :] = last[:, 128 * q : 128 * q + 128]
    out_ref[:, COLS:WIDE] = extra[...].astype(BF16)


def mixing(route_ref, gates_ref, plan_ref, main_ref, last_ref):
    rank, gate = routed(route_ref[...], gates_ref[...], plan_ref[...])
    rank = rank.T
    gate = gate.T
    code = rank.astype(BF16)
    parts = thirds(gate)
    for b in range(4):
        c = iota((EXP, 256), 1)
        spread = onehot(iota((EXP, 256), 0) == 32 * b + c // 8)
        here = mm(code, spread) == (c % 8).astype(F32)
        for n, part in enumerate(parts):
            main_ref[128 * n : 128 * n + 128, 256 * b : 256 * b + 256] = jnp.where(
                here, mm(part, spread), 0.0
            ).astype(BF16)
    for n, part in enumerate(parts):
        last_ref[128 * n : 128 * n + 128, :] = jnp.where(
            rank == 8.0, part.astype(F32), 0.0
        ).astype(BF16)


def combine(main_ref, last_ref, payload_ref, out_ref, extra):
    total = mm(main_ref[...], payload_ref[:, 0:COLS]) + mm(
        last_ref[...], last_rows(payload_ref, extra)
    )
    out_ref[...] = (total[0:128] + (total[128:256] + total[256:384])).astype(BF16)


def shape(*extents, dtype=BF16):
    return jax.ShapeDtypeStruct(extents, dtype)


def exchange(x):
    return lax.all_to_all(x, "expert", split_axis=0, concat_axis=0, tiled=True)


def shards(
    cotangent,
    route_first,
    gates_first,
    hidden_first,
    route_second,
    gates_second,
    hidden_second,
    master,
    moment_one,
    moment_two,
    old_plan,
    new_plan,
):
    labels = jnp.arange(EXP, dtype=jnp.int32)
    plan = old_plan.reshape(1, EXP)
    source = jnp.sum(
        jnp.where(new_plan[None, :] == old_plan[:, None], labels[None, :], 0), axis=1
    )
    extra = pltpu.VMEM((MAIN, 128), F32)

    with jax.named_scope("second_hidden_out"):
        pieces = pl.pallas_call(
            prepare_second, out_shape=shape(EXP * 16, 128), compiler_params=params()
        )(hidden_second[0].T)
        spread = exchange(pieces.reshape(EXP, 16, 128))

    with jax.named_scope("dispatch"):
        rows = pl.pallas_call(
            build_rows,
            out_shape=shape(MAIN, WIDE),
            scratch_shapes=[extra],
            compiler_params=params(),
        )(route_first.T, gates_first.T, plan, cotangent)
        arrived = exchange(rows.reshape(EXP, 8, WIDE)).reshape(MAIN, WIDE)

    with jax.named_scope("first_hidden"):
        first = pl.pallas_call(
            prepare_first, out_shape=shape(HPART, ROWS), compiler_params=params()
        )(hidden_first[0].T)
        first = lax.all_gather(first, "tensor", axis=0, tiled=True)

    with jax.named_scope("second_hidden_in"):
        chosen = pl.pallas_call(
            choose,
            out_shape=shape(EXP, 16, 128),
            in_specs=[
                pl.BlockSpec(memory_space=pltpu.SMEM),
                pl.BlockSpec(memory_space=pltpu.VMEM),
            ],
            compiler_params=params(),
        )(source, spread)
        mine = exchange(chosen)[:PIECES].reshape(PROWS, 128)
        second = lax.all_gather(mine, "tensor", axis=0)

    with jax.named_scope("mixing"):
        mix, mix_last = pl.pallas_call(
            mixing,
            out_shape=(shape(3 * TOK, MAIN), shape(3 * TOK, EXP)),
            compiler_params=params(),
        )(route_second.T, gates_second.T, plan)

    with jax.named_scope("update"):
        step = 128
        weight = pl.pallas_call(
            update,
            grid=(HID // step,),
            in_specs=[
                pl.BlockSpec((step, ROWS), lambda i: (i, 0)),
                pl.BlockSpec((MAIN, WIDE), lambda i: (0, 0)),
                pl.BlockSpec((step, COLS), lambda i: (i, 0)),
                pl.BlockSpec((step, COLS), lambda i: (i, 0)),
                pl.BlockSpec((step, COLS), lambda i: (i, 0)),
            ],
            out_specs=pl.BlockSpec((step, COLS), lambda i: (i, 0)),
            out_shape=shape(HID, COLS),
            scratch_shapes=[extra, pltpu.VMEM((EXP, COLS), BF16)],
            compiler_params=params(),
        )(first, arrived, master[0], moment_one[0], moment_two[0])

    with jax.named_scope("forward"):
        produced = pl.pallas_call(
            forward,
            out_shape=shape(MAIN, WIDE),
            scratch_shapes=[extra],
            compiler_params=params(),
        )(second, weight)
        returned = exchange(produced.reshape(EXP, 8, WIDE)).reshape(MAIN, WIDE)

    with jax.named_scope("combine"):
        return pl.pallas_call(
            combine,
            out_shape=shape(TOK, COLS),
            scratch_shapes=[extra],
            compiler_params=params(),
        )(mix, mix_last, returned)


def solution(mesh):
    placed = (
        P("expert", "tensor"),
        P("expert", None),
        P("expert", None),
        P("expert", None, "tensor"),
        P("expert", None),
        P("expert", None),
        P("expert", None, "tensor"),
        P("expert", None, "tensor"),
        P("expert", None, "tensor"),
        P("expert", None, "tensor"),
        P(),
        P(),
    )
    return jax.shard_map(
        shards, mesh=mesh, in_specs=placed, out_specs=P("expert", "tensor"), check_vma=False
    )
```

time: 310 us -> 194 us (0.63)
  the two profiles are of different devices: /device:TPU:12 before, /device:TPU:8 now
where the time goes in v1:
time: 194 us
  waiting for transfers between devices  122 us (63%)
  starting transfers between devices  35.4 us (18%)
  Pallas kernels  18.4 us (9%)
  between operations  13.5 us (7%)
  local copies, waits for them, and re-layouts  4.51 us (2%)
    all_to_all x4, waiting for transfers between devices, exchange(): return lax.all_to_all(x, 'expert', split_axis=0, concat_axis=0, tiled=True)  121 us
    all_to_all x4, starting transfers between devices, exchange(): return lax.all_to_all(x, 'expert', split_axis=0, concat_axis=0, tiled=True)  35.4 us
    pallas_call x1, Pallas kernels, shards(): pl.pallas_call(update, grid=(HID // step,), in_specs=[pl.BlockSpec((step,...  5.9 us
  transfers between devices with their start and end apart: 6, of which 4 were waited for; matrix products, arithmetic and copies ran while one was open for 0% of the time, Pallas kernels for 6%

profile of v1, /device:TPU:8, one launch (start us, length us, event | category | flops | bytes accessed | tf_op | source)
XLA Modules:
  0.0 193.6 jit_solution(6186294516196470426)
XLA Ops:
  6.5 0.0 all-gather.5.cloned.1.call-start
  6.5 1.0 copy-done.3
  7.6 1.3 first_hidden.1
  8.9 0.0 all-gather.5.cloned.1.call-update
  8.9 0.0 copy-done.4
  8.9 1.5 second_hidden_out.1
  10.4 17.5 %all-to-all-start = ((bf16[128,16,128]{2,1,0:T(8,128)(2,1)}), bf16[128,16,128]{2,1,0:T(8,128)(2,1)S(1)}, u32[]{:S(2)}, u32[]{:S(2)}) async-start(bf16[128,16,128]{2,1,0:T(8,128)(2,1)} %bitcast.5), calls=%async_computation | async-start | bytes 1048576 | tf_op jit(solution)/shard_map/second_hidden_out/all_to_all | solution.py:248
  27.9 0.0 copy-done.10
  27.9 0.0 copy-done.11
  27.9 0.2 select_reduce_fusion.source_ref
  28.1 20.0 %all-to-all-done.in_ref = bf16[128,16,128]{2,1,0:T(8,128)(2,1)S(1)} async-done(((bf16[128,16,128]{2,1,0:T(8,128)(2,1)}), bf16[128,16,128]{2,1,0:T(8,128)(2,1)S(1)}, u32[]{:S(2)}, u32[]{:S(2)}) %all-to-all-start) | async-done | bytes 524320 | tf_op jit(solution)/shard_map/second_hidden_out/all_to_all | solution.py:248
  48.1 1.6 second_hidden_in.1
  49.6 5.8 %all-to-all-start.1 = ((bf16[128,16,128]{2,1,0:T(8,128)(2,1)}), bf16[128,16,128]{2,1,0:T(8,128)(2,1)S(1)}, u32[]{:S(2)}, u32[]{:S(2)}) async-start(bf16[128,16,128]{2,1,0:T(8,128)(2,1)} %second_hidden_in.1), calls=%async_computation.1 | async-start | bytes 1048576 | tf_op jit(solution)/shard_map/second_hidden_in/all_to_all | solution.py:248
  55.4 0.0 copy-done.5
  55.5 2.5 %dispatch.1 = bf16[1024,768]{1,0:T(8,128)(2,1)} custom-call(s32[6,128]{1,0:T(8,128)S(1)} %bitcast.26, f32[6,128]{1,0:T(8,128)S(1)} %bitcast.27, s32[1,128]{1,0:T(1,128)S(1)} %bitcast.30, bf16[128,640]{1,0:T(8,128)(2,1)S(1)} %copy-done.5), custom_call_target="tpu_custom_call" | custom-call | tf_op jit(solution)/shard_map/dispatch/pallas_call | solution.py:279
  57.9 17.7 %all-to-all-done.1 = bf16[128,16,128]{2,1,0:T(8,128)(2,1)S(1)} async-done(((bf16[128,16,128]{2,1,0:T(8,128)(2,1)}), bf16[128,16,128]{2,1,0:T(8,128)(2,1)S(1)}, u32[]{:S(2)}, u32[]{:S(2)}) %all-to-all-start.1) | async-done | bytes 524320 | tf_op jit(solution)/shard_map/second_hidden_in/all_to_all | solution.py:248
  75.6 5.9 %all-to-all-start.2 = ((bf16[128,8,768]{2,1,0:T(8,128)(2,1)}), bf16[128,8,768]{2,1,0:T(8,128)(2,1)S(1)}, u32[]{:S(2)}, u32[]{:S(2)}) async-start(bf16[128,8,768]{2,1,0:T(8,128)(2,1)} %bitcast.11), calls=%async_computation.2 | async-start | bytes 3145728 | tf_op jit(solution)/shard_map/dispatch/all_to_all | solution.py:248
  81.6 0.0 all-gather.3.cloned.1.call-start
  81.6 0.8 slice.4
  82.4 0.0 all-gather.3.cloned.1.call-update
  82.4 0.0 all-gather.5.cloned.1.call-done.hidden_ref
  82.5 41.8 %all-to-all-done.2 = bf16[128,8,768]{2,1,0:T(8,128)(2,1)S(1)} async-done(((bf16[128,8,768]{2,1,0:T(8,128)(2,1)}), bf16[128,8,768]{2,1,0:T(8,128)(2,1)S(1)}, u32[]{:S(2)}, u32[]{:S(2)}) %all-to-all-start.2) | async-done | bytes 1572896 | tf_op jit(solution)/shard_map/dispatch/all_to_all | solution.py:248
  124.2 0.0 copy-done.1
  124.2 1.2 copy-done.2
  125.5 5.9 %update.1.weight_ref = bf16[768,640]{1,0:T(8,128)(2,1)S(1)} custom-call(bf16[768,1152]{1,0:T(8,128)(2,1)} %all-gather.5.cloned.1.call-done.hidden_ref, bf16[1024,768]{1,0:T(8,128)(2,1)S(1)} %bitcast.21, f32[768,640]{1,0:T(8,128)} %bitcast.32, bf16[768,640]{1,0:T(8,128)(2,1)S(1)} %bitcast.22, bf16[768,640]{1,0:T(8,128)(2,1)S(1)} %bitcast.23), custom_call_target="tpu_custom_call" | custom-call | tf_op jit(solution)/shard_map/update/pallas_call | solution.py:315
  131.4 0.0 all-gather.3.cloned.1.call-done.hidden_ref
  131.4 1.5 copy-done
  132.9 3.4 %forward.1 = bf16[1024,768]{1,0:T(8,128)(2,1)} custom-call(bf16[4,1728,128]{2,1,0:T(8,128)(2,1)S(1)} %copy-done, bf16[768,640]{1,0:T(8,128)(2,1)S(1)} %update.1.weight_ref), custom_call_target="tpu_custom_call" | custom-call | tf_op jit(solution)/shard_map/forward/pallas_call | solution.py:332
  136.2 6.2 %all-to-all-start.3 = ((bf16[128,8,768]{2,1,0:T(8,128)(2,1)}), bf16[128,8,768]{2,1,0:T(8,128)(2,1)S(1)}, u32[]{:S(2)}, u32[]{:S(2)}) async-start(bf16[128,8,768]{2,1,0:T(8,128)(2,1)} %bitcast.16), calls=%async_computation.3 | async-start | bytes 3145728 | tf_op jit(solution)/shard_map/forward/all_to_all | solution.py:248
  142.5 0.7 mixing.1
  143.1 42.0 %all-to-all-done.3 = bf16[128,8,768]{2,1,0:T(8,128)(2,1)S(1)} async-done(((bf16[128,8,768]{2,1,0:T(8,128)(2,1)}), bf16[128,8,768]{2,1,0:T(8,128)(2,1)S(1)}, u32[]{:S(2)}, u32[]{:S(2)}) %all-to-all-start.3) | async-done | bytes 1572896 | tf_op jit(solution)/shard_map/forward/all_to_all | solution.py:248
  185.1 1.6 combine.1
  (16 shorter events, 0.0 us)
Async XLA Ops:
  6.5 75.9 %all-gather.5.cloned.1.call-start = ((), (), s32[]{:S(2)}) async-start(), calls=%async_computation.5 | async-start | bytes 2211840 | tf_op jit(solution)/shard_map/first_hidden/all_gather | solution.py:291
  6.5 1.0 copy-start.3
  7.6 1.3 copy-start.4
  7.6 20.3 %copy-start.10 = (s32[128]{0:T(128)S(1)}, s32[128]{0:T(128)}, u32[]{:S(2)}) copy-start(s32[128]{0:T(128)} %param.22) | copy-start | bytes 1540
  7.6 20.3 %copy-start.11 = (s32[128]{0:T(128)S(1)}, s32[128]{0:T(128)}, u32[]{:S(2)}) copy-start(s32[128]{0:T(128)} %param.23) | copy-start | bytes 1540
  10.4 45.1 %copy-start.5 = (bf16[128,640]{1,0:T(8,128)(2,1)S(1)}, bf16[128,640]{1,0:T(8,128)(2,1)}, u32[]{:S(2)}) copy-start(bf16[128,640]{1,0:T(8,128)(2,1)} %tokens_ref.1) | copy-start | bytes 491524
  10.4 45.1 %copy-start.6 = (s32[128,6]{0,1:T(8,128)S(1)}, s32[128,6]{0,1:T(8,128)}, u32[]{:S(2)}) copy-start(s32[128,6]{0,1:T(8,128)} %param.13) | copy-start | bytes 9220
  10.4 45.1 %copy-start.7 = (f32[128,6]{0,1:T(8,128)S(1)}, f32[128,6]{0,1:T(8,128)}, u32[]{:S(2)}) copy-start(f32[128,6]{0,1:T(8,128)} %param.14) | copy-start | bytes 9220
  10.4 37.7 %all-to-all-start = ((bf16[128,16,128]{2,1,0:T(8,128)(2,1)}), bf16[128,16,128]{2,1,0:T(8,128)(2,1)S(1)}, u32[]{:S(2)}, u32[]{:S(2)}) async-start(bf16[128,16,128]{2,1,0:T(8,128)(2,1)} %bitcast.5), calls=%async_computation | async-start | bytes 1048576 | tf_op jit(solution)/shard_map/second_hidden_out/all_to_all | solution.py:248
  49.6 26.0 %all-to-all-start.1 = ((bf16[128,16,128]{2,1,0:T(8,128)(2,1)}), bf16[128,16,128]{2,1,0:T(8,128)(2,1)S(1)}, u32[]{:S(2)}, u32[]{:S(2)}) async-start(bf16[128,16,128]{2,1,0:T(8,128)(2,1)} %second_hidden_in.1), calls=%async_computation.1 | async-start | bytes 1048576 | tf_op jit(solution)/shard_map/second_hidden_in/all_to_all | solution.py:248
  75.6 48.6 %copy-start.1 = (bf16[1,768,640]{2,1,0:T(8,128)(2,1)S(1)}, bf16[1,768,640]{2,1,0:T(8,128)(2,1)}, u32[]{:S(2)}) copy-start(bf16[1,768,640]{2,1,0:T(8,128)(2,1)} %param.20) | copy-start | bytes 2949124
  75.6 48.6 %all-to-all-start.2 = ((bf16[128,8,768]{2,1,0:T(8,128)(2,1)}), bf16[128,8,768]{2,1,0:T(8,128)(2,1)S(1)}, u32[]{:S(2)}, u32[]{:S(2)}) async-start(bf16[128,8,768]{2,1,0:T(8,128)(2,1)} %bitcast.11), calls=%async_computation.2 | async-start | bytes 3145728 | tf_op jit(solution)/shard_map/dispatch/all_to_all | solution.py:248
  81.6 49.8 %all-gather.3.cloned.1.call-start = ((), (), s32[]{:S(2)}) async-start(), calls=%async_computation.4 | async-start | bytes 2211840 | tf_op jit(solution)/shard_map/second_hidden_in/all_gather | solution.py:304
  124.2 1.2 copy-start.2
  131.4 1.5 copy-start
  136.2 6.2 %copy-start.8 = (s32[128,6]{0,1:T(8,128)S(1)}, s32[128,6]{0,1:T(8,128)}, u32[]{:S(2)}) copy-start(s32[128,6]{0,1:T(8,128)} %param.16) | copy-start | bytes 9220
  136.2 6.2 %copy-start.9 = (f32[128,6]{0,1:T(8,128)S(1)}, f32[128,6]{0,1:T(8,128)}, u32[]{:S(2)}) copy-start(f32[128,6]{0,1:T(8,128)} %param.17) | copy-start | bytes 9220
  136.2 48.9 %all-to-all-start.3 = ((bf16[128,8,768]{2,1,0:T(8,128)(2,1)}), bf16[128,8,768]{2,1,0:T(8,128)(2,1)S(1)}, u32[]{:S(2)}, u32[]{:S(2)}) async-start(bf16[128,8,768]{2,1,0:T(8,128)(2,1)} %bitcast.16), calls=%async_computation.3 | async-start | bytes 3145728 | tf_op jit(solution)/shard_map/forward/all_to_all | solution.py:248
Sparse Core Ops, SparseCore 0:
  9.5 38.0 all-gather.4
  84.5 34.3 all-gather.2

commit v2 on v1

--- a/solution.py
+++ b/solution.py
@@ -12,6 +12,11 @@
 LEARN_RATE = 0.04
 WEIGHT_DECAY = 0.1
 EPSILON = 1e-08
+KEEP = 1.0 - LEARN_RATE * WEIGHT_DECAY
+ONE_OLD = LEARN_RATE * BETA_ONE / CORRECT_ONE
+ONE_NEW = LEARN_RATE * (1.0 - BETA_ONE) / CORRECT_ONE
+TWO_OLD = BETA_TWO / CORRECT_TWO
+TWO_NEW = (1.0 - BETA_TWO) / CORRECT_TWO
 
 EXP = 128
 TOK = 128
@@ -23,10 +28,12 @@
 HPART = 192
 COLS = 640
 WIDE = 768
-PIECES = 108
-PROWS = PIECES * 16
+PROWS = ROWS * HPART // 128
 NONE = 99.0
-VMEM_LIMIT = 48 * 1024 * 1024
+LEG = (7, 2, 128)
+MOVES = 8
+STEP = 256
+HALF = ROWS // 2
 F32 = jnp.float32
 BF16 = jnp.bfloat16
 
@@ -34,8 +41,8 @@
 NT = (((1,), (1,)), ((), ()))
 
 
-def params():
-    return pltpu.CompilerParams(vmem_limit_bytes=VMEM_LIMIT)
+def params(limit=16):
+    return pltpu.CompilerParams(vmem_limit_bytes=limit * 1024 * 1024)
 
 
 def iota(shape, dim):
@@ -92,8 +99,11 @@
     last = last_pick()
     for b in range(8):
         win = slice(128 * b, 128 * b + 256)
-        out_ref[128 * b : 128 * b + 128, :] = mm(pick[b], first[:, win], NT).astype(BF16)
-    out_ref[MAIN:ROWS, :] = mm(last, first, NT).astype(BF16)
+        at = 128 * b + 64 * (b // 4)
+        out_ref[at : at + 128, :] = mm(pick[b], first[:, win], NT).astype(BF16)
+    ends = mm(last, first, NT).astype(BF16)
+    out_ref[512:HALF, :] = ends[0:64]
+    out_ref[HALF + 512 : ROWS, :] = ends[64:128]
     for b in range(4):
         win_low = slice(128 * b, 128 * b + 256)
         win_high = slice(128 * b + 512, 128 * b + 768)
@@ -101,7 +111,6 @@
         out_ref[ROWS + 128 * b : ROWS + 128 * b + 128, :] = both.astype(BF16)
     both = mm(last[0:64], low, NT) + mm(last[64:128], high, NT)
     out_ref[ROWS + 512 : PROWS, :] = both.astype(BF16)
-    out_ref[PROWS:, :] = jnp.zeros((128 * 16 - PROWS, 128), BF16)
 
 
 def prepare_first(h_ref, out_ref):
@@ -133,12 +142,10 @@
     out_ref[:, COLS:WIDE] = extra[...].astype(BF16)
 
 
-def choose(source_ref, in_ref, out_ref):
-    def body(slot, carry):
-        out_ref[slot] = in_ref[source_ref[slot]]
-        return carry
-
-    lax.fori_loop(0, EXP, body, 0, unroll=8)
+def choose(to_ref, from_ref, in_ref, out_ref):
+    out_ref[...] = in_ref[...]
+    for m in range(MOVES):
+        out_ref[to_ref[m]] = in_ref[from_ref[m]]
 
 
 def last_rows(payload_ref, extra):
@@ -148,68 +155,71 @@
     ).astype(BF16)
 
 
-def update(hidden_ref, payload_ref, master_ref, one_ref, two_ref, out_ref, extra, last):
-    @pl.when(pl.program_id(0) == 0)
-    def _():
-        last[...] = last_rows(payload_ref, extra)
-
-    gradient = mm(hidden_ref[:, 0:MAIN], payload_ref[:, 0:COLS]) + mm(
-        hidden_ref[:, MAIN:ROWS], last[...]
-    )
-    master = master_ref[...]
-    moment_new = BETA_ONE * one_ref[...].astype(F32) + (1.0 - BETA_ONE) * gradient
-    second = BETA_TWO * two_ref[...].astype(F32) + (1.0 - BETA_TWO) * gradient * gradient
-    ratio = moment_new / CORRECT_ONE / (jnp.sqrt(second / CORRECT_TWO) + EPSILON)
-    updated = master - LEARN_RATE * (ratio + WEIGHT_DECAY * master)
-    out_ref[...] = updated.astype(BF16)
-
-
-def forward(hidden_ref, weight_ref, out_ref, extra):
-    def part(t, low, high):
-        return weight_ref[t * HPART + low : t * HPART + high, :]
-
-    blank = jnp.zeros((64, COLS), BF16)
-    pairs = [jnp.concatenate([part(t, 0, 128), part(t + 1, 0, 128)], axis=0) for t in (0, 2)]
-    lows = [
-        jnp.concatenate([part(t, 128, 192), blank, part(t + 1, 128, 192), blank], axis=0)
-        for t in (0, 2)
-    ]
-    highs = [
-        jnp.concatenate([blank, part(t, 128, 192), blank, part(t + 1, 128, 192)], axis=0)
-        for t in (0, 2)
-    ]
-
-    def rows(at, count, packed_at, weights):
-        total = None
-        for n, t in enumerate((0, 2)):
-            one = jnp.concatenate(
-                [hidden_ref[t, at : at + count, :], hidden_ref[t + 1, at : at + count, :]], axis=1
-            )
-            two = jnp.concatenate(
-                [
-                    hidden_ref[t, packed_at : packed_at + count, :],
-                    hidden_ref[t + 1, packed_at : packed_at + count, :],
-                ],
-                axis=1,
-            )
-            term = mm(one, pairs[n]) + mm(two, weights[n])
-            total = term if total is None else total + term
-        return total.astype(BF16)
-
-    for b in range(4):
-        for half, weights in ((0, lows), (512, highs)):
-            at = half + 128 * b
-            out_ref[at : at + 128, 0:COLS] = rows(at, 128, ROWS + 128 * b, weights)
-    last = jnp.concatenate(
-        [
-            rows(MAIN, 64, ROWS + 512, lows),
-            rows(MAIN + 64, 64, ROWS + 512, highs),
-        ],
-        axis=0,
-    ).astype(F32)
+def finish(
+    payload_ref, hidden_hbm, master_hbm, one_hbm, two_hbm, second_hbm, out_ref,
+    hidden, master, one, two, second, weight, last, extra, sems,
+):
+    sources = (hidden_hbm, master_hbm, one_hbm, two_hbm)
+    targets = (hidden, master, one, two)
+    steps = HID // STEP
+    copies = []
+    for n in range(steps):
+        at = pl.ds(n * STEP, STEP)
+        copies.append(
+            [
+                pltpu.make_async_copy(sources[i].at[at], targets[i].at[at], sems.at[4 * n + i])
+                for i in range(4)
+            ]
+        )
+        for copy in copies[n]:
+            copy.start()
+    rest = pltpu.make_async_copy(second_hbm, second, sems.at[4 * steps])
+    rest.start()
+
+    last[...] = last_rows(payload_ref, extra)
+    for n in range(steps):
+        at = slice(n * STEP, n * STEP + STEP)
+        for copy in copies[n]:
+            copy.wait()
+        gradient = mm(hidden[at, 0:MAIN], payload_ref[:, 0:COLS]) + mm(
+            hidden[at, MAIN:ROWS], last[...]
+        )
+        moment_new = ONE_OLD * one[at].astype(F32) + ONE_NEW * gradient
+        moment_two = TWO_OLD * two[at].astype(F32) + TWO_NEW * gradient * gradient
+        updated = KEEP * master[at] - moment_new / (jnp.sqrt(moment_two) + EPSILON)
+        weight[at, :] = updated.astype(BF16)
+    rest.wait()
+
+    def part(t, low, high, cols):
+        return weight[t * HPART + low : t * HPART + high, cols]
+
+    def pair(t, rows):
+        return jnp.concatenate([second[t, rows, :], second[t + 1, rows, :]], axis=1)
+
     extra[...] = jnp.zeros_like(extra)
-    for q in range(5):
-        extra[pl.ds(q, EXP, stride=8), :] = last[:, 128 * q : 128 * q + 128]
+    packed = [pair(t, slice(ROWS, PROWS)) for t in (0, 2)]
+    for half in range(2):
+        rows = slice(HALF * half, HALF * half + HALF)
+        whole = [pair(t, rows) for t in (0, 2)]
+        for start, stop in ((0, 256), (256, 512), (512, 640)):
+            cols = slice(start, stop)
+            blank = jnp.zeros((64, stop - start), BF16)
+            total = None
+            for n, t in enumerate((0, 2)):
+                both = jnp.concatenate([part(t, 0, 128, cols), part(t + 1, 0, 128, cols)], axis=0)
+                ends = [part(t, 128, 192, cols), part(t + 1, 128, 192, cols)]
+                if half == 0:
+                    ends = [ends[0], blank, ends[1], blank]
+                else:
+                    ends = [blank, ends[0], blank, ends[1]]
+                term = mm(whole[n], both) + mm(packed[n], jnp.concatenate(ends, axis=0))
+                total = term if total is None else total + term
+            total = total.astype(BF16)
+            out_ref[512 * half : 512 * half + 512, cols] = total[0:512]
+            ends = total[512:HALF].astype(F32)
+            for q in range(start // 128, stop // 128):
+                at = 128 * q - start
+                extra[pl.ds(512 * half + q, 64, stride=8), :] = ends[:, at : at + 128]
     out_ref[:, COLS:WIDE] = extra[...].astype(BF16)
 
 
@@ -264,16 +274,21 @@
 ):
     labels = jnp.arange(EXP, dtype=jnp.int32)
     plan = old_plan.reshape(1, EXP)
-    source = jnp.sum(
-        jnp.where(new_plan[None, :] == old_plan[:, None], labels[None, :], 0), axis=1
-    )
+    moved = old_plan != new_plan
+    order = jnp.sum(jnp.where((labels[None, :] < labels[:, None]) & moved[None, :], 1, 0), axis=1)
+    chosen = (order[None, :] == labels[:MOVES, None]) & moved[None, :]
+    to = jnp.sum(jnp.where(chosen, labels[None, :], 0), axis=1)
+    source = jnp.sum(jnp.where(new_plan[None, :] == old_plan[:, None], labels[None, :], 0), axis=1)
+    origin = jnp.sum(jnp.where(labels[None, :] == to[:, None], source[None, :], 0), axis=1)
     extra = pltpu.VMEM((MAIN, 128), F32)
+    hbm = pl.BlockSpec(memory_space=pltpu.HBM)
+    smem = pl.BlockSpec(memory_space=pltpu.SMEM)
+    vmem = pl.BlockSpec(memory_space=pltpu.VMEM)
 
     with jax.named_scope("second_hidden_out"):
-        pieces = pl.pallas_call(
-            prepare_second, out_shape=shape(EXP * 16, 128), compiler_params=params()
-        )(hidden_second[0].T)
-        spread = exchange(pieces.reshape(EXP, 16, 128))
+        tiles = hidden_second[0].T.reshape(24, 8, 9, 128).transpose(0, 2, 1, 3)
+        tiles = jnp.pad(tiles.reshape(PROWS, 128), ((0, EXP * 14 - PROWS), (0, 0)))
+        spread = exchange(tiles.reshape(EXP, *LEG))
 
     with jax.named_scope("dispatch"):
         rows = pl.pallas_call(
@@ -285,22 +300,23 @@
         arrived = exchange(rows.reshape(EXP, 8, WIDE)).reshape(MAIN, WIDE)
 
     with jax.named_scope("first_hidden"):
+        first = lax.all_gather(hidden_first[0].T, "tensor", axis=0, tiled=True)
         first = pl.pallas_call(
-            prepare_first, out_shape=shape(HPART, ROWS), compiler_params=params()
-        )(hidden_first[0].T)
-        first = lax.all_gather(first, "tensor", axis=0, tiled=True)
+            prepare_first, out_shape=shape(HID, ROWS), compiler_params=params()
+        )(first)
 
     with jax.named_scope("second_hidden_in"):
-        chosen = pl.pallas_call(
+        kept = pl.pallas_call(
             choose,
-            out_shape=shape(EXP, 16, 128),
-            in_specs=[
-                pl.BlockSpec(memory_space=pltpu.SMEM),
-                pl.BlockSpec(memory_space=pltpu.VMEM),
-            ],
+            out_shape=shape(EXP, *LEG),
+            in_specs=[smem, smem, vmem],
             compiler_params=params(),
-        )(source, spread)
-        mine = exchange(chosen)[:PIECES].reshape(PROWS, 128)
+        )(to, origin, spread)
+        mine = exchange(kept).reshape(EXP * 14, 128)[:PROWS]
+        mine = mine.reshape(24, 9, 8, 128).transpose(0, 2, 1, 3).reshape(HPART, ROWS)
+        mine = pl.pallas_call(
+            prepare_second, out_shape=shape(PROWS, 128), compiler_params=params()
+        )(mine)
         second = lax.all_gather(mine, "tensor", axis=0)
 
     with jax.named_scope("mixing"):
@@ -310,31 +326,24 @@
             compiler_params=params(),
         )(route_second.T, gates_second.T, plan)
 
-    with jax.named_scope("update"):
-        step = 128
-        weight = pl.pallas_call(
-            update,
-            grid=(HID // step,),
-            in_specs=[
-                pl.BlockSpec((step, ROWS), lambda i: (i, 0)),
-                pl.BlockSpec((MAIN, WIDE), lambda i: (0, 0)),
-                pl.BlockSpec((step, COLS), lambda i: (i, 0)),
-                pl.BlockSpec((step, COLS), lambda i: (i, 0)),
-                pl.BlockSpec((step, COLS), lambda i: (i, 0)),
+    with jax.named_scope("finish"):
+        produced = pl.pallas_call(
+            finish,
+            in_specs=[vmem, hbm, hbm, hbm, hbm, hbm],
+            out_shape=shape(MAIN, WIDE),
+            scratch_shapes=[
+                pltpu.VMEM((HID, ROWS), BF16),
+                pltpu.VMEM((HID, COLS), F32),
+                pltpu.VMEM((HID, COLS), BF16),
+                pltpu.VMEM((HID, COLS), BF16),
+                pltpu.VMEM((4, PROWS, 128), BF16),
+                pltpu.VMEM((HID, COLS), BF16),
+                pltpu.VMEM((EXP, COLS), BF16),
+                extra,
+                pltpu.SemaphoreType.DMA((4 * (HID // STEP) + 1,)),
             ],
-            out_specs=pl.BlockSpec((step, COLS), lambda i: (i, 0)),
-            out_shape=shape(HID, COLS),
-            scratch_shapes=[extra, pltpu.VMEM((EXP, COLS), BF16)],
-            compiler_params=params(),
-        )(first, arrived, master[0], moment_one[0], moment_two[0])
-
-    with jax.named_scope("forward"):
-        produced = pl.pallas_call(
-            forward,
-            out_shape=shape(MAIN, WIDE),
-            scratch_shapes=[extra],
-            compiler_params=params(),
-        )(second, weight)
+            compiler_params=params(48),
+        )(arrived, first, master[0], moment_one[0], moment_two[0], second)
         returned = exchange(produced.reshape(EXP, 8, WIDE)).reshape(MAIN, WIDE)
 
     with jax.named_scope("combine"):

time: 194 us -> 188 us (0.969)
  waiting for transfers between devices: 122 us -> 114 us
  starting transfers between devices: 35.4 us -> 37.9 us
  Pallas kernels: 18.4 us -> 16.4 us
    all_to_all x4, waiting for transfers between devices: 121 us -> 113 us  [exchange(): return lax.all_to_all(x, 'expert', split_axis=0, concat_axis=0, tiled=True)]
    all_to_all x4, starting transfers between devices: 35.4 us -> 37.7 us  [exchange(): return lax.all_to_all(x, 'expert', split_axis=0, concat_axis=0, tiled=True)]
    pallas_call x5 -> x4, Pallas kernels: 13.6 us -> 11.6 us  [the longest x1 7.36 us: shards(): pl.pallas_call(finish, in_specs=[vmem, hbm, hbm, hbm, hbm, hbm], out_shap...]
  transfers between devices with their start and end apart: 6 -> 6, of which waited for: 4 -> 4; matrix products, arithmetic and copies ran while one was open for 0% -> 1% of each run, Pallas kernels for 6% -> 4%
where the time goes in v2:
time: 188 us; the launch traced here: 187 us
  waiting for transfers between devices  114 us (61%)
  starting transfers between devices  37.9 us (20%)
  Pallas kernels  16.4 us (9%)
  between operations  13.6 us (7%)
  local copies, waits for them, and re-layouts  4.66 us (2%)
    all_to_all x4, waiting for transfers between devices, exchange(): return lax.all_to_all(x, 'expert', split_axis=0, concat_axis=0, tiled=True)  113 us
    all_to_all x4, starting transfers between devices, exchange(): return lax.all_to_all(x, 'expert', split_axis=0, concat_axis=0, tiled=True)  37.7 us
    pallas_call x1, Pallas kernels, shards(): pl.pallas_call(finish, in_specs=[vmem, hbm, hbm, hbm, hbm, hbm], out_shap...  7.36 us
  transfers between devices with their start and end apart: 6, of which 4 were waited for; matrix products, arithmetic and copies ran while one was open for 1% of the time, Pallas kernels for 4%

profile of v2, /device:TPU:8, one launch (start us, length us, event | category | flops | bytes accessed | tf_op | source)
XLA Modules:
  0.0 187.2 jit_solution(15892288977152766665)
XLA Ops:
  6.5 0.0 all-gather.4.cloned.1.call-start
  6.5 0.7 all-gather.4.cloned.1.call-update
  7.3 0.0 copy-start.4
  7.3 0.0 copy-start.5
  7.3 1.9 %pad.4 = bf16[1792,128]{1,0:T(8,128)(2,1)} pad(bf16[1728,128]{1,0:T(8,128)(2,1)} %bitcast.47, bf16[]{:T(256)} %constant.5.clone.1), padding=0_64x0_0 | pad | bytes 901122 | tf_op jit(solution)/shard_map/second_hidden_out/jit(_pad)/pad | solution.py:290
  9.2 17.4 %all-to-all-start.1 = ((bf16[128,7,2,128]{3,2,1,0:T(2,128)(2,1)}), bf16[128,7,2,128]{3,2,1,0:T(2,128)(2,1)S(1)}, u32[]{:S(2)}, u32[]{:S(2)}) async-start(bf16[128,7,2,128]{3,2,1,0:T(2,128)(2,1)} %bitcast.17), calls=%async_computation.1 | async-start | bytes 917504 | tf_op jit(solution)/shard_map/second_hidden_out/all_to_all | solution.py:258
  26.6 0.1 select_reduce_fusion.1
  26.7 0.2 select_reduce_fusion.3.to_ref
  26.9 0.2 select_reduce_fusion
  27.1 0.2 select_reduce_fusion.2.from_ref
  27.3 18.1 %all-to-all-done.1.in_ref = bf16[128,7,2,128]{3,2,1,0:T(2,128)(2,1)S(1)} async-done(((bf16[128,7,2,128]{3,2,1,0:T(2,128)(2,1)}), bf16[128,7,2,128]{3,2,1,0:T(2,128)(2,1)S(1)}, u32[]{:S(2)}, u32[]{:S(2)}) %all-to-all-start.1) | async-done | bytes 458784 | tf_op jit(solution)/shard_map/second_hidden_out/all_to_all | solution.py:258
  45.4 1.4 second_hidden_in.2
  46.8 5.7 %all-to-all-start.2 = ((bf16[128,7,2,128]{3,2,1,0:T(2,128)(2,1)}), bf16[128,7,2,128]{3,2,1,0:T(2,128)(2,1)S(1)}, u32[]{:S(2)}, u32[]{:S(2)}) async-start(bf16[128,7,2,128]{3,2,1,0:T(2,128)(2,1)} %second_hidden_in.2), calls=%async_computation.2 | async-start | bytes 917504 | tf_op jit(solution)/shard_map/second_hidden_in/all_to_all | solution.py:258
  52.5 2.5 %dispatch.1 = bf16[1024,768]{1,0:T(8,128)(2,1)} custom-call(s32[6,128]{1,0:T(8,128)S(1)} %bitcast.38, f32[6,128]{1,0:T(8,128)S(1)} %bitcast.39, s32[1,128]{1,0:T(1,128)S(1)} %bitcast.42, bf16[128,640]{1,0:T(8,128)(2,1)S(1)} %copy-done.4), custom_call_target="tpu_custom_call" | custom-call | tf_op jit(solution)/shard_map/dispatch/pallas_call | solution.py:294
  55.0 16.4 %all-to-all-done.2 = bf16[128,7,2,128]{3,2,1,0:T(2,128)(2,1)S(1)} async-done(((bf16[128,7,2,128]{3,2,1,0:T(2,128)(2,1)}), bf16[128,7,2,128]{3,2,1,0:T(2,128)(2,1)S(1)}, u32[]{:S(2)}, u32[]{:S(2)}) %all-to-all-start.2) | async-done | bytes 458784 | tf_op jit(solution)/shard_map/second_hidden_in/all_to_all | solution.py:258
  71.4 5.7 %all-to-all-start = ((bf16[128,8,768]{2,1,0:T(8,128)(2,1)}), bf16[128,8,768]{2,1,0:T(8,128)(2,1)S(1)}, u32[]{:S(2)}, u32[]{:S(2)}) async-start(bf16[128,8,768]{2,1,0:T(8,128)(2,1)} %bitcast.5), calls=%async_computation | async-start | bytes 3145728 | tf_op jit(solution)/shard_map/dispatch/all_to_all | solution.py:258
  77.1 0.2 all-gather.6.cloned.1.call-start
  77.4 1.5 second_hidden_in.3
  78.8 0.0 all-gather.6.cloned.1.call-update
  78.8 0.0 all-gather.4.cloned.1.call-done.h_ref
  78.9 1.5 copy-done.1
  80.4 1.5 first_hidden.1.hidden_hbm
  81.8 0.0 copy-start
  81.8 1.2 copy-done
  83.1 36.7 %all-to-all-done = bf16[128,8,768]{2,1,0:T(8,128)(2,1)S(1)} async-done(((bf16[128,8,768]{2,1,0:T(8,128)(2,1)}), bf16[128,8,768]{2,1,0:T(8,128)(2,1)S(1)}, u32[]{:S(2)}, u32[]{:S(2)}) %all-to-all-start) | async-done | bytes 1572896 | tf_op jit(solution)/shard_map/dispatch/all_to_all | solution.py:258
  119.8 7.4 %finish.1 = bf16[1024,768]{1,0:T(8,128)(2,1)} custom-call(bf16[1024,768]{1,0:T(8,128)(2,1)S(1)} %bitcast.34, bf16[768,1152]{1,0:T(8,128)(2,1)} %copy-done, f32[768,640]{1,0:T(8,128)} %bitcast.44, bf16[768,640]{1,0:T(8,128)(2,1)S(1)} %bitcast.36, bf16[768,640]{1,0:T(8,128)(2,1)S(1)} %bitcast.37, bf16[4,1728,128]{2,1,0:T(8,128)(2,1)} %bitcast.46), custom_call_target="tpu_custom_call" | custom-call | tf_op jit(solution)/shard_map/finish/pallas_call | solution.py:330
  127.2 0.0 copy-start.7
  127.2 0.0 copy-start.8
  127.2 8.8 %all-to-all-start.3 = ((bf16[128,8,768]{2,1,0:T(8,128)(2,1)}), bf16[128,8,768]{2,1,0:T(8,128)(2,1)S(1)}, u32[]{:S(2)}, u32[]{:S(2)}) async-start(bf16[128,8,768]{2,1,0:T(8,128)(2,1)} %bitcast.23), calls=%async_computation.3 | async-start | bytes 3145728 | tf_op jit(solution)/shard_map/finish/all_to_all | solution.py:258
  136.1 0.7 mixing.1
  136.7 42.0 %all-to-all-done.3 = bf16[128,8,768]{2,1,0:T(8,128)(2,1)S(1)} async-done(((bf16[128,8,768]{2,1,0:T(8,128)(2,1)}), bf16[128,8,768]{2,1,0:T(8,128)(2,1)S(1)}, u32[]{:S(2)}, u32[]{:S(2)}) %all-to-all-start.3) | async-done | bytes 1572896 | tf_op jit(solution)/shard_map/finish/all_to_all | solution.py:258
  178.7 1.6 combine.1
  (19 shorter events, 0.1 us)
Async XLA Ops:
  6.5 20.0 %copy-start.9 = (s32[128]{0:T(128)S(1)}, s32[128]{0:T(128)}, u32[]{:S(2)}) copy-start(s32[128]{0:T(128)} %param.22) | copy-start | bytes 1540
  6.5 20.0 %copy-start.10 = (s32[128]{0:T(128)S(1)}, s32[128]{0:T(128)}, u32[]{:S(2)}) copy-start(s32[128]{0:T(128)} %param.23) | copy-start | bytes 1540
  6.5 72.3 %all-gather.4.cloned.1.call-start = ((), (), s32[]{:S(2)}) async-start(), calls=%async_computation.4 | async-start | bytes 2211840 | tf_op jit(solution)/shard_map/first_hidden/all_gather | solution.py:303
  7.3 45.3 %copy-start.4 = (bf16[128,640]{1,0:T(8,128)(2,1)S(1)}, bf16[128,640]{1,0:T(8,128)(2,1)}, u32[]{:S(2)}) copy-start(bf16[128,640]{1,0:T(8,128)(2,1)} %tokens_ref.1) | copy-start | bytes 491524
  7.3 45.3 %copy-start.5 = (s32[128,6]{0,1:T(8,128)S(1)}, s32[128,6]{0,1:T(8,128)}, u32[]{:S(2)}) copy-start(s32[128,6]{0,1:T(8,128)} %param.13) | copy-start | bytes 9220
  7.3 45.3 %copy-start.6 = (f32[128,6]{0,1:T(8,128)S(1)}, f32[128,6]{0,1:T(8,128)}, u32[]{:S(2)}) copy-start(f32[128,6]{0,1:T(8,128)} %param.14) | copy-start | bytes 9220
  9.2 36.2 %all-to-all-start.1 = ((bf16[128,7,2,128]{3,2,1,0:T(2,128)(2,1)}), bf16[128,7,2,128]{3,2,1,0:T(2,128)(2,1)S(1)}, u32[]{:S(2)}, u32[]{:S(2)}) async-start(bf16[128,7,2,128]{3,2,1,0:T(2,128)(2,1)} %bitcast.17), calls=%async_computation.1 | async-start | bytes 917504 | tf_op jit(solution)/shard_map/second_hidden_out/all_to_all | solution.py:258
  46.8 24.6 %all-to-all-start.2 = ((bf16[128,7,2,128]{3,2,1,0:T(2,128)(2,1)}), bf16[128,7,2,128]{3,2,1,0:T(2,128)(2,1)S(1)}, u32[]{:S(2)}, u32[]{:S(2)}) async-start(bf16[128,7,2,128]{3,2,1,0:T(2,128)(2,1)} %second_hidden_in.2), calls=%async_computation.2 | async-start | bytes 917504 | tf_op jit(solution)/shard_map/second_hidden_in/all_to_all | solution.py:258
  71.4 48.4 %all-to-all-start = ((bf16[128,8,768]{2,1,0:T(8,128)(2,1)}), bf16[128,8,768]{2,1,0:T(8,128)(2,1)S(1)}, u32[]{:S(2)}, u32[]{:S(2)}) async-start(bf16[128,8,768]{2,1,0:T(8,128)(2,1)} %bitcast.5), calls=%async_computation | async-start | bytes 3145728 | tf_op jit(solution)/shard_map/dispatch/all_to_all | solution.py:258
  77.1 42.7 %all-gather.6.cloned.1.call-start = ((), (), s32[]{:S(2)}) async-start(), calls=%async_computation.5 | async-start | bytes 2211840 | tf_op jit(solution)/shard_map/second_hidden_in/all_gather | solution.py:320
  78.9 1.5 copy-start.1
  80.4 39.4 %copy-start.2 = (bf16[1,768,640]{2,1,0:T(8,128)(2,1)S(1)}, bf16[1,768,640]{2,1,0:T(8,128)(2,1)}, u32[]{:S(2)}) copy-start(bf16[1,768,640]{2,1,0:T(8,128)(2,1)} %param.20) | copy-start | bytes 2949124
  80.4 39.4 %copy-start.3 = (bf16[1,768,640]{2,1,0:T(8,128)(2,1)S(1)}, bf16[1,768,640]{2,1,0:T(8,128)(2,1)}, u32[]{:S(2)}) copy-start(bf16[1,768,640]{2,1,0:T(8,128)(2,1)} %param.21) | copy-start | bytes 2949124
  81.8 1.2 copy-start
  127.2 8.9 %copy-start.7 = (s32[128,6]{0,1:T(8,128)S(1)}, s32[128,6]{0,1:T(8,128)}, u32[]{:S(2)}) copy-start(s32[128,6]{0,1:T(8,128)} %param.16) | copy-start | bytes 9220
  127.2 8.9 %copy-start.8 = (f32[128,6]{0,1:T(8,128)S(1)}, f32[128,6]{0,1:T(8,128)}, u32[]{:S(2)}) copy-start(f32[128,6]{0,1:T(8,128)} %param.17) | copy-start | bytes 9220
  127.2 51.5 %all-to-all-start.3 = ((bf16[128,8,768]{2,1,0:T(8,128)(2,1)}), bf16[128,8,768]{2,1,0:T(8,128)(2,1)S(1)}, u32[]{:S(2)}, u32[]{:S(2)}) async-start(bf16[128,8,768]{2,1,0:T(8,128)(2,1)} %bitcast.23), calls=%async_computation.3 | async-start | bytes 3145728 | tf_op jit(solution)/shard_map/finish/all_to_all | solution.py:258
Sparse Core Ops, SparseCore 0:
  9.5 38.0 all-gather.3
  80.0 34.3 all-gather.5

commit v3 on v2

--- a/solution.py
+++ b/solution.py
@@ -90,27 +90,10 @@
 
 
 def prepare_second(h_ref, out_ref):
-    first = h_ref[0:128, :]
-    second = h_ref[128:192, :]
-    blank = jnp.zeros_like(second)
-    low = jnp.concatenate([second, blank], axis=0)
-    high = jnp.concatenate([blank, second], axis=0)
-    pick = [main_pick(b) for b in range(8)]
-    last = last_pick()
     for b in range(8):
         win = slice(128 * b, 128 * b + 256)
-        at = 128 * b + 64 * (b // 4)
-        out_ref[at : at + 128, :] = mm(pick[b], first[:, win], NT).astype(BF16)
-    ends = mm(last, first, NT).astype(BF16)
-    out_ref[512:HALF, :] = ends[0:64]
-    out_ref[HALF + 512 : ROWS, :] = ends[64:128]
-    for b in range(4):
-        win_low = slice(128 * b, 128 * b + 256)
-        win_high = slice(128 * b + 512, 128 * b + 768)
-        both = mm(pick[b], low[:, win_low], NT) + mm(pick[b + 4], high[:, win_high], NT)
-        out_ref[ROWS + 128 * b : ROWS + 128 * b + 128, :] = both.astype(BF16)
-    both = mm(last[0:64], low, NT) + mm(last[64:128], high, NT)
-    out_ref[ROWS + 512 : PROWS, :] = both.astype(BF16)
+        out_ref[128 * b : 128 * b + 128, :] = mm(main_pick(b), h_ref[:, win], NT).astype(BF16)
+    out_ref[MAIN:ROWS, :] = mm(last_pick(), h_ref[...], NT).astype(BF16)
 
 
 def prepare_first(h_ref, out_ref):
@@ -142,10 +125,10 @@
     out_ref[:, COLS:WIDE] = extra[...].astype(BF16)
 
 
-def choose(to_ref, from_ref, in_ref, out_ref):
+def choose(moves_ref, in_ref, out_ref):
     out_ref[...] = in_ref[...]
     for m in range(MOVES):
-        out_ref[to_ref[m]] = in_ref[from_ref[m]]
+        out_ref[moves_ref[m]] = in_ref[moves_ref[MOVES + m]]
 
 
 def last_rows(payload_ref, extra):
@@ -156,71 +139,56 @@
 
 
 def finish(
-    payload_ref, hidden_hbm, master_hbm, one_hbm, two_hbm, second_hbm, out_ref,
-    hidden, master, one, two, second, weight, last, extra, sems,
+    payload_ref, one, two, first_hbm, master_hbm, second_hbm, out_hbm,
+    first, master, second, weight, rows, extra, out, sems,
 ):
-    sources = (hidden_hbm, master_hbm, one_hbm, two_hbm)
-    targets = (hidden, master, one, two)
     steps = HID // STEP
     copies = []
     for n in range(steps):
         at = pl.ds(n * STEP, STEP)
-        copies.append(
-            [
-                pltpu.make_async_copy(sources[i].at[at], targets[i].at[at], sems.at[4 * n + i])
-                for i in range(4)
-            ]
-        )
-        for copy in copies[n]:
-            copy.start()
-    rest = pltpu.make_async_copy(second_hbm, second, sems.at[4 * steps])
-    rest.start()
-
-    last[...] = last_rows(payload_ref, extra)
+        for i, (source, target) in enumerate(((first_hbm, first), (master_hbm, master))):
+            copies.append(
+                pltpu.make_async_copy(source.at[at], target.at[at], sems.at[2 * n + i])
+            )
+    copies.append(pltpu.make_async_copy(second_hbm, second, sems.at[2 * steps]))
+    for copy in copies:
+        copy.start()
+
+    rows[0:MAIN, :] = payload_ref[:, 0:COLS]
+    rows[MAIN:ROWS, :] = last_rows(payload_ref, extra)
     for n in range(steps):
         at = slice(n * STEP, n * STEP + STEP)
-        for copy in copies[n]:
-            copy.wait()
-        gradient = mm(hidden[at, 0:MAIN], payload_ref[:, 0:COLS]) + mm(
-            hidden[at, MAIN:ROWS], last[...]
-        )
+        copies[2 * n].wait()
+        gradient = mm(first[at, :], rows[...])
+        copies[2 * n + 1].wait()
         moment_new = ONE_OLD * one[at].astype(F32) + ONE_NEW * gradient
         moment_two = TWO_OLD * two[at].astype(F32) + TWO_NEW * gradient * gradient
-        updated = KEEP * master[at] - moment_new / (jnp.sqrt(moment_two) + EPSILON)
+        root = moment_two * lax.rsqrt(moment_two)
+        updated = KEEP * master[at] - moment_new * pl.reciprocal(root + EPSILON)
         weight[at, :] = updated.astype(BF16)
-    rest.wait()
-
-    def part(t, low, high, cols):
-        return weight[t * HPART + low : t * HPART + high, cols]
-
-    def pair(t, rows):
-        return jnp.concatenate([second[t, rows, :], second[t + 1, rows, :]], axis=1)
+    copies[-1].wait()
 
     extra[...] = jnp.zeros_like(extra)
-    packed = [pair(t, slice(ROWS, PROWS)) for t in (0, 2)]
-    for half in range(2):
-        rows = slice(HALF * half, HALF * half + HALF)
-        whole = [pair(t, rows) for t in (0, 2)]
-        for start, stop in ((0, 256), (256, 512), (512, 640)):
-            cols = slice(start, stop)
-            blank = jnp.zeros((64, stop - start), BF16)
-            total = None
-            for n, t in enumerate((0, 2)):
-                both = jnp.concatenate([part(t, 0, 128, cols), part(t + 1, 0, 128, cols)], axis=0)
-                ends = [part(t, 128, 192, cols), part(t + 1, 128, 192, cols)]
-                if half == 0:
-                    ends = [ends[0], blank, ends[1], blank]
-                else:
-                    ends = [blank, ends[0], blank, ends[1]]
-                term = mm(whole[n], both) + mm(packed[n], jnp.concatenate(ends, axis=0))
-                total = term if total is None else total + term
-            total = total.astype(BF16)
-            out_ref[512 * half : 512 * half + 512, cols] = total[0:512]
-            ends = total[512:HALF].astype(F32)
-            for q in range(start // 128, stop // 128):
-                at = 128 * q - start
-                extra[pl.ds(512 * half + q, 64, stride=8), :] = ends[:, at : at + 128]
-    out_ref[:, COLS:WIDE] = extra[...].astype(BF16)
+    sent = []
+    for n, (start, stop) in enumerate(((0, 256), (256, 512), (512, 640))):
+        total = mm(second[...], weight[:, start:stop]).astype(BF16)
+        out[:, start:stop] = total[0:MAIN]
+        ends = total[MAIN:ROWS].astype(F32)
+        for q in range(start // 128, stop // 128):
+            at = 128 * q - start
+            extra[pl.ds(q, EXP, stride=8), :] = ends[:, at : at + 128]
+        if stop == COLS:
+            out[:, COLS:WIDE] = extra[...].astype(BF16)
+            stop = WIDE
+        cols = pl.ds(start, stop - start)
+        sent.append(
+            pltpu.make_async_copy(
+                out.at[:, cols], out_hbm.at[:, cols], sems.at[2 * steps + 1 + n]
+            )
+        )
+        sent[-1].start()
+    for copy in sent:
+        copy.wait()
 
 
 def mixing(route_ref, gates_ref, plan_ref, main_ref, last_ref):
@@ -280,6 +248,7 @@
     to = jnp.sum(jnp.where(chosen, labels[None, :], 0), axis=1)
     source = jnp.sum(jnp.where(new_plan[None, :] == old_plan[:, None], labels[None, :], 0), axis=1)
     origin = jnp.sum(jnp.where(labels[None, :] == to[:, None], source[None, :], 0), axis=1)
+    moves = jnp.concatenate([to, origin])
     extra = pltpu.VMEM((MAIN, 128), F32)
     hbm = pl.BlockSpec(memory_space=pltpu.HBM)
     smem = pl.BlockSpec(memory_space=pltpu.SMEM)
@@ -297,6 +266,22 @@
             scratch_shapes=[extra],
             compiler_params=params(),
         )(route_first.T, gates_first.T, plan, cotangent)
+    with jax.named_scope("second_hidden_in"):
+        kept = pl.pallas_call(
+            choose,
+            out_shape=shape(EXP, *LEG),
+            in_specs=[smem, vmem],
+            compiler_params=params(),
+        )(moves, spread)
+        kept, rows = lax.optimization_barrier((kept, rows))
+        mine = exchange(kept).reshape(EXP * 14, 128)[:PROWS]
+        mine = mine.reshape(24, 9, 8, 128).transpose(0, 2, 1, 3).reshape(HPART, ROWS)
+        second = lax.all_gather(mine, "tensor", axis=0, tiled=True)
+        second = pl.pallas_call(
+            prepare_second, out_shape=shape(ROWS, HID), compiler_params=params(), cost_estimate=pl.CostEstimate(flops=10*1000*1000000, bytes_accessed=0, transcendentals=0)
+        )(second)
+
+    with jax.named_scope("dispatch"):
         arrived = exchange(rows.reshape(EXP, 8, WIDE)).reshape(MAIN, WIDE)
 
     with jax.named_scope("first_hidden"):
@@ -304,20 +289,6 @@
         first = pl.pallas_call(
             prepare_first, out_shape=shape(HID, ROWS), compiler_params=params()
         )(first)
-
-    with jax.named_scope("second_hidden_in"):
-        kept = pl.pallas_call(
-            choose,
-            out_shape=shape(EXP, *LEG),
-            in_specs=[smem, smem, vmem],
-            compiler_params=params(),
-        )(to, origin, spread)
-        mine = exchange(kept).reshape(EXP * 14, 128)[:PROWS]
-        mine = mine.reshape(24, 9, 8, 128).transpose(0, 2, 1, 3).reshape(HPART, ROWS)
-        mine = pl.pallas_call(
-            prepare_second, out_shape=shape(PROWS, 128), compiler_params=params()
-        )(mine)
-        second = lax.all_gather(mine, "tensor", axis=0)
 
     with jax.named_scope("mixing"):
         mix, mix_last = pl.pallas_call(
@@ -329,21 +300,21 @@
     with jax.named_scope("finish"):
         produced = pl.pallas_call(
             finish,
-            in_specs=[vmem, hbm, hbm, hbm, hbm, hbm],
+            in_specs=[vmem, vmem, vmem, hbm, hbm, hbm],
+            out_specs=hbm,
             out_shape=shape(MAIN, WIDE),
             scratch_shapes=[
                 pltpu.VMEM((HID, ROWS), BF16),
                 pltpu.VMEM((HID, COLS), F32),
+                pltpu.VMEM((ROWS, HID), BF16),
                 pltpu.VMEM((HID, COLS), BF16),
-                pltpu.VMEM((HID, COLS), BF16),
-                pltpu.VMEM((4, PROWS, 128), BF16),
-                pltpu.VMEM((HID, COLS), BF16),
-                pltpu.VMEM((EXP, COLS), BF16),
+                pltpu.VMEM((ROWS, COLS), BF16),
                 extra,
-                pltpu.SemaphoreType.DMA((4 * (HID // STEP) + 1,)),
+                pltpu.VMEM((MAIN, WIDE), BF16),
+                pltpu.SemaphoreType.DMA((2 * (HID // STEP) + 4,)),
             ],
             compiler_params=params(48),
-        )(arrived, first, master[0], moment_one[0], moment_two[0], second)
+        )(arrived, moment_one[0], moment_two[0], first, master[0], second)
         returned = exchange(produced.reshape(EXP, 8, WIDE)).reshape(MAIN, WIDE)
 
     with jax.named_scope("combine"):

time: 188 us -> 184 us (0.979)
  the two profiles are of different devices: /device:TPU:8 before, /device:TPU:14 now
where the time goes in v3:
time: 184 us
  waiting for transfers between devices  92.3 us (50%)
  starting transfers between devices  29.3 us (16%)
  blocking collectives  24.4 us (13%)
  Pallas kernels  15.3 us (8%)
  between operations  13.6 us (7%)
  local copies, waits for them, and re-layouts  8.12 us (4%)
    all_to_all x3, waiting for transfers between devices, exchange(): return lax.all_to_all(x, 'expert', split_axis=0, concat_axis=0, tiled=True)  76.6 us
    all_to_all x3, starting transfers between devices, exchange(): return lax.all_to_all(x, 'expert', split_axis=0, concat_axis=0, tiled=True)  29.2 us
    all_to_all x1, blocking collectives, exchange(): return lax.all_to_all(x, 'expert', split_axis=0, concat_axis=0, tiled=True)  24.4 us
    all_gather x1, waiting for transfers between devices, shards(): second = lax.all_gather(mine, 'tensor', axis=0, tiled=True)  15 us
    pallas_call x1, Pallas kernels, shards(): pl.pallas_call(finish, in_specs=[vmem, vmem, vmem, hbm, hbm, hbm], out_sp...  6.82 us
    unnamed x26, local copies, waits for them, and re-layouts  5.47 us
  transfers between devices with their start and end apart: 5, of which 4 were waited for; matrix products, arithmetic and copies ran while one was open for 2% of the time, Pallas kernels for 4%

profile of v3, /device:TPU:14, one launch (start us, length us, event | category | flops | bytes accessed | tf_op | source)
XLA Modules:
  0.0 183.7 jit_solution(11423743333263497048)
XLA Ops:
  6.5 0.0 all-gather.3.cloned.1.call-start
  6.6 0.7 all-gather.3.cloned.1.call-update
  7.3 1.8 %pad.4 = bf16[1792,128]{1,0:T(8,128)(2,1)} pad(bf16[1728,128]{1,0:T(8,128)(2,1)} %bitcast.45, bf16[]{:T(256)} %constant.5.clone.1), padding=0_64x0_0 | pad | bytes 901122 | tf_op jit(solution)/shard_map/second_hidden_out/jit(_pad)/pad | solution.py:259
  9.1 17.4 %all-to-all-start = ((bf16[128,7,2,128]{3,2,1,0:T(2,128)(2,1)}), bf16[128,7,2,128]{3,2,1,0:T(2,128)(2,1)S(1)}, u32[]{:S(2)}, u32[]{:S(2)}) async-start(bf16[128,7,2,128]{3,2,1,0:T(2,128)(2,1)} %bitcast.8), calls=%async_computation | async-start | bytes 917504 | tf_op jit(solution)/shard_map/second_hidden_out/all_to_all | solution.py:226
  26.5 0.0 all-gather.5.cloned.1.call-start
  26.6 2.5 %dispatch.1 = bf16[1024,768]{1,0:T(8,128)(2,1)} custom-call(s32[6,128]{1,0:T(8,128)S(1)} %bitcast.36, f32[6,128]{1,0:T(8,128)S(1)} %bitcast.37, s32[1,128]{1,0:T(1,128)S(1)} %bitcast.40, bf16[128,640]{1,0:T(8,128)(2,1)S(1)} %copy-done.5), custom_call_target="tpu_custom_call" | custom-call | tf_op jit(solution)/shard_map/dispatch/pallas_call | solution.py:263
  29.1 0.1 select_reduce_fusion.1
  29.2 0.2 select_reduce_fusion.3
  29.4 0.2 select_reduce_fusion
  29.6 0.2 select_reduce_fusion.2
  29.7 0.1 pad_add_fusion.moves_ref
  29.8 15.5 %all-to-all-done.in_ref = bf16[128,7,2,128]{3,2,1,0:T(2,128)(2,1)S(1)} async-done(((bf16[128,7,2,128]{3,2,1,0:T(2,128)(2,1)}), bf16[128,7,2,128]{3,2,1,0:T(2,128)(2,1)S(1)}, u32[]{:S(2)}, u32[]{:S(2)}) %all-to-all-start) | async-done | bytes 458784 | tf_op jit(solution)/shard_map/second_hidden_out/all_to_all | solution.py:226
  45.3 0.6 second_hidden_in.2
  45.9 24.4 %all_to_all.20 = bf16[128,7,2,128]{3,2,1,0:T(2,128)(2,1)S(1)} all-to-all(bf16[128,7,2,128]{3,2,1,0:T(2,128)(2,1)S(1)} %second_hidden_in.2), channel_id=1, replica_groups=mesh['expert'=128,'tensor'=4] {'expert'}, dimensions={0} | all-to-all | bytes 917504 | tf_op jit(solution)/shard_map/second_hidden_in/all_to_all | solution.py:226
  70.3 0.8 slice.8
  71.1 0.0 all-gather.5.cloned.1.call-update
  71.2 5.7 %all-to-all-start.1 = ((bf16[128,8,768]{2,1,0:T(8,128)(2,1)}), bf16[128,8,768]{2,1,0:T(8,128)(2,1)S(1)}, u32[]{:S(2)}, u32[]{:S(2)}) async-start(bf16[128,8,768]{2,1,0:T(8,128)(2,1)} %bitcast.11), calls=%async_computation.1 | async-start | bytes 3145728 | tf_op jit(solution)/shard_map/dispatch/all_to_all | solution.py:226
  76.9 0.0 all-gather.3.cloned.1.call-done.h_ref
  76.9 1.5 copy-done.1
  78.5 1.5 first_hidden.1.first_hbm
  79.9 1.2 copy-done
  81.2 15.0 %all-gather.5.cloned.1.call-done.h_ref = bf16[768,1152]{1,0:T(8,128)(2,1)} async-done(((bf16[192,1152]{1,0:T(8,128)(2,1)}), bf16[768,1152]{1,0:T(8,128)(2,1)}) %all-gather.5.cloned.1.call-update) | async-done | bytes 1769488 | tf_op jit(solution)/shard_map/second_hidden_in/all_gather | solution.py:279
  96.1 1.5 copy-done.11
  97.6 1.7 second_hidden_in.3.second_hbm
  99.3 1.2 copy-done.2
  100.5 19.1 %all-to-all-done.1 = bf16[128,8,768]{2,1,0:T(8,128)(2,1)S(1)} async-done(((bf16[128,8,768]{2,1,0:T(8,128)(2,1)}), bf16[128,8,768]{2,1,0:T(8,128)(2,1)S(1)}, u32[]{:S(2)}, u32[]{:S(2)}) %all-to-all-start.1) | async-done | bytes 1572896 | tf_op jit(solution)/shard_map/dispatch/all_to_all | solution.py:226
  119.6 6.8 %finish.1 = bf16[1024,768]{1,0:T(8,128)(2,1)} custom-call(bf16[1024,768]{1,0:T(8,128)(2,1)S(1)} %bitcast.33, bf16[768,640]{1,0:T(8,128)(2,1)S(1)} %bitcast.34, bf16[768,640]{1,0:T(8,128)(2,1)S(1)} %bitcast.35, bf16[768,1152]{1,0:T(8,128)(2,1)} %copy-done, f32[768,640]{1,0:T(8,128)} %bitcast.42, bf16[1152,768]{1,0:T(8,128)(2,1)} %copy-done.2), custom_call_target="tpu_custom_call" | custom-call | tf_op jit(solution)/shard_map/finish/pallas_call | solution.py:301
  126.4 0.0 copy-start.9
  126.4 6.1 %all-to-all-start.3 = ((bf16[128,8,768]{2,1,0:T(8,128)(2,1)}), bf16[128,8,768]{2,1,0:T(8,128)(2,1)S(1)}, u32[]{:S(2)}, u32[]{:S(2)}) async-start(bf16[128,8,768]{2,1,0:T(8,128)(2,1)} %bitcast.22), calls=%async_computation.3 | async-start | bytes 3145728 | tf_op jit(solution)/shard_map/finish/all_to_all | solution.py:226
  132.6 0.7 mixing.1
  133.2 42.0 %all-to-all-done.3 = bf16[128,8,768]{2,1,0:T(8,128)(2,1)S(1)} async-done(((bf16[128,8,768]{2,1,0:T(8,128)(2,1)}), bf16[128,8,768]{2,1,0:T(8,128)(2,1)S(1)}, u32[]{:S(2)}, u32[]{:S(2)}) %all-to-all-start.3) | async-done | bytes 1572896 | tf_op jit(solution)/shard_map/finish/all_to_all | solution.py:226
  175.2 1.6 combine.1
  (23 shorter events, 0.1 us)
Async XLA Ops:
  6.5 20.0 %copy-start.10 = (s32[128]{0:T(128)S(1)}, s32[128]{0:T(128)}, u32[]{:S(2)}) copy-start(s32[128]{0:T(128)} %param.22) | copy-start | bytes 1540
  6.5 20.0 %copy-start.12 = (s32[128]{0:T(128)S(1)}, s32[128]{0:T(128)}, u32[]{:S(2)}) copy-start(s32[128]{0:T(128)} %param.23) | copy-start | bytes 1540
  6.5 20.0 %copy-start.7 = (f32[128,6]{0,1:T(8,128)S(1)}, f32[128,6]{0,1:T(8,128)}, u32[]{:S(2)}) copy-start(f32[128,6]{0,1:T(8,128)} %param.14) | copy-start | bytes 9220
  6.5 20.1 %copy-start.6 = (s32[128,6]{0,1:T(8,128)S(1)}, s32[128,6]{0,1:T(8,128)}, u32[]{:S(2)}) copy-start(s32[128,6]{0,1:T(8,128)} %param.13) | copy-start | bytes 9220
  6.5 20.1 %copy-start.5 = (bf16[128,640]{1,0:T(8,128)(2,1)S(1)}, bf16[128,640]{1,0:T(8,128)(2,1)}, u32[]{:S(2)}) copy-start(bf16[128,640]{1,0:T(8,128)(2,1)} %tokens_ref.1) | copy-start | bytes 491524
  6.5 70.4 %all-gather.3.cloned.1.call-start = ((), (), s32[]{:S(2)}) async-start(), calls=%async_computation.4 | async-start | bytes 2211840 | tf_op jit(solution)/shard_map/first_hidden/all_gather | solution.py:288
  9.1 36.2 %all-to-all-start = ((bf16[128,7,2,128]{3,2,1,0:T(2,128)(2,1)}), bf16[128,7,2,128]{3,2,1,0:T(2,128)(2,1)S(1)}, u32[]{:S(2)}, u32[]{:S(2)}) async-start(bf16[128,7,2,128]{3,2,1,0:T(2,128)(2,1)} %bitcast.8), calls=%async_computation | async-start | bytes 917504 | tf_op jit(solution)/shard_map/second_hidden_out/all_to_all | solution.py:226
  26.5 69.6 %all-gather.5.cloned.1.call-start = ((), (), s32[]{:S(2)}) async-start(), calls=%async_computation.5 | async-start | bytes 2211840 | tf_op jit(solution)/shard_map/second_hidden_in/all_gather | solution.py:279
  71.2 48.4 %all-to-all-start.1 = ((bf16[128,8,768]{2,1,0:T(8,128)(2,1)}), bf16[128,8,768]{2,1,0:T(8,128)(2,1)S(1)}, u32[]{:S(2)}, u32[]{:S(2)}) async-start(bf16[128,8,768]{2,1,0:T(8,128)(2,1)} %bitcast.11), calls=%async_computation.1 | async-start | bytes 3145728 | tf_op jit(solution)/shard_map/dispatch/all_to_all | solution.py:226
  76.9 1.5 copy-start.1
  79.9 1.2 copy-start
  81.2 38.4 %copy-start.3 = (bf16[1,768,640]{2,1,0:T(8,128)(2,1)S(1)}, bf16[1,768,640]{2,1,0:T(8,128)(2,1)}, u32[]{:S(2)}) copy-start(bf16[1,768,640]{2,1,0:T(8,128)(2,1)} %param.20) | copy-start | bytes 2949124
  81.2 38.4 %copy-start.4 = (bf16[1,768,640]{2,1,0:T(8,128)(2,1)S(1)}, bf16[1,768,640]{2,1,0:T(8,128)(2,1)}, u32[]{:S(2)}) copy-start(bf16[1,768,640]{2,1,0:T(8,128)(2,1)} %param.21) | copy-start | bytes 2949124
  96.1 1.5 copy-start.11
  99.3 1.2 copy-start.2
  126.4 6.1 %copy-start.8 = (s32[128,6]{0,1:T(8,128)S(1)}, s32[128,6]{0,1:T(8,128)}, u32[]{:S(2)}) copy-start(s32[128,6]{0,1:T(8,128)} %param.16) | copy-start | bytes 9220
  126.4 6.1 %copy-start.9 = (f32[128,6]{0,1:T(8,128)S(1)}, f32[128,6]{0,1:T(8,128)}, u32[]{:S(2)}) copy-start(f32[128,6]{0,1:T(8,128)} %param.17) | copy-start | bytes 9220
  126.4 48.8 %all-to-all-start.3 = ((bf16[128,8,768]{2,1,0:T(8,128)(2,1)}), bf16[128,8,768]{2,1,0:T(8,128)(2,1)S(1)}, u32[]{:S(2)}, u32[]{:S(2)}) async-start(bf16[128,8,768]{2,1,0:T(8,128)(2,1)} %bitcast.22), calls=%async_computation.3 | async-start | bytes 3145728 | tf_op jit(solution)/shard_map/finish/all_to_all | solution.py:226
Sparse Core Ops, SparseCore 0:
  9.5 36.4 all-gather.2
  71.3 24.8 all-gather.4

commit v4 on v3

--- a/solution.py
+++ b/solution.py
@@ -32,8 +32,6 @@
 NONE = 99.0
 LEG = (7, 2, 128)
 MOVES = 8
-STEP = 256
-HALF = ROWS // 2
 F32 = jnp.float32
 BF16 = jnp.bfloat16
 
@@ -89,18 +87,22 @@
     return onehot(iota((EXP, ROWS), 1) == iota((EXP, ROWS), 0) * 9 + 8)
 
 
-def prepare_second(h_ref, out_ref):
+def prepare_second(zero_ref, one_ref, two_ref, three_ref, out_ref):
+    parts = [ref[...] for ref in (zero_ref, one_ref, two_ref, three_ref)]
+    whole = jnp.concatenate(parts, axis=0)
     for b in range(8):
         win = slice(128 * b, 128 * b + 256)
-        out_ref[128 * b : 128 * b + 128, :] = mm(main_pick(b), h_ref[:, win], NT).astype(BF16)
-    out_ref[MAIN:ROWS, :] = mm(last_pick(), h_ref[...], NT).astype(BF16)
-
-
-def prepare_first(h_ref, out_ref):
-    for b in range(8):
-        win = slice(128 * b, 128 * b + 256)
-        out_ref[:, 128 * b : 128 * b + 128] = mm(h_ref[:, win], main_pick(b), NT).astype(BF16)
-    out_ref[:, MAIN:ROWS] = mm(h_ref[...], last_pick(), NT).astype(BF16)
+        out_ref[128 * b : 128 * b + 128, :] = mm(main_pick(b), whole[:, win], NT).astype(BF16)
+    out_ref[MAIN:ROWS, :] = mm(last_pick(), whole, NT).astype(BF16)
+
+
+def prepare_first(zero_ref, one_ref, two_ref, three_ref, out_ref):
+    for n, ref in enumerate((zero_ref, one_ref, two_ref, three_ref)):
+        at = slice(n * HPART, n * HPART + HPART)
+        for b in range(8):
+            win = slice(128 * b, 128 * b + 256)
+            out_ref[at, 128 * b : 128 * b + 128] = mm(ref[:, win], main_pick(b), NT).astype(BF16)
+        out_ref[at, MAIN:ROWS] = mm(ref[...], last_pick(), NT).astype(BF16)
 
 
 def build_rows(route_ref, gates_ref, plan_ref, tokens_ref, out_ref, extra):
@@ -142,29 +144,31 @@
     payload_ref, one, two, first_hbm, master_hbm, second_hbm, out_hbm,
     first, master, second, weight, rows, extra, out, sems,
 ):
-    steps = HID // STEP
-    copies = []
-    for n in range(steps):
-        at = pl.ds(n * STEP, STEP)
-        for i, (source, target) in enumerate(((first_hbm, first), (master_hbm, master))):
-            copies.append(
-                pltpu.make_async_copy(source.at[at], target.at[at], sems.at[2 * n + i])
-            )
-    copies.append(pltpu.make_async_copy(second_hbm, second, sems.at[2 * steps]))
+    me = lax.axis_index("tensor")
+    copies, places = [], []
+    for n in range(4):
+        at = pl.ds(n * HPART, HPART)
+        place = pl.ds(pl.multiple_of(lax.rem(me + 4 - n, 4) * HPART, HPART), HPART)
+        places.append(place)
+        copies.append(pltpu.make_async_copy(first_hbm.at[at], first.at[at], sems.at[2 * n]))
+        copies.append(
+            pltpu.make_async_copy(master_hbm.at[place], master.at[at], sems.at[2 * n + 1])
+        )
+    copies.append(pltpu.make_async_copy(second_hbm, second, sems.at[8]))
     for copy in copies:
         copy.start()
 
     rows[0:MAIN, :] = payload_ref[:, 0:COLS]
     rows[MAIN:ROWS, :] = last_rows(payload_ref, extra)
-    for n in range(steps):
-        at = slice(n * STEP, n * STEP + STEP)
+    for n in range(4):
+        at = slice(n * HPART, n * HPART + HPART)
         copies[2 * n].wait()
         gradient = mm(first[at, :], rows[...])
         copies[2 * n + 1].wait()
-        moment_new = ONE_OLD * one[at].astype(F32) + ONE_NEW * gradient
-        moment_two = TWO_OLD * two[at].astype(F32) + TWO_NEW * gradient * gradient
+        moment_new = ONE_OLD * one[places[n], :].astype(F32) + ONE_NEW * gradient
+        moment_two = TWO_OLD * two[places[n], :].astype(F32) + TWO_NEW * gradient * gradient
         root = moment_two * lax.rsqrt(moment_two)
-        updated = KEEP * master[at] - moment_new * pl.reciprocal(root + EPSILON)
+        updated = KEEP * master[at, :] - moment_new * pl.reciprocal(root + EPSILON)
         weight[at, :] = updated.astype(BF16)
     copies[-1].wait()
 
@@ -183,7 +187,7 @@
         cols = pl.ds(start, stop - start)
         sent.append(
             pltpu.make_async_copy(
-                out.at[:, cols], out_hbm.at[:, cols], sems.at[2 * steps + 1 + n]
+                out.at[:, cols], out_hbm.at[:, cols], sems.at[9 + n]
             )
         )
         sent[-1].start()
@@ -224,6 +228,14 @@
 
 def exchange(x):
     return lax.all_to_all(x, "expert", split_axis=0, concat_axis=0, tiled=True)
+
+
+def before(x, shift):
+    return lax.ppermute(x, "tensor", [(i, (i + shift) % 4) for i in range(4)])
+
+
+def gather(x):
+    return [x] + [before(x, shift) for shift in (1, 2, 3)]
 
 
 def shards(
@@ -273,22 +285,28 @@
             in_specs=[smem, vmem],
             compiler_params=params(),
         )(moves, spread)
-        kept, rows = lax.optimization_barrier((kept, rows))
-        mine = exchange(kept).reshape(EXP * 14, 128)[:PROWS]
-        mine = mine.reshape(24, 9, 8, 128).transpose(0, 2, 1, 3).reshape(HPART, ROWS)
-        second = lax.all_gather(mine, "tensor", axis=0, tiled=True)
+        part = hidden_first[0].T
+        near, far = before(part, 1), before(part, 3)
+        kept, rows, near, far = lax.optimization_barrier((kept, rows, near, far))
+        second = [
+            piece.reshape(EXP * 14, 128)[:PROWS]
+            .reshape(24, 9, 8, 128)
+            .transpose(0, 2, 1, 3)
+            .reshape(HPART, ROWS)
+            for piece in gather(exchange(kept))
+        ]
         second = pl.pallas_call(
-            prepare_second, out_shape=shape(ROWS, HID), compiler_params=params(), cost_estimate=pl.CostEstimate(flops=10*1000*1000000, bytes_accessed=0, transcendentals=0)
-        )(second)
+            prepare_second, out_shape=shape(ROWS, HID), compiler_params=params()
+        )(*second)
 
     with jax.named_scope("dispatch"):
+        rows, across = lax.optimization_barrier((rows, before(part, 2)))
         arrived = exchange(rows.reshape(EXP, 8, WIDE)).reshape(MAIN, WIDE)
 
     with jax.named_scope("first_hidden"):
-        first = lax.all_gather(hidden_first[0].T, "tensor", axis=0, tiled=True)
         first = pl.pallas_call(
             prepare_first, out_shape=shape(HID, ROWS), compiler_params=params()
-        )(first)
+        )(part, near, across, far)
 
     with jax.named_scope("mixing"):
         mix, mix_last = pl.pallas_call(
@@ -311,7 +329,7 @@
                 pltpu.VMEM((ROWS, COLS), BF16),
                 extra,
                 pltpu.VMEM((MAIN, WIDE), BF16),
-                pltpu.SemaphoreType.DMA((2 * (HID // STEP) + 4,)),
+                pltpu.SemaphoreType.DMA((12,)),
             ],
             compiler_params=params(48),
         )(arrived, moment_one[0], moment_two[0], first, master[0], second)

time: 184 us -> 181 us (0.984)
  starting transfers between devices: 29.3 us -> 63.1 us
  blocking collectives: 24.4 us -> 0 us
  between operations: 13.6 us -> 0.31 us
  local copies, waits for them, and re-layouts: 8.12 us -> 4.56 us
  waiting for transfers between devices: 92.3 us -> 95.4 us
    ppermute x0 -> x6, waiting for transfers between devices: none -> 29 us  [before(): return lax.ppermute(x, 'tensor', [(i, (i + shift) % 4) for i in range(4)])]
    all_to_all x1 -> x0, blocking collectives: 24.4 us -> none  [exchange(): return lax.all_to_all(x, 'expert', split_axis=0, concat_axis=0, tiled=True)]
    ppermute x0 -> x6, starting transfers between devices: none -> 17.5 us  [before(): return lax.ppermute(x, 'tensor', [(i, (i + shift) % 4) for i in range(4)])]
    all_to_all x3 -> x4, starting transfers between devices: 29.2 us -> 45.6 us  [exchange(): return lax.all_to_all(x, 'expert', split_axis=0, concat_axis=0, tiled=True)]
    all_gather x2 -> x0, waiting for transfers between devices: 15 us -> none  [the longest x1 15 us: shards(): second = lax.all_gather(mine, 'tensor', axis=0, tiled=True)]
    all_to_all x3 -> x4, waiting for transfers between devices: 76.6 us -> 66.5 us  [exchange(): return lax.all_to_all(x, 'expert', split_axis=0, concat_axis=0, tiled=True)]
    unnamed x26 -> x24, local copies, waits for them, and re-layouts: 5.47 us -> 1.25 us
  transfers between devices with their start and end apart: 5 -> 10, of which waited for: 4 -> 8; matrix products, arithmetic and copies ran while one was open for 2% -> 1% of each run, Pallas kernels for 4% -> 4%
where the time goes in v4:
time: 181 us; the launch traced here: 180 us
  waiting for transfers between devices  95.4 us (53%)
  starting transfers between devices  63.1 us (35%)
  Pallas kernels  16.3 us (9%)
  local copies, waits for them, and re-layouts  4.56 us (3%)
    all_to_all x4, waiting for transfers between devices, exchange(): return lax.all_to_all(x, 'expert', split_axis=0, concat_axis=0, tiled=True)  66.5 us
    all_to_all x4, starting transfers between devices, exchange(): return lax.all_to_all(x, 'expert', split_axis=0, concat_axis=0, tiled=True)  45.6 us
    ppermute x6, waiting for transfers between devices, before(): return lax.ppermute(x, 'tensor', [(i, (i + shift) % 4) for i in range(4)])  29 us
    ppermute x6, starting transfers between devices, before(): return lax.ppermute(x, 'tensor', [(i, (i + shift) % 4) for i in range(4)])  17.5 us
    pallas_call x1, Pallas kernels, shards(): pl.pallas_call(finish, in_specs=[vmem, vmem, vmem, hbm, hbm, hbm], out_sp...  7.03 us
  transfers between devices with their start and end apart: 10, of which 8 were waited for; matrix products, arithmetic and copies ran while one was open for 1% of the time, Pallas kernels for 4%

profile of v4, /device:TPU:14, one launch (start us, length us, event | category | flops | bytes accessed | tf_op | source)
XLA Modules:
  0.0 180.4 jit_solution(6716016003287847517)
XLA Ops:
  0.0 1.9 %pad.4 = bf16[1792,128]{1,0:T(8,128)(2,1)} pad(bf16[1728,128]{1,0:T(8,128)(2,1)} %bitcast.69, bf16[]{:T(256)} %constant.5.clone.1), padding=0_64x0_0 | pad | bytes 901122 | tf_op jit(solution)/shard_map/second_hidden_out/jit(_pad)/pad | solution.py:271
  1.9 17.4 %all-to-all-start = ((bf16[128,7,2,128]{3,2,1,0:T(2,128)(2,1)}), bf16[128,7,2,128]{3,2,1,0:T(2,128)(2,1)S(1)}, u32[]{:S(2)}, u32[]{:S(2)}) async-start(bf16[128,7,2,128]{3,2,1,0:T(2,128)(2,1)} %bitcast.8), calls=%async_computation | async-start | bytes 917504 | tf_op jit(solution)/shard_map/second_hidden_out/all_to_all | solution.py:230
  19.3 2.4 %collective-permute-start = (bf16[192,1152]{1,0:T(8,128)(2,1)S(1)}, bf16[192,1152]{1,0:T(8,128)(2,1)S(1)}, u32[]{:S(2)}, u32[]{:S(2)}) collective-permute-start(bf16[192,1152]{1,0:T(8,128)(2,1)S(1)} %bitcast.58), channel_id=1, source_target_pairs={{0,1},{1,2},{2,3},{3,0},{4,5},{5,6},{6,7},{7,4},{8,9},{9,10},{10,1... | collective-permute-start | bytes 1327112 | tf_op jit(solution)/shard_map/second_hidden_in/ppermute | solution.py:234
  21.7 3.5 %collective-permute-start.1 = (bf16[192,1152]{1,0:T(8,128)(2,1)S(1)}, bf16[192,1152]{1,0:T(8,128)(2,1)S(1)}, u32[]{:S(2)}, u32[]{:S(2)}) collective-permute-start(bf16[192,1152]{1,0:T(8,128)(2,1)S(1)} %bitcast.59), channel_id=1, source_target_pairs={{0,3},{1,0},{2,1},{3,2},{4,7},{5,4},{6,5},{7,6},{8,11},{9,8},{10,9... | collective-permute-start | bytes 1327112 | tf_op jit(solution)/shard_map/second_hidden_in/ppermute | solution.py:234
  25.2 2.5 %dispatch.1 = bf16[1024,768]{1,0:T(8,128)(2,1)} custom-call(s32[6,128]{1,0:T(8,128)S(1)} %bitcast.62, f32[6,128]{1,0:T(8,128)S(1)} %bitcast.63, s32[1,128]{1,0:T(1,128)S(1)} %bitcast.66, bf16[128,640]{1,0:T(8,128)(2,1)S(1)} %copy-done.5), custom_call_target="tpu_custom_call" | custom-call | tf_op jit(solution)/shard_map/dispatch/pallas_call | solution.py:275
  27.7 0.1 select_reduce_fusion.1
  27.8 0.2 select_reduce_fusion.3
  28.0 0.2 select_reduce_fusion
  28.2 0.2 select_reduce_fusion.2
  28.4 9.7 %all-to-all-done.in_ref = bf16[128,7,2,128]{3,2,1,0:T(2,128)(2,1)S(1)} async-done(((bf16[128,7,2,128]{3,2,1,0:T(2,128)(2,1)}), bf16[128,7,2,128]{3,2,1,0:T(2,128)(2,1)S(1)}, u32[]{:S(2)}, u32[]{:S(2)}) %all-to-all-start) | async-done | bytes 458784 | tf_op jit(solution)/shard_map/second_hidden_out/all_to_all | solution.py:230
  38.1 1.3 second_hidden_in.2
  39.5 11.4 %all-to-all-start.2 = ((bf16[128,7,2,128]{3,2,1,0:T(2,128)(2,1)}), bf16[128,7,2,128]{3,2,1,0:T(2,128)(2,1)}, u32[]{:S(2)}, u32[]{:S(2)}) async-start(bf16[128,7,2,128]{3,2,1,0:T(2,128)(2,1)} %second_hidden_in.2), calls=%async_computation.2 | async-start | bytes 917504 | tf_op jit(solution)/shard_map/second_hidden_in/all_to_all | solution.py:230
  50.9 3.1 %collective-permute-start.2 = (bf16[192,1152]{1,0:T(8,128)(2,1)S(1)}, bf16[192,1152]{1,0:T(8,128)(2,1)S(1)}, u32[]{:S(2)}, u32[]{:S(2)}) collective-permute-start(bf16[192,1152]{1,0:T(8,128)(2,1)S(1)} %bitcast.60), channel_id=1, source_target_pairs={{0,2},{1,3},{2,0},{3,1},{4,6},{5,7},{6,4},{7,5},{8,10},{9,11},{10,... | collective-permute-start | bytes 1327112 | tf_op jit(solution)/shard_map/dispatch/ppermute | solution.py:234
  54.0 12.5 %collective-permute-done.2.two_ref = bf16[192,1152]{1,0:T(8,128)(2,1)S(1)} collective-permute-done((bf16[192,1152]{1,0:T(8,128)(2,1)S(1)}, bf16[192,1152]{1,0:T(8,128)(2,1)S(1)}, u32[]{:S(2)}, u32[]{:S(2)}) %collective-permute-start.2) | collective-permute-done | bytes 442400 | tf_op jit(solution)/shard_map/dispatch/ppermute | solution.py:234
  66.5 2.9 %all-to-all-done.2 = bf16[128,7,2,128]{3,2,1,0:T(2,128)(2,1)} async-done(((bf16[128,7,2,128]{3,2,1,0:T(2,128)(2,1)}), bf16[128,7,2,128]{3,2,1,0:T(2,128)(2,1)}, u32[]{:S(2)}, u32[]{:S(2)}) %all-to-all-start.2) | async-done | bytes 458784 | tf_op jit(solution)/shard_map/second_hidden_in/all_to_all | solution.py:230
  69.4 10.8 %all-to-all-start.1 = ((bf16[128,8,768]{2,1,0:T(8,128)(2,1)}), bf16[128,8,768]{2,1,0:T(8,128)(2,1)S(1)}, u32[]{:S(2)}, u32[]{:S(2)}) async-start(bf16[128,8,768]{2,1,0:T(8,128)(2,1)} %bitcast.14), calls=%async_computation.1 | async-start | bytes 3145728 | tf_op jit(solution)/shard_map/dispatch/all_to_all | solution.py:230
  80.2 2.2 %collective-permute-start.3 = (bf16[128,7,2,128]{3,2,1,0:T(2,128)(2,1)}, bf16[128,7,2,128]{3,2,1,0:T(2,128)(2,1)S(1)}, u32[]{:S(2)}, u32[]{:S(2)}) collective-permute-start(bf16[128,7,2,128]{3,2,1,0:T(2,128)(2,1)} %all-to-all-done.2), channel_id=1, source_target_pairs={{0,1},{1,2},{2,3},{3,0},{4,5},{5,6},{6,7},{7,4},{8,9},{9,10},{10,1... | collective-permute-start | bytes 1376264 | tf_op jit(solution)/shard_map/second_hidden_in/ppermute | solution.py:234
  82.4 4.0 %collective-permute-start.4 = (bf16[128,7,2,128]{3,2,1,0:T(2,128)(2,1)}, bf16[128,7,2,128]{3,2,1,0:T(2,128)(2,1)S(1)}, u32[]{:S(2)}, u32[]{:S(2)}) collective-permute-start(bf16[128,7,2,128]{3,2,1,0:T(2,128)(2,1)} %all-to-all-done.2), channel_id=1, source_target_pairs={{0,2},{1,3},{2,0},{3,1},{4,6},{5,7},{6,4},{7,5},{8,10},{9,11},{10,... | collective-permute-start | bytes 1376264 | tf_op jit(solution)/shard_map/second_hidden_in/ppermute | solution.py:234
  86.5 2.3 %collective-permute-start.5 = (bf16[128,7,2,128]{3,2,1,0:T(2,128)(2,1)}, bf16[128,7,2,128]{3,2,1,0:T(2,128)(2,1)S(1)}, u32[]{:S(2)}, u32[]{:S(2)}) collective-permute-start(bf16[128,7,2,128]{3,2,1,0:T(2,128)(2,1)} %all-to-all-done.2), channel_id=1, source_target_pairs={{0,3},{1,0},{2,1},{3,2},{4,7},{5,4},{6,5},{7,6},{8,11},{9,8},{10,9... | collective-permute-start | bytes 1376264 | tf_op jit(solution)/shard_map/second_hidden_in/ppermute | solution.py:234
  88.8 1.5 first_hidden.1.first_hbm
  90.3 1.4 slice.20
  91.6 4.1 %collective-permute-done.3 = bf16[128,7,2,128]{3,2,1,0:T(2,128)(2,1)S(1)} collective-permute-done((bf16[128,7,2,128]{3,2,1,0:T(2,128)(2,1)}, bf16[128,7,2,128]{3,2,1,0:T(2,128)(2,1)S(1)}, u32[]{:S(2)}, u32[]{:S(2)}) %collective-permute-start.3) | collective-permute-done | bytes 458784 | tf_op jit(solution)/shard_map/second_hidden_in/ppermute | solution.py:234
  95.7 3.7 %collective-permute-done.4 = bf16[128,7,2,128]{3,2,1,0:T(2,128)(2,1)S(1)} collective-permute-done((bf16[128,7,2,128]{3,2,1,0:T(2,128)(2,1)}, bf16[128,7,2,128]{3,2,1,0:T(2,128)(2,1)S(1)}, u32[]{:S(2)}, u32[]{:S(2)}) %collective-permute-start.4) | collective-permute-done | bytes 458784 | tf_op jit(solution)/shard_map/second_hidden_in/ppermute | solution.py:234
  99.5 8.7 %collective-permute-done.5 = bf16[128,7,2,128]{3,2,1,0:T(2,128)(2,1)S(1)} collective-permute-done((bf16[128,7,2,128]{3,2,1,0:T(2,128)(2,1)}, bf16[128,7,2,128]{3,2,1,0:T(2,128)(2,1)S(1)}, u32[]{:S(2)}, u32[]{:S(2)}) %collective-permute-start.5) | collective-permute-done | bytes 458784 | tf_op jit(solution)/shard_map/second_hidden_in/ppermute | solution.py:234
  108.2 1.6 second_hidden_in.3.second_hbm
  109.9 1.2 copy-done.1
  111.1 11.8 %all-to-all-done.1 = bf16[128,8,768]{2,1,0:T(8,128)(2,1)S(1)} async-done(((bf16[128,8,768]{2,1,0:T(8,128)(2,1)}), bf16[128,8,768]{2,1,0:T(8,128)(2,1)S(1)}, u32[]{:S(2)}, u32[]{:S(2)}) %all-to-all-start.1) | async-done | bytes 1572896 | tf_op jit(solution)/shard_map/dispatch/all_to_all | solution.py:230
  122.9 7.0 %finish.1 = bf16[1024,768]{1,0:T(8,128)(2,1)} custom-call(bf16[1024,768]{1,0:T(8,128)(2,1)S(1)} %bitcast.51, bf16[768,640]{1,0:T(8,128)(2,1)S(1)} %bitcast.56, bf16[768,640]{1,0:T(8,128)(2,1)S(1)} %bitcast.57, bf16[768,1152]{1,0:T(8,128)(2,1)} %copy-done, f32[768,640]{1,0:T(8,128)} %bitcast.68, bf16[1152,768]{1,0:T(8,128)(2,1)} %copy-done.1), custom_call_target="tpu_custom_call" | custom-call | tf_op jit(solution)/shard_map/finish/pallas_call | solution.py:319
  130.0 6.1 %all-to-all-start.3 = ((bf16[128,8,768]{2,1,0:T(8,128)(2,1)}), bf16[128,8,768]{2,1,0:T(8,128)(2,1)S(1)}, u32[]{:S(2)}, u32[]{:S(2)}) async-start(bf16[128,8,768]{2,1,0:T(8,128)(2,1)} %bitcast.35), calls=%async_computation.3 | async-start | bytes 3145728 | tf_op jit(solution)/shard_map/finish/all_to_all | solution.py:230
  136.1 0.7 mixing.1
  136.8 42.0 %all-to-all-done.3 = bf16[128,8,768]{2,1,0:T(8,128)(2,1)S(1)} async-done(((bf16[128,8,768]{2,1,0:T(8,128)(2,1)}), bf16[128,8,768]{2,1,0:T(8,128)(2,1)S(1)}, u32[]{:S(2)}, u32[]{:S(2)}) %all-to-all-start.3) | async-done | bytes 1572896 | tf_op jit(solution)/shard_map/finish/all_to_all | solution.py:230
  178.8 1.6 combine.1
  (31 shorter events, 0.2 us)
Async XLA Ops:
  0.0 19.3 %copy-start.4 = (bf16[1,1152,192]{1,2,0:T(8,128)(2,1)S(1)}, bf16[1,1152,192]{1,2,0:T(8,128)(2,1)}, u32[]{:S(2)}) copy-start(bf16[1,1152,192]{1,2,0:T(8,128)(2,1)} %param.15) | copy-start | bytes 1327108
  0.0 25.1 %copy-start.10 = (s32[128]{0:T(128)S(1)}, s32[128]{0:T(128)}, u32[]{:S(2)}) copy-start(s32[128]{0:T(128)} %param.22) | copy-start | bytes 1540
  0.0 25.2 %copy-start.11 = (s32[128]{0:T(128)S(1)}, s32[128]{0:T(128)}, u32[]{:S(2)}) copy-start(s32[128]{0:T(128)} %param.23) | copy-start | bytes 1540
  0.0 25.2 %copy-start.7 = (f32[128,6]{0,1:T(8,128)S(1)}, f32[128,6]{0,1:T(8,128)}, u32[]{:S(2)}) copy-start(f32[128,6]{0,1:T(8,128)} %param.14) | copy-start | bytes 9220
  0.0 25.2 %copy-start.6 = (s32[128,6]{0,1:T(8,128)S(1)}, s32[128,6]{0,1:T(8,128)}, u32[]{:S(2)}) copy-start(s32[128,6]{0,1:T(8,128)} %param.13) | copy-start | bytes 9220
  0.0 25.2 %copy-start.5 = (bf16[128,640]{1,0:T(8,128)(2,1)S(1)}, bf16[128,640]{1,0:T(8,128)(2,1)}, u32[]{:S(2)}) copy-start(bf16[128,640]{1,0:T(8,128)(2,1)} %tokens_ref.1) | copy-start | bytes 491524
  1.9 36.2 %all-to-all-start = ((bf16[128,7,2,128]{3,2,1,0:T(2,128)(2,1)}), bf16[128,7,2,128]{3,2,1,0:T(2,128)(2,1)S(1)}, u32[]{:S(2)}, u32[]{:S(2)}) async-start(bf16[128,7,2,128]{3,2,1,0:T(2,128)(2,1)} %bitcast.8), calls=%async_computation | async-start | bytes 917504 | tf_op jit(solution)/shard_map/second_hidden_out/all_to_all | solution.py:230
  19.3 20.2 %collective-permute-start = (bf16[192,1152]{1,0:T(8,128)(2,1)S(1)}, bf16[192,1152]{1,0:T(8,128)(2,1)S(1)}, u32[]{:S(2)}, u32[]{:S(2)}) collective-permute-start(bf16[192,1152]{1,0:T(8,128)(2,1)S(1)} %bitcast.58), channel_id=1, source_target_pairs={{0,1},{1,2},{2,3},{3,0},{4,5},{5,6},{6,7},{7,4},{8,9},{9,10},{10,1... | collective-permute-start | bytes 1327112 | tf_op jit(solution)/shard_map/second_hidden_in/ppermute | solution.py:234
  21.7 17.8 %collective-permute-start.1 = (bf16[192,1152]{1,0:T(8,128)(2,1)S(1)}, bf16[192,1152]{1,0:T(8,128)(2,1)S(1)}, u32[]{:S(2)}, u32[]{:S(2)}) collective-permute-start(bf16[192,1152]{1,0:T(8,128)(2,1)S(1)} %bitcast.59), channel_id=1, source_target_pairs={{0,3},{1,0},{2,1},{3,2},{4,7},{5,4},{6,5},{7,6},{8,11},{9,8},{10,9... | collective-permute-start | bytes 1327112 | tf_op jit(solution)/shard_map/second_hidden_in/ppermute | solution.py:234
  39.5 29.9 %all-to-all-start.2 = ((bf16[128,7,2,128]{3,2,1,0:T(2,128)(2,1)}), bf16[128,7,2,128]{3,2,1,0:T(2,128)(2,1)}, u32[]{:S(2)}, u32[]{:S(2)}) async-start(bf16[128,7,2,128]{3,2,1,0:T(2,128)(2,1)} %second_hidden_in.2), calls=%async_computation.2 | async-start | bytes 917504 | tf_op jit(solution)/shard_map/second_hidden_in/all_to_all | solution.py:230
  50.9 15.6 %collective-permute-start.2 = (bf16[192,1152]{1,0:T(8,128)(2,1)S(1)}, bf16[192,1152]{1,0:T(8,128)(2,1)S(1)}, u32[]{:S(2)}, u32[]{:S(2)}) collective-permute-start(bf16[192,1152]{1,0:T(8,128)(2,1)S(1)} %bitcast.60), channel_id=1, source_target_pairs={{0,2},{1,3},{2,0},{3,1},{4,6},{5,7},{6,4},{7,5},{8,10},{9,11},{10,... | collective-permute-start | bytes 1327112 | tf_op jit(solution)/shard_map/dispatch/ppermute | solution.py:234
  69.4 53.5 %all-to-all-start.1 = ((bf16[128,8,768]{2,1,0:T(8,128)(2,1)}), bf16[128,8,768]{2,1,0:T(8,128)(2,1)S(1)}, u32[]{:S(2)}, u32[]{:S(2)}) async-start(bf16[128,8,768]{2,1,0:T(8,128)(2,1)} %bitcast.14), calls=%async_computation.1 | async-start | bytes 3145728 | tf_op jit(solution)/shard_map/dispatch/all_to_all | solution.py:230
  80.2 15.5 %collective-permute-start.3 = (bf16[128,7,2,128]{3,2,1,0:T(2,128)(2,1)}, bf16[128,7,2,128]{3,2,1,0:T(2,128)(2,1)S(1)}, u32[]{:S(2)}, u32[]{:S(2)}) collective-permute-start(bf16[128,7,2,128]{3,2,1,0:T(2,128)(2,1)} %all-to-all-done.2), channel_id=1, source_target_pairs={{0,1},{1,2},{2,3},{3,0},{4,5},{5,6},{6,7},{7,4},{8,9},{9,10},{10,1... | collective-permute-start | bytes 1376264 | tf_op jit(solution)/shard_map/second_hidden_in/ppermute | solution.py:234
  82.4 17.1 %collective-permute-start.4 = (bf16[128,7,2,128]{3,2,1,0:T(2,128)(2,1)}, bf16[128,7,2,128]{3,2,1,0:T(2,128)(2,1)S(1)}, u32[]{:S(2)}, u32[]{:S(2)}) collective-permute-start(bf16[128,7,2,128]{3,2,1,0:T(2,128)(2,1)} %all-to-all-done.2), channel_id=1, source_target_pairs={{0,2},{1,3},{2,0},{3,1},{4,6},{5,7},{6,4},{7,5},{8,10},{9,11},{10,... | collective-permute-start | bytes 1376264 | tf_op jit(solution)/shard_map/second_hidden_in/ppermute | solution.py:234
  86.5 21.7 %collective-permute-start.5 = (bf16[128,7,2,128]{3,2,1,0:T(2,128)(2,1)}, bf16[128,7,2,128]{3,2,1,0:T(2,128)(2,1)S(1)}, u32[]{:S(2)}, u32[]{:S(2)}) collective-permute-start(bf16[128,7,2,128]{3,2,1,0:T(2,128)(2,1)} %all-to-all-done.2), channel_id=1, source_target_pairs={{0,3},{1,0},{2,1},{3,2},{4,7},{5,4},{6,5},{7,6},{8,11},{9,8},{10,9... | collective-permute-start | bytes 1376264 | tf_op jit(solution)/shard_map/second_hidden_in/ppermute | solution.py:234
  90.3 17.9 %copy-start = (bf16[768,1152]{1,0:T(8,128)(2,1)}, bf16[768,1152]{1,0:T(8,128)(2,1)S(1)}, u32[]{:S(2)}) copy-start(bf16[768,1152]{1,0:T(8,128)(2,1)S(1)} %first_hidden.1.first_hbm) | copy-start | bytes 5308420
  108.2 14.7 %copy-start.2 = (bf16[1,768,640]{2,1,0:T(8,128)(2,1)S(1)}, bf16[1,768,640]{2,1,0:T(8,128)(2,1)}, u32[]{:S(2)}) copy-start(bf16[1,768,640]{2,1,0:T(8,128)(2,1)} %param.20) | copy-start | bytes 2949124
  108.2 14.7 %copy-start.3 = (bf16[1,768,640]{2,1,0:T(8,128)(2,1)S(1)}, bf16[1,768,640]{2,1,0:T(8,128)(2,1)}, u32[]{:S(2)}) copy-start(bf16[1,768,640]{2,1,0:T(8,128)(2,1)} %param.21) | copy-start | bytes 2949124
  109.9 1.2 copy-start.1
  130.0 6.1 %copy-start.8 = (s32[128,6]{0,1:T(8,128)S(1)}, s32[128,6]{0,1:T(8,128)}, u32[]{:S(2)}) copy-start(s32[128,6]{0,1:T(8,128)} %param.16) | copy-start | bytes 9220
  130.0 6.1 %copy-start.9 = (f32[128,6]{0,1:T(8,128)S(1)}, f32[128,6]{0,1:T(8,128)}, u32[]{:S(2)}) copy-start(f32[128,6]{0,1:T(8,128)} %param.17) | copy-start | bytes 9220
  130.0 48.8 %all-to-all-start.3 = ((bf16[128,8,768]{2,1,0:T(8,128)(2,1)}), bf16[128,8,768]{2,1,0:T(8,128)(2,1)S(1)}, u32[]{:S(2)}, u32[]{:S(2)}) async-start(bf16[128,8,768]{2,1,0:T(8,128)(2,1)} %bitcast.35), calls=%async_computation.3 | async-start | bytes 3145728 | tf_op jit(solution)/shard_map/finish/all_to_all | solution.py:230

commit v5 on v4

--- a/solution.py
+++ b/solution.py
@@ -286,8 +286,8 @@
             compiler_params=params(),
         )(moves, spread)
         part = hidden_first[0].T
-        near, far = before(part, 1), before(part, 3)
-        kept, rows, near, far = lax.optimization_barrier((kept, rows, near, far))
+        near = before(part, 1)
+        kept, rows, near = lax.optimization_barrier((kept, rows, near))
         second = [
             piece.reshape(EXP * 14, 128)[:PROWS]
             .reshape(24, 9, 8, 128)
@@ -300,7 +300,7 @@
         )(*second)
 
     with jax.named_scope("dispatch"):
-        rows, across = lax.optimization_barrier((rows, before(part, 2)))
+        rows, across, far = lax.optimization_barrier((rows, before(near, 1), before(part, 3)))
         arrived = exchange(rows.reshape(EXP, 8, WIDE)).reshape(MAIN, WIDE)
 
     with jax.named_scope("first_hidden"):

time: 181 us -> 182 us (level)
  the two profiles are of different devices: /device:TPU:14 before, /device:TPU:8 now
where the time goes in v5:
time: 182 us; the launch traced here: 181 us
  waiting for transfers between devices  94.5 us (52%)
  starting transfers between devices  64.8 us (36%)
  Pallas kernels  16.3 us (9%)
  local copies, waits for them, and re-layouts  4.56 us (3%)
    all_to_all x4, waiting for transfers between devices, exchange(): return lax.all_to_all(x, 'expert', split_axis=0, concat_axis=0, tiled=True)  65.7 us
    all_to_all x4, starting transfers between devices, exchange(): return lax.all_to_all(x, 'expert', split_axis=0, concat_axis=0, tiled=True)  46.4 us
    ppermute x6, waiting for transfers between devices, before(): return lax.ppermute(x, 'tensor', [(i, (i + shift) % 4) for i in range(4)])  28.8 us
    ppermute x6, starting transfers between devices, before(): return lax.ppermute(x, 'tensor', [(i, (i + shift) % 4) for i in range(4)])  18.4 us
    pallas_call x1, Pallas kernels, shards(): pl.pallas_call(finish, in_specs=[vmem, vmem, vmem, hbm, hbm, hbm], out_sp...  7.03 us
  transfers between devices with their start and end apart: 10, of which 7 were waited for; matrix products, arithmetic and copies ran while one was open for 1% of the time, Pallas kernels for 4%

profile of v5, /device:TPU:8, one launch (start us, length us, event | category | flops | bytes accessed | tf_op | source)
XLA Modules:
  0.0 181.2 jit_solution(11258824869243656486)
XLA Ops:
  0.0 1.9 %pad.4 = bf16[1792,128]{1,0:T(8,128)(2,1)} pad(bf16[1728,128]{1,0:T(8,128)(2,1)} %bitcast.68, bf16[]{:T(256)} %constant.5.clone.1), padding=0_64x0_0 | pad | bytes 901122 | tf_op jit(solution)/shard_map/second_hidden_out/jit(_pad)/pad | solution.py:271
  1.9 17.4 %all-to-all-start = ((bf16[128,7,2,128]{3,2,1,0:T(2,128)(2,1)}), bf16[128,7,2,128]{3,2,1,0:T(2,128)(2,1)S(1)}, u32[]{:S(2)}, u32[]{:S(2)}) async-start(bf16[128,7,2,128]{3,2,1,0:T(2,128)(2,1)} %bitcast.8), calls=%async_computation | async-start | bytes 917504 | tf_op jit(solution)/shard_map/second_hidden_out/all_to_all | solution.py:230
  19.3 3.4 %collective-permute-start = (bf16[192,1152]{1,0:T(8,128)(2,1)S(1)}, bf16[192,1152]{1,0:T(8,128)(2,1)S(1)}, u32[]{:S(2)}, u32[]{:S(2)}) collective-permute-start(bf16[192,1152]{1,0:T(8,128)(2,1)S(1)} %bitcast.58), channel_id=1, source_target_pairs={{0,1},{1,2},{2,3},{3,0},{4,5},{5,6},{6,7},{7,4},{8,9},{9,10},{10,1... | collective-permute-start | bytes 1327112 | tf_op jit(solution)/shard_map/second_hidden_in/ppermute | solution.py:234
  22.8 2.5 %dispatch.1 = bf16[1024,768]{1,0:T(8,128)(2,1)} custom-call(s32[6,128]{1,0:T(8,128)S(1)} %bitcast.61, f32[6,128]{1,0:T(8,128)S(1)} %bitcast.62, s32[1,128]{1,0:T(1,128)S(1)} %bitcast.65, bf16[128,640]{1,0:T(8,128)(2,1)S(1)} %copy-done.5), custom_call_target="tpu_custom_call" | custom-call | tf_op jit(solution)/shard_map/dispatch/pallas_call | solution.py:275
  25.2 0.1 select_reduce_fusion.1
  25.3 0.2 select_reduce_fusion.3
  25.5 0.2 select_reduce_fusion
  25.7 0.2 select_reduce_fusion.2
  25.9 0.1 pad_add_fusion.moves_ref
  26.0 12.2 %all-to-all-done.in_ref = bf16[128,7,2,128]{3,2,1,0:T(2,128)(2,1)S(1)} async-done(((bf16[128,7,2,128]{3,2,1,0:T(2,128)(2,1)}), bf16[128,7,2,128]{3,2,1,0:T(2,128)(2,1)S(1)}, u32[]{:S(2)}, u32[]{:S(2)}) %all-to-all-start) | async-done | bytes 458784 | tf_op jit(solution)/shard_map/second_hidden_out/all_to_all | solution.py:230
  38.1 1.3 second_hidden_in.2
  39.5 9.3 %all-to-all-start.2 = ((bf16[128,7,2,128]{3,2,1,0:T(2,128)(2,1)}), bf16[128,7,2,128]{3,2,1,0:T(2,128)(2,1)}, u32[]{:S(2)}, u32[]{:S(2)}) async-start(bf16[128,7,2,128]{3,2,1,0:T(2,128)(2,1)} %second_hidden_in.2), calls=%async_computation.2 | async-start | bytes 917504 | tf_op jit(solution)/shard_map/second_hidden_in/all_to_all | solution.py:230
  48.8 3.5 %collective-permute-start.2 = (bf16[192,1152]{1,0:T(8,128)(2,1)S(1)}, bf16[192,1152]{1,0:T(8,128)(2,1)S(1)}, u32[]{:S(2)}, u32[]{:S(2)}) collective-permute-start(bf16[192,1152]{1,0:T(8,128)(2,1)S(1)} %bitcast.59), channel_id=1, source_target_pairs={{0,3},{1,0},{2,1},{3,2},{4,7},{5,4},{6,5},{7,6},{8,11},{9,8},{10,9... | collective-permute-start | bytes 1327112 | tf_op jit(solution)/shard_map/dispatch/ppermute | solution.py:234
  52.2 2.4 %collective-permute-start.1 = (bf16[192,1152]{1,0:T(8,128)(2,1)S(1)}, bf16[192,1152]{1,0:T(8,128)(2,1)S(1)}, u32[]{:S(2)}, u32[]{:S(2)}) collective-permute-start(bf16[192,1152]{1,0:T(8,128)(2,1)S(1)} %collective-permute-done.one_ref), channel_id=1, source_target_pairs={{0,1},{1,2},{2,3},{3,0},{4,5},{5,6},{6,7},{7,4},{8,9},{9,10},{10,1... | collective-permute-start | bytes 1327112 | tf_op jit(solution)/shard_map/dispatch/ppermute | solution.py:234
  54.6 8.3 %collective-permute-done.2.three_ref = bf16[192,1152]{1,0:T(8,128)(2,1)S(1)} collective-permute-done((bf16[192,1152]{1,0:T(8,128)(2,1)S(1)}, bf16[192,1152]{1,0:T(8,128)(2,1)S(1)}, u32[]{:S(2)}, u32[]{:S(2)}) %collective-permute-start.2) | collective-permute-done | bytes 442400 | tf_op jit(solution)/shard_map/dispatch/ppermute | solution.py:234
  62.9 4.4 %collective-permute-done.1.two_ref = bf16[192,1152]{1,0:T(8,128)(2,1)S(1)} collective-permute-done((bf16[192,1152]{1,0:T(8,128)(2,1)S(1)}, bf16[192,1152]{1,0:T(8,128)(2,1)S(1)}, u32[]{:S(2)}, u32[]{:S(2)}) %collective-permute-start.1) | collective-permute-done | bytes 442400 | tf_op jit(solution)/shard_map/dispatch/ppermute | solution.py:234
  67.3 13.7 %all-to-all-start.1 = ((bf16[128,8,768]{2,1,0:T(8,128)(2,1)}), bf16[128,8,768]{2,1,0:T(8,128)(2,1)S(1)}, u32[]{:S(2)}, u32[]{:S(2)}) async-start(bf16[128,8,768]{2,1,0:T(8,128)(2,1)} %bitcast.14), calls=%async_computation.1 | async-start | bytes 3145728 | tf_op jit(solution)/shard_map/dispatch/all_to_all | solution.py:230
  81.0 1.9 %collective-permute-start.3 = (bf16[128,7,2,128]{3,2,1,0:T(2,128)(2,1)}, bf16[128,7,2,128]{3,2,1,0:T(2,128)(2,1)S(1)}, u32[]{:S(2)}, u32[]{:S(2)}) collective-permute-start(bf16[128,7,2,128]{3,2,1,0:T(2,128)(2,1)} %all-to-all-done.2), channel_id=1, source_target_pairs={{0,1},{1,2},{2,3},{3,0},{4,5},{5,6},{6,7},{7,4},{8,9},{9,10},{10,1... | collective-permute-start | bytes 1376264 | tf_op jit(solution)/shard_map/second_hidden_in/ppermute | solution.py:234
  82.9 3.0 %collective-permute-start.4 = (bf16[128,7,2,128]{3,2,1,0:T(2,128)(2,1)}, bf16[128,7,2,128]{3,2,1,0:T(2,128)(2,1)S(1)}, u32[]{:S(2)}, u32[]{:S(2)}) collective-permute-start(bf16[128,7,2,128]{3,2,1,0:T(2,128)(2,1)} %all-to-all-done.2), channel_id=1, source_target_pairs={{0,2},{1,3},{2,0},{3,1},{4,6},{5,7},{6,4},{7,5},{8,10},{9,11},{10,... | collective-permute-start | bytes 1376264 | tf_op jit(solution)/shard_map/second_hidden_in/ppermute | solution.py:234
  85.9 4.3 %collective-permute-start.5 = (bf16[128,7,2,128]{3,2,1,0:T(2,128)(2,1)}, bf16[128,7,2,128]{3,2,1,0:T(2,128)(2,1)S(1)}, u32[]{:S(2)}, u32[]{:S(2)}) collective-permute-start(bf16[128,7,2,128]{3,2,1,0:T(2,128)(2,1)} %all-to-all-done.2), channel_id=1, source_target_pairs={{0,3},{1,0},{2,1},{3,2},{4,7},{5,4},{6,5},{7,6},{8,11},{9,8},{10,9... | collective-permute-start | bytes 1376264 | tf_op jit(solution)/shard_map/second_hidden_in/ppermute | solution.py:234
  90.2 1.5 first_hidden.1.first_hbm
  91.7 1.4 slice.20
  93.0 13.7 %collective-permute-done.3 = bf16[128,7,2,128]{3,2,1,0:T(2,128)(2,1)S(1)} collective-permute-done((bf16[128,7,2,128]{3,2,1,0:T(2,128)(2,1)}, bf16[128,7,2,128]{3,2,1,0:T(2,128)(2,1)S(1)}, u32[]{:S(2)}, u32[]{:S(2)}) %collective-permute-start.3) | collective-permute-done | bytes 458784 | tf_op jit(solution)/shard_map/second_hidden_in/ppermute | solution.py:234
  106.8 2.5 %collective-permute-done.5 = bf16[128,7,2,128]{3,2,1,0:T(2,128)(2,1)S(1)} collective-permute-done((bf16[128,7,2,128]{3,2,1,0:T(2,128)(2,1)}, bf16[128,7,2,128]{3,2,1,0:T(2,128)(2,1)S(1)}, u32[]{:S(2)}, u32[]{:S(2)}) %collective-permute-start.5) | collective-permute-done | bytes 458784 | tf_op jit(solution)/shard_map/second_hidden_in/ppermute | solution.py:234
  109.3 1.6 second_hidden_in.3.second_hbm
  111.0 1.2 copy-done.1
  112.2 11.5 %all-to-all-done.1 = bf16[128,8,768]{2,1,0:T(8,128)(2,1)S(1)} async-done(((bf16[128,8,768]{2,1,0:T(8,128)(2,1)}), bf16[128,8,768]{2,1,0:T(8,128)(2,1)S(1)}, u32[]{:S(2)}, u32[]{:S(2)}) %all-to-all-start.1) | async-done | bytes 1572896 | tf_op jit(solution)/shard_map/dispatch/all_to_all | solution.py:230
  123.7 7.0 %finish.1 = bf16[1024,768]{1,0:T(8,128)(2,1)} custom-call(bf16[1024,768]{1,0:T(8,128)(2,1)S(1)} %bitcast.51, bf16[768,640]{1,0:T(8,128)(2,1)S(1)} %bitcast.56, bf16[768,640]{1,0:T(8,128)(2,1)S(1)} %bitcast.57, bf16[768,1152]{1,0:T(8,128)(2,1)} %copy-done, f32[768,640]{1,0:T(8,128)} %bitcast.67, bf16[1152,768]{1,0:T(8,128)(2,1)} %copy-done.1), custom_call_target="tpu_custom_call" | custom-call | tf_op jit(solution)/shard_map/finish/pallas_call | solution.py:319
  130.8 6.1 %all-to-all-start.3 = ((bf16[128,8,768]{2,1,0:T(8,128)(2,1)}), bf16[128,8,768]{2,1,0:T(8,128)(2,1)S(1)}, u32[]{:S(2)}, u32[]{:S(2)}) async-start(bf16[128,8,768]{2,1,0:T(8,128)(2,1)} %bitcast.35), calls=%async_computation.3 | async-start | bytes 3145728 | tf_op jit(solution)/shard_map/finish/all_to_all | solution.py:230
  136.9 0.7 mixing.1
  137.5 42.0 %all-to-all-done.3 = bf16[128,8,768]{2,1,0:T(8,128)(2,1)S(1)} async-done(((bf16[128,8,768]{2,1,0:T(8,128)(2,1)}), bf16[128,8,768]{2,1,0:T(8,128)(2,1)S(1)}, u32[]{:S(2)}, u32[]{:S(2)}) %all-to-all-start.3) | async-done | bytes 1572896 | tf_op jit(solution)/shard_map/finish/all_to_all | solution.py:230
  179.5 1.6 combine.1
  (31 shorter events, 0.2 us)
Async XLA Ops:
  0.0 19.3 %copy-start.4 = (bf16[1,1152,192]{1,2,0:T(8,128)(2,1)S(1)}, bf16[1,1152,192]{1,2,0:T(8,128)(2,1)}, u32[]{:S(2)}) copy-start(bf16[1,1152,192]{1,2,0:T(8,128)(2,1)} %param.15) | copy-start | bytes 1327108
  0.0 22.7 %copy-start.10 = (s32[128]{0:T(128)S(1)}, s32[128]{0:T(128)}, u32[]{:S(2)}) copy-start(s32[128]{0:T(128)} %param.22) | copy-start | bytes 1540
  0.0 22.7 %copy-start.11 = (s32[128]{0:T(128)S(1)}, s32[128]{0:T(128)}, u32[]{:S(2)}) copy-start(s32[128]{0:T(128)} %param.23) | copy-start | bytes 1540
  0.0 22.7 %copy-start.7 = (f32[128,6]{0,1:T(8,128)S(1)}, f32[128,6]{0,1:T(8,128)}, u32[]{:S(2)}) copy-start(f32[128,6]{0,1:T(8,128)} %param.14) | copy-start | bytes 9220
  0.0 22.7 %copy-start.6 = (s32[128,6]{0,1:T(8,128)S(1)}, s32[128,6]{0,1:T(8,128)}, u32[]{:S(2)}) copy-start(s32[128,6]{0,1:T(8,128)} %param.13) | copy-start | bytes 9220
  0.0 22.7 %copy-start.5 = (bf16[128,640]{1,0:T(8,128)(2,1)S(1)}, bf16[128,640]{1,0:T(8,128)(2,1)}, u32[]{:S(2)}) copy-start(bf16[128,640]{1,0:T(8,128)(2,1)} %tokens_ref.1) | copy-start | bytes 491524
  1.9 36.2 %all-to-all-start = ((bf16[128,7,2,128]{3,2,1,0:T(2,128)(2,1)}), bf16[128,7,2,128]{3,2,1,0:T(2,128)(2,1)S(1)}, u32[]{:S(2)}, u32[]{:S(2)}) async-start(bf16[128,7,2,128]{3,2,1,0:T(2,128)(2,1)} %bitcast.8), calls=%async_computation | async-start | bytes 917504 | tf_op jit(solution)/shard_map/second_hidden_out/all_to_all | solution.py:230
  19.3 20.2 %collective-permute-start = (bf16[192,1152]{1,0:T(8,128)(2,1)S(1)}, bf16[192,1152]{1,0:T(8,128)(2,1)S(1)}, u32[]{:S(2)}, u32[]{:S(2)}) collective-permute-start(bf16[192,1152]{1,0:T(8,128)(2,1)S(1)} %bitcast.58), channel_id=1, source_target_pairs={{0,1},{1,2},{2,3},{3,0},{4,5},{5,6},{6,7},{7,4},{8,9},{9,10},{10,1... | collective-permute-start | bytes 1327112 | tf_op jit(solution)/shard_map/second_hidden_in/ppermute | solution.py:234
  39.5 27.8 %all-to-all-start.2 = ((bf16[128,7,2,128]{3,2,1,0:T(2,128)(2,1)}), bf16[128,7,2,128]{3,2,1,0:T(2,128)(2,1)}, u32[]{:S(2)}, u32[]{:S(2)}) async-start(bf16[128,7,2,128]{3,2,1,0:T(2,128)(2,1)} %second_hidden_in.2), calls=%async_computation.2 | async-start | bytes 917504 | tf_op jit(solution)/shard_map/second_hidden_in/all_to_all | solution.py:230
  48.8 14.1 %collective-permute-start.2 = (bf16[192,1152]{1,0:T(8,128)(2,1)S(1)}, bf16[192,1152]{1,0:T(8,128)(2,1)S(1)}, u32[]{:S(2)}, u32[]{:S(2)}) collective-permute-start(bf16[192,1152]{1,0:T(8,128)(2,1)S(1)} %bitcast.59), channel_id=1, source_target_pairs={{0,3},{1,0},{2,1},{3,2},{4,7},{5,4},{6,5},{7,6},{8,11},{9,8},{10,9... | collective-permute-start | bytes 1327112 | tf_op jit(solution)/shard_map/dispatch/ppermute | solution.py:234
  52.2 15.0 %collective-permute-start.1 = (bf16[192,1152]{1,0:T(8,128)(2,1)S(1)}, bf16[192,1152]{1,0:T(8,128)(2,1)S(1)}, u32[]{:S(2)}, u32[]{:S(2)}) collective-permute-start(bf16[192,1152]{1,0:T(8,128)(2,1)S(1)} %collective-permute-done.one_ref), channel_id=1, source_target_pairs={{0,1},{1,2},{2,3},{3,0},{4,5},{5,6},{6,7},{7,4},{8,9},{9,10},{10,1... | collective-permute-start | bytes 1327112 | tf_op jit(solution)/shard_map/dispatch/ppermute | solution.py:234
  67.3 56.4 %all-to-all-start.1 = ((bf16[128,8,768]{2,1,0:T(8,128)(2,1)}), bf16[128,8,768]{2,1,0:T(8,128)(2,1)S(1)}, u32[]{:S(2)}, u32[]{:S(2)}) async-start(bf16[128,8,768]{2,1,0:T(8,128)(2,1)} %bitcast.14), calls=%async_computation.1 | async-start | bytes 3145728 | tf_op jit(solution)/shard_map/dispatch/all_to_all | solution.py:230
  81.0 25.7 %collective-permute-start.3 = (bf16[128,7,2,128]{3,2,1,0:T(2,128)(2,1)}, bf16[128,7,2,128]{3,2,1,0:T(2,128)(2,1)S(1)}, u32[]{:S(2)}, u32[]{:S(2)}) collective-permute-start(bf16[128,7,2,128]{3,2,1,0:T(2,128)(2,1)} %all-to-all-done.2), channel_id=1, source_target_pairs={{0,1},{1,2},{2,3},{3,0},{4,5},{5,6},{6,7},{7,4},{8,9},{9,10},{10,1... | collective-permute-start | bytes 1376264 | tf_op jit(solution)/shard_map/second_hidden_in/ppermute | solution.py:234
  82.9 23.8 %collective-permute-start.4 = (bf16[128,7,2,128]{3,2,1,0:T(2,128)(2,1)}, bf16[128,7,2,128]{3,2,1,0:T(2,128)(2,1)S(1)}, u32[]{:S(2)}, u32[]{:S(2)}) collective-permute-start(bf16[128,7,2,128]{3,2,1,0:T(2,128)(2,1)} %all-to-all-done.2), channel_id=1, source_target_pairs={{0,2},{1,3},{2,0},{3,1},{4,6},{5,7},{6,4},{7,5},{8,10},{9,11},{10,... | collective-permute-start | bytes 1376264 | tf_op jit(solution)/shard_map/second_hidden_in/ppermute | solution.py:234
  85.9 23.3 %collective-permute-start.5 = (bf16[128,7,2,128]{3,2,1,0:T(2,128)(2,1)}, bf16[128,7,2,128]{3,2,1,0:T(2,128)(2,1)S(1)}, u32[]{:S(2)}, u32[]{:S(2)}) collective-permute-start(bf16[128,7,2,128]{3,2,1,0:T(2,128)(2,1)} %all-to-all-done.2), channel_id=1, source_target_pairs={{0,3},{1,0},{2,1},{3,2},{4,7},{5,4},{6,5},{7,6},{8,11},{9,8},{10,9... | collective-permute-start | bytes 1376264 | tf_op jit(solution)/shard_map/second_hidden_in/ppermute | solution.py:234
  91.7 17.6 %copy-start = (bf16[768,1152]{1,0:T(8,128)(2,1)}, bf16[768,1152]{1,0:T(8,128)(2,1)S(1)}, u32[]{:S(2)}) copy-start(bf16[768,1152]{1,0:T(8,128)(2,1)S(1)} %first_hidden.1.first_hbm) | copy-start | bytes 5308420
  109.3 14.4 %copy-start.2 = (bf16[1,768,640]{2,1,0:T(8,128)(2,1)S(1)}, bf16[1,768,640]{2,1,0:T(8,128)(2,1)}, u32[]{:S(2)}) copy-start(bf16[1,768,640]{2,1,0:T(8,128)(2,1)} %param.20) | copy-start | bytes 2949124
  109.3 14.4 %copy-start.3 = (bf16[1,768,640]{2,1,0:T(8,128)(2,1)S(1)}, bf16[1,768,640]{2,1,0:T(8,128)(2,1)}, u32[]{:S(2)}) copy-start(bf16[1,768,640]{2,1,0:T(8,128)(2,1)} %param.21) | copy-start | bytes 2949124
  111.0 1.2 copy-start.1
  130.7 6.1 %copy-start.8 = (s32[128,6]{0,1:T(8,128)S(1)}, s32[128,6]{0,1:T(8,128)}, u32[]{:S(2)}) copy-start(s32[128,6]{0,1:T(8,128)} %param.16) | copy-start | bytes 9220
  130.7 6.1 %copy-start.9 = (f32[128,6]{0,1:T(8,128)S(1)}, f32[128,6]{0,1:T(8,128)}, u32[]{:S(2)}) copy-start(f32[128,6]{0,1:T(8,128)} %param.17) | copy-start | bytes 9220
  130.8 48.8 %all-to-all-start.3 = ((bf16[128,8,768]{2,1,0:T(8,128)(2,1)}), bf16[128,8,768]{2,1,0:T(8,128)(2,1)S(1)}, u32[]{:S(2)}, u32[]{:S(2)}) async-start(bf16[128,8,768]{2,1,0:T(8,128)(2,1)} %bitcast.35), calls=%async_computation.3 | async-start | bytes 3145728 | tf_op jit(solution)/shard_map/finish/all_to_all | solution.py:230

commit v6 on v5

--- a/solution.py
+++ b/solution.py
@@ -87,22 +87,25 @@
     return onehot(iota((EXP, ROWS), 1) == iota((EXP, ROWS), 0) * 9 + 8)
 
 
-def prepare_second(zero_ref, one_ref, two_ref, three_ref, out_ref):
-    parts = [ref[...] for ref in (zero_ref, one_ref, two_ref, three_ref)]
-    whole = jnp.concatenate(parts, axis=0)
+def prepare_second(zero_ref, one_ref, three_ref, two_low_ref, two_high_ref, out_ref):
+    refs = (zero_ref, one_ref, three_ref, two_low_ref, two_high_ref)
+    whole = jnp.concatenate([ref[...] for ref in refs], axis=0)
     for b in range(8):
         win = slice(128 * b, 128 * b + 256)
         out_ref[128 * b : 128 * b + 128, :] = mm(main_pick(b), whole[:, win], NT).astype(BF16)
     out_ref[MAIN:ROWS, :] = mm(last_pick(), whole, NT).astype(BF16)
 
 
-def prepare_first(zero_ref, one_ref, two_ref, three_ref, out_ref):
-    for n, ref in enumerate((zero_ref, one_ref, two_ref, three_ref)):
-        at = slice(n * HPART, n * HPART + HPART)
+def prepare_first(zero_ref, one_ref, three_ref, two_low_ref, two_high_ref, out_ref):
+    at = 0
+    for ref in (zero_ref, one_ref, three_ref, two_low_ref, two_high_ref):
+        to = at + ref.shape[0]
         for b in range(8):
             win = slice(128 * b, 128 * b + 256)
-            out_ref[at, 128 * b : 128 * b + 128] = mm(ref[:, win], main_pick(b), NT).astype(BF16)
-        out_ref[at, MAIN:ROWS] = mm(ref[...], last_pick(), NT).astype(BF16)
+            picked = mm(ref[:, win], main_pick(b), NT).astype(BF16)
+            out_ref[at:to, 128 * b : 128 * b + 128] = picked
+        out_ref[at:to, MAIN:ROWS] = mm(ref[...], last_pick(), NT).astype(BF16)
+        at = to
 
 
 def build_rows(route_ref, gates_ref, plan_ref, tokens_ref, out_ref, extra):
@@ -146,9 +149,9 @@
 ):
     me = lax.axis_index("tensor")
     copies, places = [], []
-    for n in range(4):
+    for n, behind in enumerate((0, 1, 3, 2)):
         at = pl.ds(n * HPART, HPART)
-        place = pl.ds(pl.multiple_of(lax.rem(me + 4 - n, 4) * HPART, HPART), HPART)
+        place = pl.ds(pl.multiple_of(lax.rem(me + 4 - behind, 4) * HPART, HPART), HPART)
         places.append(place)
         copies.append(pltpu.make_async_copy(first_hbm.at[at], first.at[at], sems.at[2 * n]))
         copies.append(
@@ -235,7 +238,9 @@
 
 
 def gather(x):
-    return [x] + [before(x, shift) for shift in (1, 2, 3)]
+    half = x.shape[0] // 2
+    near, far = before(x, 1), before(x, 3)
+    return [x, near, far, before(near[:half], 1), before(far[half:], 3)]
 
 
 def shards(
@@ -286,27 +291,21 @@
             compiler_params=params(),
         )(moves, spread)
         part = hidden_first[0].T
-        near = before(part, 1)
-        kept, rows, near = lax.optimization_barrier((kept, rows, near))
-        second = [
-            piece.reshape(EXP * 14, 128)[:PROWS]
-            .reshape(24, 9, 8, 128)
-            .transpose(0, 2, 1, 3)
-            .reshape(HPART, ROWS)
-            for piece in gather(exchange(kept))
-        ]
+        kept, rows = lax.optimization_barrier((kept, rows))
+        mine = exchange(kept).reshape(EXP * 14, 128)[:PROWS]
+        mine = mine.reshape(24, 9, 8, 128).transpose(0, 2, 1, 3).reshape(HPART, ROWS)
+        second = gather(mine)
         second = pl.pallas_call(
             prepare_second, out_shape=shape(ROWS, HID), compiler_params=params()
         )(*second)
 
     with jax.named_scope("dispatch"):
-        rows, across, far = lax.optimization_barrier((rows, before(near, 1), before(part, 3)))
         arrived = exchange(rows.reshape(EXP, 8, WIDE)).reshape(MAIN, WIDE)
 
     with jax.named_scope("first_hidden"):
         first = pl.pallas_call(
             prepare_first, out_shape=shape(HID, ROWS), compiler_params=params()
-        )(part, near, across, far)
+        )(*gather(part))
 
     with jax.named_scope("mixing"):
         mix, mix_last = pl.pallas_call(

time: 182 us -> 175 us (0.962)
  the two profiles are of different devices: /device:TPU:8 before, /device:TPU:14 now
where the time goes in v6:
time: 175 us; the launch traced here: 174 us
  waiting for transfers between devices  70.7 us (40%)
  starting transfers between devices  57.8 us (33%)
  blocking collectives  24.4 us (14%)
  Pallas kernels  15.7 us (9%)
  local copies, waits for them, and re-layouts  4.45 us (3%)
    all_to_all x3, waiting for transfers between devices, exchange(): return lax.all_to_all(x, 'expert', split_axis=0, concat_axis=0, tiled=True)  60.3 us
    all_to_all x3, starting transfers between devices, exchange(): return lax.all_to_all(x, 'expert', split_axis=0, concat_axis=0, tiled=True)  34.2 us
    all_to_all x1, blocking collectives, exchange(): return lax.all_to_all(x, 'expert', split_axis=0, concat_axis=0, tiled=True)  24.4 us
    ppermute x8, starting transfers between devices, before(): return lax.ppermute(x, 'tensor', [(i, (i + shift) % 4) for i in range(4)])  23.6 us
    ppermute x8, waiting for transfers between devices, before(): return lax.ppermute(x, 'tensor', [(i, (i + shift) % 4) for i in range(4)])  10.4 us
    pallas_call x1, Pallas kernels, shards(): pl.pallas_call(finish, in_specs=[vmem, vmem, vmem, hbm, hbm, hbm], out_sp...  7.03 us
  transfers between devices with their start and end apart: 11, of which 7 were waited for; matrix products, arithmetic and copies ran while one was open for 0% of the time, Pallas kernels for 4%

profile of v6, /device:TPU:14, one launch (start us, length us, event | category | flops | bytes accessed | tf_op | source)
XLA Modules:
  0.0 174.0 jit_solution(7238346970968569916)
XLA Ops:
  0.0 1.9 %pad.4 = bf16[1792,128]{1,0:T(8,128)(2,1)} pad(bf16[1728,128]{1,0:T(8,128)(2,1)} %bitcast.50, bf16[]{:T(256)} %constant.5.clone.1), padding=0_64x0_0 | pad | bytes 901122 | tf_op jit(solution)/shard_map/second_hidden_out/jit(_pad)/pad | solution.py:276
  1.9 17.4 %all-to-all-start = ((bf16[128,7,2,128]{3,2,1,0:T(2,128)(2,1)}), bf16[128,7,2,128]{3,2,1,0:T(2,128)(2,1)S(1)}, u32[]{:S(2)}, u32[]{:S(2)}) async-start(bf16[128,7,2,128]{3,2,1,0:T(2,128)(2,1)} %bitcast.8), calls=%async_computation | async-start | bytes 917504 | tf_op jit(solution)/shard_map/second_hidden_out/all_to_all | solution.py:233
  19.3 2.5 %dispatch.1 = bf16[1024,768]{1,0:T(8,128)(2,1)} custom-call(s32[6,128]{1,0:T(8,128)S(1)} %bitcast.42, f32[6,128]{1,0:T(8,128)S(1)} %bitcast.43, s32[1,128]{1,0:T(1,128)S(1)} %bitcast.46, bf16[128,640]{1,0:T(8,128)(2,1)S(1)} %copy-done.5), custom_call_target="tpu_custom_call" | custom-call | tf_op jit(solution)/shard_map/dispatch/pallas_call | solution.py:280
  21.9 0.2 select_reduce_fusion.3
  22.1 0.2 select_reduce_fusion
  22.3 0.2 select_reduce_fusion.2
  22.5 15.6 %all-to-all-done.in_ref = bf16[128,7,2,128]{3,2,1,0:T(2,128)(2,1)S(1)} async-done(((bf16[128,7,2,128]{3,2,1,0:T(2,128)(2,1)}), bf16[128,7,2,128]{3,2,1,0:T(2,128)(2,1)S(1)}, u32[]{:S(2)}, u32[]{:S(2)}) %all-to-all-start) | async-done | bytes 458784 | tf_op jit(solution)/shard_map/second_hidden_out/all_to_all | solution.py:233
  38.1 0.6 second_hidden_in.2
  38.7 24.4 %all_to_all.20 = bf16[128,7,2,128]{3,2,1,0:T(2,128)(2,1)S(1)} all-to-all(bf16[128,7,2,128]{3,2,1,0:T(2,128)(2,1)S(1)} %second_hidden_in.2), channel_id=1, replica_groups=mesh['expert'=128,'tensor'=4] {'expert'}, dimensions={0} | all-to-all | bytes 917504 | tf_op jit(solution)/shard_map/second_hidden_in/all_to_all | solution.py:233
  63.1 5.9 %all-to-all-start.1 = ((bf16[128,8,768]{2,1,0:T(8,128)(2,1)}), bf16[128,8,768]{2,1,0:T(8,128)(2,1)S(1)}, u32[]{:S(2)}, u32[]{:S(2)}) async-start(bf16[128,8,768]{2,1,0:T(8,128)(2,1)} %bitcast.11), calls=%async_computation.1 | async-start | bytes 3145728 | tf_op jit(solution)/shard_map/dispatch/all_to_all | solution.py:233
  69.0 2.4 %collective-permute-start = (bf16[192,1152]{1,0:T(8,128)(2,1)S(1)}, bf16[192,1152]{1,0:T(8,128)(2,1)S(1)}, u32[]{:S(2)}, u32[]{:S(2)}) collective-permute-start(bf16[192,1152]{1,0:T(8,128)(2,1)S(1)} %bitcast.39), channel_id=1, source_target_pairs={{0,1},{1,2},{2,3},{3,0},{4,5},{5,6},{6,7},{7,4},{8,9},{9,10},{10,1... | collective-permute-start | bytes 1327112 | tf_op jit(solution)/shard_map/first_hidden/ppermute | solution.py:237
  71.4 3.5 %collective-permute-start.1 = (bf16[192,1152]{1,0:T(8,128)(2,1)S(1)}, bf16[192,1152]{1,0:T(8,128)(2,1)S(1)}, u32[]{:S(2)}, u32[]{:S(2)}) collective-permute-start(bf16[192,1152]{1,0:T(8,128)(2,1)S(1)} %bitcast.40), channel_id=1, source_target_pairs={{0,3},{1,0},{2,1},{3,2},{4,7},{5,4},{6,5},{7,6},{8,11},{9,8},{10,9... | collective-permute-start | bytes 1327112 | tf_op jit(solution)/shard_map/first_hidden/ppermute | solution.py:237
  74.9 3.6 %collective-permute-start.4 = (bf16[192,1152]{1,0:T(8,128)(2,1)S(1)}, bf16[192,1152]{1,0:T(8,128)(2,1)S(1)}, u32[]{:S(2)}, u32[]{:S(2)}) collective-permute-start(bf16[192,1152]{1,0:T(8,128)(2,1)S(1)} %bitcast.34), channel_id=1, source_target_pairs={{0,1},{1,2},{2,3},{3,0},{4,5},{5,6},{6,7},{7,4},{8,9},{9,10},{10,1... | collective-permute-start | bytes 1327112 | tf_op jit(solution)/shard_map/second_hidden_in/ppermute | solution.py:237
  78.5 2.2 %collective-permute-start.5 = (bf16[192,1152]{1,0:T(8,128)(2,1)S(1)}, bf16[192,1152]{1,0:T(8,128)(2,1)S(1)}, u32[]{:S(2)}, u32[]{:S(2)}) collective-permute-start(bf16[192,1152]{1,0:T(8,128)(2,1)S(1)} %bitcast.35), channel_id=1, source_target_pairs={{0,3},{1,0},{2,1},{3,2},{4,7},{5,4},{6,5},{7,6},{8,11},{9,8},{10,9... | collective-permute-start | bytes 1327112 | tf_op jit(solution)/shard_map/second_hidden_in/ppermute | solution.py:237
  80.7 3.2 %collective-permute-done.one_ref = bf16[192,1152]{1,0:T(8,128)(2,1)S(1)} collective-permute-done((bf16[192,1152]{1,0:T(8,128)(2,1)S(1)}, bf16[192,1152]{1,0:T(8,128)(2,1)S(1)}, u32[]{:S(2)}, u32[]{:S(2)}) %collective-permute-start) | collective-permute-done | bytes 442400 | tf_op jit(solution)/shard_map/first_hidden/ppermute | solution.py:237
  83.9 3.6 %collective-permute-start.2 = (bf16[96,1152]{1,0:T(8,128)(2,1)S(1)}, bf16[96,1152]{1,0:T(8,128)(2,1)S(1)}, u32[]{:S(2)}, u32[]{:S(2)}) collective-permute-start(bf16[96,1152]{1,0:T(8,128)(2,1)S(1)} %slice.24), channel_id=1, source_target_pairs={{0,1},{1,2},{2,3},{3,0},{4,5},{5,6},{6,7},{7,4},{8,9},{9,10},{10,1... | collective-permute-start | bytes 663560 | tf_op jit(solution)/shard_map/first_hidden/ppermute | solution.py:237
  87.5 2.2 %collective-permute-start.3 = (bf16[96,1152]{1,0:T(8,128)(2,1)S(1)}, bf16[96,1152]{1,0:T(8,128)(2,1)S(1)}, u32[]{:S(2)}, u32[]{:S(2)}) collective-permute-start(bf16[96,1152]{1,0:T(8,128)(2,1)S(1)} %slice.25), channel_id=1, source_target_pairs={{0,3},{1,0},{2,1},{3,2},{4,7},{5,4},{6,5},{7,6},{8,11},{9,8},{10,9... | collective-permute-start | bytes 663560 | tf_op jit(solution)/shard_map/first_hidden/ppermute | solution.py:237
  89.8 3.6 %collective-permute-done.4.one_ref = bf16[192,1152]{1,0:T(8,128)(2,1)S(1)} collective-permute-done((bf16[192,1152]{1,0:T(8,128)(2,1)S(1)}, bf16[192,1152]{1,0:T(8,128)(2,1)S(1)}, u32[]{:S(2)}, u32[]{:S(2)}) %collective-permute-start.4) | collective-permute-done | bytes 442400 | tf_op jit(solution)/shard_map/second_hidden_in/ppermute | solution.py:237
  93.4 3.6 %collective-permute-start.6 = (bf16[96,1152]{1,0:T(8,128)(2,1)S(1)}, bf16[96,1152]{1,0:T(8,128)(2,1)S(1)}, u32[]{:S(2)}, u32[]{:S(2)}) collective-permute-start(bf16[96,1152]{1,0:T(8,128)(2,1)S(1)} %slice.27), channel_id=1, source_target_pairs={{0,1},{1,2},{2,3},{3,0},{4,5},{5,6},{6,7},{7,4},{8,9},{9,10},{10,1... | collective-permute-start | bytes 663560 | tf_op jit(solution)/shard_map/second_hidden_in/ppermute | solution.py:237
  97.0 2.4 %collective-permute-start.7 = (bf16[96,1152]{1,0:T(8,128)(2,1)S(1)}, bf16[96,1152]{1,0:T(8,128)(2,1)S(1)}, u32[]{:S(2)}, u32[]{:S(2)}) collective-permute-start(bf16[96,1152]{1,0:T(8,128)(2,1)S(1)} %slice.28), channel_id=1, source_target_pairs={{0,3},{1,0},{2,1},{3,2},{4,7},{5,4},{6,5},{7,6},{8,11},{9,8},{10,9... | collective-permute-start | bytes 663560 | tf_op jit(solution)/shard_map/second_hidden_in/ppermute | solution.py:237
  99.5 1.2 collective-permute-done.3.two_high_ref
  100.6 1.7 first_hidden.1.first_hbm
  102.3 1.2 copy-done
  103.5 2.5 %collective-permute-done.7.two_high_ref = bf16[96,1152]{1,0:T(8,128)(2,1)S(1)} collective-permute-done((bf16[96,1152]{1,0:T(8,128)(2,1)S(1)}, bf16[96,1152]{1,0:T(8,128)(2,1)S(1)}, u32[]{:S(2)}, u32[]{:S(2)}) %collective-permute-start.7) | collective-permute-done | bytes 221216 | tf_op jit(solution)/shard_map/second_hidden_in/ppermute | solution.py:237
  106.1 1.7 second_hidden_in.3.second_hbm
  107.7 1.2 copy-done.1
  108.9 2.7 %all-to-all-done.1 = bf16[128,8,768]{2,1,0:T(8,128)(2,1)S(1)} async-done(((bf16[128,8,768]{2,1,0:T(8,128)(2,1)}), bf16[128,8,768]{2,1,0:T(8,128)(2,1)S(1)}, u32[]{:S(2)}, u32[]{:S(2)}) %all-to-all-start.1) | async-done | bytes 1572896 | tf_op jit(solution)/shard_map/dispatch/all_to_all | solution.py:233
  111.7 7.0 %finish.1 = bf16[1024,768]{1,0:T(8,128)(2,1)} custom-call(bf16[1024,768]{1,0:T(8,128)(2,1)S(1)} %bitcast.33, bf16[768,640]{1,0:T(8,128)(2,1)S(1)} %bitcast.37, bf16[768,640]{1,0:T(8,128)(2,1)S(1)} %bitcast.38, bf16[768,1152]{1,0:T(8,128)(2,1)} %copy-done, f32[768,640]{1,0:T(8,128)} %bitcast.48, bf16[1152,768]{1,0:T(8,128)(2,1)} %copy-done.1), custom_call_target="tpu_custom_call" | custom-call | tf_op jit(solution)/shard_map/finish/pallas_call | solution.py:318
  118.7 11.0 %all-to-all-start.3 = ((bf16[128,8,768]{2,1,0:T(8,128)(2,1)}), bf16[128,8,768]{2,1,0:T(8,128)(2,1)S(1)}, u32[]{:S(2)}, u32[]{:S(2)}) async-start(bf16[128,8,768]{2,1,0:T(8,128)(2,1)} %bitcast.25), calls=%async_computation.3 | async-start | bytes 3145728 | tf_op jit(solution)/shard_map/finish/all_to_all | solution.py:233
  129.8 0.7 mixing.1
  130.4 42.0 %all-to-all-done.3 = bf16[128,8,768]{2,1,0:T(8,128)(2,1)S(1)} async-done(((bf16[128,8,768]{2,1,0:T(8,128)(2,1)}), bf16[128,8,768]{2,1,0:T(8,128)(2,1)S(1)}, u32[]{:S(2)}, u32[]{:S(2)}) %all-to-all-start.3) | async-done | bytes 1572896 | tf_op jit(solution)/shard_map/finish/all_to_all | solution.py:233
  172.4 1.6 combine.1
  (35 shorter events, 0.4 us)
Async XLA Ops:
  0.0 19.3 %copy-start.10 = (s32[128]{0:T(128)S(1)}, s32[128]{0:T(128)}, u32[]{:S(2)}) copy-start(s32[128]{0:T(128)} %param.22) | copy-start | bytes 1540
  0.0 19.3 %copy-start.11 = (s32[128]{0:T(128)S(1)}, s32[128]{0:T(128)}, u32[]{:S(2)}) copy-start(s32[128]{0:T(128)} %param.23) | copy-start | bytes 1540
  0.0 19.3 %copy-start.7 = (f32[128,6]{0,1:T(8,128)S(1)}, f32[128,6]{0,1:T(8,128)}, u32[]{:S(2)}) copy-start(f32[128,6]{0,1:T(8,128)} %param.14) | copy-start | bytes 9220
  0.0 19.3 %copy-start.6 = (s32[128,6]{0,1:T(8,128)S(1)}, s32[128,6]{0,1:T(8,128)}, u32[]{:S(2)}) copy-start(s32[128,6]{0,1:T(8,128)} %param.13) | copy-start | bytes 9220
  0.0 19.3 %copy-start.5 = (bf16[128,640]{1,0:T(8,128)(2,1)S(1)}, bf16[128,640]{1,0:T(8,128)(2,1)}, u32[]{:S(2)}) copy-start(bf16[128,640]{1,0:T(8,128)(2,1)} %tokens_ref.1) | copy-start | bytes 491524
  1.9 36.2 %all-to-all-start = ((bf16[128,7,2,128]{3,2,1,0:T(2,128)(2,1)}), bf16[128,7,2,128]{3,2,1,0:T(2,128)(2,1)S(1)}, u32[]{:S(2)}, u32[]{:S(2)}) async-start(bf16[128,7,2,128]{3,2,1,0:T(2,128)(2,1)} %bitcast.8), calls=%async_computation | async-start | bytes 917504 | tf_op jit(solution)/shard_map/second_hidden_out/all_to_all | solution.py:233
  63.1 5.9 %copy-start.4 = (bf16[1,1152,192]{1,2,0:T(8,128)(2,1)S(1)}, bf16[1,1152,192]{1,2,0:T(8,128)(2,1)}, u32[]{:S(2)}) copy-start(bf16[1,1152,192]{1,2,0:T(8,128)(2,1)} %param.15) | copy-start | bytes 1327108
  63.1 48.6 %all-to-all-start.1 = ((bf16[128,8,768]{2,1,0:T(8,128)(2,1)}), bf16[128,8,768]{2,1,0:T(8,128)(2,1)S(1)}, u32[]{:S(2)}, u32[]{:S(2)}) async-start(bf16[128,8,768]{2,1,0:T(8,128)(2,1)} %bitcast.11), calls=%async_computation.1 | async-start | bytes 3145728 | tf_op jit(solution)/shard_map/dispatch/all_to_all | solution.py:233
  69.0 14.9 %collective-permute-start = (bf16[192,1152]{1,0:T(8,128)(2,1)S(1)}, bf16[192,1152]{1,0:T(8,128)(2,1)S(1)}, u32[]{:S(2)}, u32[]{:S(2)}) collective-permute-start(bf16[192,1152]{1,0:T(8,128)(2,1)S(1)} %bitcast.39), channel_id=1, source_target_pairs={{0,1},{1,2},{2,3},{3,0},{4,5},{5,6},{6,7},{7,4},{8,9},{9,10},{10,1... | collective-permute-start | bytes 1327112 | tf_op jit(solution)/shard_map/first_hidden/ppermute | solution.py:237
  71.4 16.2 %collective-permute-start.1 = (bf16[192,1152]{1,0:T(8,128)(2,1)S(1)}, bf16[192,1152]{1,0:T(8,128)(2,1)S(1)}, u32[]{:S(2)}, u32[]{:S(2)}) collective-permute-start(bf16[192,1152]{1,0:T(8,128)(2,1)S(1)} %bitcast.40), channel_id=1, source_target_pairs={{0,3},{1,0},{2,1},{3,2},{4,7},{5,4},{6,5},{7,6},{8,11},{9,8},{10,9... | collective-permute-start | bytes 1327112 | tf_op jit(solution)/shard_map/first_hidden/ppermute | solution.py:237
  74.9 18.5 %collective-permute-start.4 = (bf16[192,1152]{1,0:T(8,128)(2,1)S(1)}, bf16[192,1152]{1,0:T(8,128)(2,1)S(1)}, u32[]{:S(2)}, u32[]{:S(2)}) collective-permute-start(bf16[192,1152]{1,0:T(8,128)(2,1)S(1)} %bitcast.34), channel_id=1, source_target_pairs={{0,1},{1,2},{2,3},{3,0},{4,5},{5,6},{6,7},{7,4},{8,9},{9,10},{10,1... | collective-permute-start | bytes 1327112 | tf_op jit(solution)/shard_map/second_hidden_in/ppermute | solution.py:237
  78.5 18.5 %collective-permute-start.5 = (bf16[192,1152]{1,0:T(8,128)(2,1)S(1)}, bf16[192,1152]{1,0:T(8,128)(2,1)S(1)}, u32[]{:S(2)}, u32[]{:S(2)}) collective-permute-start(bf16[192,1152]{1,0:T(8,128)(2,1)S(1)} %bitcast.35), channel_id=1, source_target_pairs={{0,3},{1,0},{2,1},{3,2},{4,7},{5,4},{6,5},{7,6},{8,11},{9,8},{10,9... | collective-permute-start | bytes 1327112 | tf_op jit(solution)/shard_map/second_hidden_in/ppermute | solution.py:237
  83.9 15.6 %collective-permute-start.2 = (bf16[96,1152]{1,0:T(8,128)(2,1)S(1)}, bf16[96,1152]{1,0:T(8,128)(2,1)S(1)}, u32[]{:S(2)}, u32[]{:S(2)}) collective-permute-start(bf16[96,1152]{1,0:T(8,128)(2,1)S(1)} %slice.24), channel_id=1, source_target_pairs={{0,1},{1,2},{2,3},{3,0},{4,5},{5,6},{6,7},{7,4},{8,9},{9,10},{10,1... | collective-permute-start | bytes 663560 | tf_op jit(solution)/shard_map/first_hidden/ppermute | solution.py:237
  87.5 13.1 %collective-permute-start.3 = (bf16[96,1152]{1,0:T(8,128)(2,1)S(1)}, bf16[96,1152]{1,0:T(8,128)(2,1)S(1)}, u32[]{:S(2)}, u32[]{:S(2)}) collective-permute-start(bf16[96,1152]{1,0:T(8,128)(2,1)S(1)} %slice.25), channel_id=1, source_target_pairs={{0,3},{1,0},{2,1},{3,2},{4,7},{5,4},{6,5},{7,6},{8,11},{9,8},{10,9... | collective-permute-start | bytes 663560 | tf_op jit(solution)/shard_map/first_hidden/ppermute | solution.py:237
  93.4 10.2 %collective-permute-start.6 = (bf16[96,1152]{1,0:T(8,128)(2,1)S(1)}, bf16[96,1152]{1,0:T(8,128)(2,1)S(1)}, u32[]{:S(2)}, u32[]{:S(2)}) collective-permute-start(bf16[96,1152]{1,0:T(8,128)(2,1)S(1)} %slice.27), channel_id=1, source_target_pairs={{0,1},{1,2},{2,3},{3,0},{4,5},{5,6},{6,7},{7,4},{8,9},{9,10},{10,1... | collective-permute-start | bytes 663560 | tf_op jit(solution)/shard_map/second_hidden_in/ppermute | solution.py:237
  97.0 9.0 %collective-permute-start.7 = (bf16[96,1152]{1,0:T(8,128)(2,1)S(1)}, bf16[96,1152]{1,0:T(8,128)(2,1)S(1)}, u32[]{:S(2)}, u32[]{:S(2)}) collective-permute-start(bf16[96,1152]{1,0:T(8,128)(2,1)S(1)} %slice.28), channel_id=1, source_target_pairs={{0,3},{1,0},{2,1},{3,2},{4,7},{5,4},{6,5},{7,6},{8,11},{9,8},{10,9... | collective-permute-start | bytes 663560 | tf_op jit(solution)/shard_map/second_hidden_in/ppermute | solution.py:237
  102.3 1.2 copy-start
  103.5 8.1 %copy-start.2 = (bf16[1,768,640]{2,1,0:T(8,128)(2,1)S(1)}, bf16[1,768,640]{2,1,0:T(8,128)(2,1)}, u32[]{:S(2)}) copy-start(bf16[1,768,640]{2,1,0:T(8,128)(2,1)} %param.20) | copy-start | bytes 2949124
  103.5 8.1 %copy-start.3 = (bf16[1,768,640]{2,1,0:T(8,128)(2,1)S(1)}, bf16[1,768,640]{2,1,0:T(8,128)(2,1)}, u32[]{:S(2)}) copy-start(bf16[1,768,640]{2,1,0:T(8,128)(2,1)} %param.21) | copy-start | bytes 2949124
  107.7 1.2 copy-start.1
  118.7 11.1 %copy-start.8 = (s32[128,6]{0,1:T(8,128)S(1)}, s32[128,6]{0,1:T(8,128)}, u32[]{:S(2)}) copy-start(s32[128,6]{0,1:T(8,128)} %param.16) | copy-start | bytes 9220
  118.7 11.1 %copy-start.9 = (f32[128,6]{0,1:T(8,128)S(1)}, f32[128,6]{0,1:T(8,128)}, u32[]{:S(2)}) copy-start(f32[128,6]{0,1:T(8,128)} %param.17) | copy-start | bytes 9220
  118.7 53.7 %all-to-all-start.3 = ((bf16[128,8,768]{2,1,0:T(8,128)(2,1)}), bf16[128,8,768]{2,1,0:T(8,128)(2,1)S(1)}, u32[]{:S(2)}, u32[]{:S(2)}) async-start(bf16[128,8,768]{2,1,0:T(8,128)(2,1)} %bitcast.25), calls=%async_computation.3 | async-start | bytes 3145728 | tf_op jit(solution)/shard_map/finish/all_to_all | solution.py:233

commit v7 on v6

--- a/solution.py
+++ b/solution.py
@@ -87,8 +87,8 @@
     return onehot(iota((EXP, ROWS), 1) == iota((EXP, ROWS), 0) * 9 + 8)
 
 
-def prepare_second(zero_ref, one_ref, three_ref, two_low_ref, two_high_ref, out_ref):
-    refs = (zero_ref, one_ref, three_ref, two_low_ref, two_high_ref)
+def prepare_second(one_ref, three_ref, two_low_ref, two_high_ref, zero_ref, out_ref):
+    refs = (one_ref, three_ref, two_low_ref, two_high_ref, zero_ref)
     whole = jnp.concatenate([ref[...] for ref in refs], axis=0)
     for b in range(8):
         win = slice(128 * b, 128 * b + 256)
@@ -96,16 +96,11 @@
     out_ref[MAIN:ROWS, :] = mm(last_pick(), whole, NT).astype(BF16)
 
 
-def prepare_first(zero_ref, one_ref, three_ref, two_low_ref, two_high_ref, out_ref):
-    at = 0
-    for ref in (zero_ref, one_ref, three_ref, two_low_ref, two_high_ref):
-        to = at + ref.shape[0]
-        for b in range(8):
-            win = slice(128 * b, 128 * b + 256)
-            picked = mm(ref[:, win], main_pick(b), NT).astype(BF16)
-            out_ref[at:to, 128 * b : 128 * b + 128] = picked
-        out_ref[at:to, MAIN:ROWS] = mm(ref[...], last_pick(), NT).astype(BF16)
-        at = to
+def prepare_first(h_ref, out_ref):
+    for b in range(8):
+        win = slice(128 * b, 128 * b + 256)
+        out_ref[:, 128 * b : 128 * b + 128] = mm(h_ref[:, win], main_pick(b), NT).astype(BF16)
+    out_ref[:, MAIN:ROWS] = mm(h_ref[...], last_pick(), NT).astype(BF16)
 
 
 def build_rows(route_ref, gates_ref, plan_ref, tokens_ref, out_ref, extra):
@@ -144,36 +139,46 @@
 
 
 def finish(
-    payload_ref, one, two, first_hbm, master_hbm, second_hbm, out_hbm,
-    first, master, second, weight, rows, extra, out, sems,
+    payload_ref, near_ref, far_ref, low_ref, high_ref, own_hbm, moments_hbm, master_hbm, second_hbm, out_hbm,
+    own, moments, master, second, weight, gradients, rows, extra, out, sems,
 ):
     me = lax.axis_index("tensor")
-    copies, places = [], []
-    for n, behind in enumerate((0, 1, 3, 2)):
+    mine = pltpu.make_async_copy(own_hbm, own, sems.at[8])
+    mine.start()
+    copies = []
+    for n, behind in enumerate((1, 3, 2, 0)):
+        place = pl.ds(pl.multiple_of(lax.rem(me + 4 - behind, 4) * HPART, HPART), HPART)
         at = pl.ds(n * HPART, HPART)
-        place = pl.ds(pl.multiple_of(lax.rem(me + 4 - behind, 4) * HPART, HPART), HPART)
-        places.append(place)
-        copies.append(pltpu.make_async_copy(first_hbm.at[at], first.at[at], sems.at[2 * n]))
-        copies.append(
-            pltpu.make_async_copy(master_hbm.at[place], master.at[at], sems.at[2 * n + 1])
+        pair = (
+            pltpu.make_async_copy(moments_hbm.at[:, place], moments.at[:, at], sems.at[2 * n]),
+            pltpu.make_async_copy(master_hbm.at[place], master.at[at], sems.at[2 * n + 1]),
         )
-    copies.append(pltpu.make_async_copy(second_hbm, second, sems.at[8]))
-    for copy in copies:
-        copy.start()
+        copies.append(pair)
+        for copy in pair:
+            copy.start()
+    rest = pltpu.make_async_copy(second_hbm, second, sems.at[9])
+    rest.start()
 
     rows[0:MAIN, :] = payload_ref[:, 0:COLS]
     rows[MAIN:ROWS, :] = last_rows(payload_ref, extra)
+    at = 0
+    for ref in (near_ref, far_ref, low_ref, high_ref, own):
+        if ref is own:
+            mine.wait()
+        to = at + ref.shape[0]
+        gradients[at:to, :] = mm(ref[...], rows[...])
+        at = to
     for n in range(4):
         at = slice(n * HPART, n * HPART + HPART)
-        copies[2 * n].wait()
-        gradient = mm(first[at, :], rows[...])
-        copies[2 * n + 1].wait()
-        moment_new = ONE_OLD * one[places[n], :].astype(F32) + ONE_NEW * gradient
-        moment_two = TWO_OLD * two[places[n], :].astype(F32) + TWO_NEW * gradient * gradient
+        for copy in copies[n]:
+            copy.wait()
+        gradient = gradients[at, :]
+        moment_new = ONE_OLD * moments[0, at].astype(F32) + ONE_NEW * gradient
+        moment_two = TWO_OLD * moments[1, at].astype(F32) + TWO_NEW * gradient * gradient
         root = moment_two * lax.rsqrt(moment_two)
         updated = KEEP * master[at, :] - moment_new * pl.reciprocal(root + EPSILON)
         weight[at, :] = updated.astype(BF16)
-    copies[-1].wait()
+    rest.wait()
 
     extra[...] = jnp.zeros_like(extra)
     sent = []
@@ -190,7 +195,7 @@
         cols = pl.ds(start, stop - start)
         sent.append(
             pltpu.make_async_copy(
-                out.at[:, cols], out_hbm.at[:, cols], sems.at[9 + n]
+                out.at[:, cols], out_hbm.at[:, cols], sems.at[10 + n]
             )
         )
         sent[-1].start()
@@ -240,7 +245,7 @@
 def gather(x):
     half = x.shape[0] // 2
     near, far = before(x, 1), before(x, 3)
-    return [x, near, far, before(near[:half], 1), before(far[half:], 3)]
+    return [near, far, before(near[:half], 1), before(far[half:], 3)]
 
 
 def shards(
@@ -290,22 +295,23 @@
             in_specs=[smem, vmem],
             compiler_params=params(),
         )(moves, spread)
-        part = hidden_first[0].T
-        kept, rows = lax.optimization_barrier((kept, rows))
+        part = pl.pallas_call(
+            prepare_first, out_shape=shape(HPART, ROWS), compiler_params=params()
+        )(hidden_first[0].T)
+        moments = jnp.stack([moment_one[0], moment_two[0]])
+        kept, rows, part, moments = lax.optimization_barrier((kept, rows, part, moments))
         mine = exchange(kept).reshape(EXP * 14, 128)[:PROWS]
         mine = mine.reshape(24, 9, 8, 128).transpose(0, 2, 1, 3).reshape(HPART, ROWS)
-        second = gather(mine)
+        second = [*gather(mine), mine]
         second = pl.pallas_call(
-            prepare_second, out_shape=shape(ROWS, HID), compiler_params=params()
+            prepare_second, out_shape=shape(ROWS, HID), compiler_params=params(), cost_estimate=pl.CostEstimate(flops=3*1000*1000000, bytes_accessed=0, transcendentals=0)
         )(*second)
 
     with jax.named_scope("dispatch"):
         arrived = exchange(rows.reshape(EXP, 8, WIDE)).reshape(MAIN, WIDE)
 
     with jax.named_scope("first_hidden"):
-        first = pl.pallas_call(
-            prepare_first, out_shape=shape(HID, ROWS), compiler_params=params()
-        )(*gather(part))
+        first = gather(part)
 
     with jax.named_scope("mixing"):
         mix, mix_last = pl.pallas_call(
@@ -317,21 +323,23 @@
     with jax.named_scope("finish"):
         produced = pl.pallas_call(
             finish,
-            in_specs=[vmem, vmem, vmem, hbm, hbm, hbm],
+            in_specs=[vmem] * 5 + [hbm] * 4,
             out_specs=hbm,
             out_shape=shape(MAIN, WIDE),
             scratch_shapes=[
-                pltpu.VMEM((HID, ROWS), BF16),
+                pltpu.VMEM((HPART, ROWS), BF16),
+                pltpu.VMEM((2, HID, COLS), BF16),
                 pltpu.VMEM((HID, COLS), F32),
                 pltpu.VMEM((ROWS, HID), BF16),
                 pltpu.VMEM((HID, COLS), BF16),
+                pltpu.VMEM((HID, COLS), F32),
                 pltpu.VMEM((ROWS, COLS), BF16),
                 extra,
                 pltpu.VMEM((MAIN, WIDE), BF16),
-                pltpu.SemaphoreType.DMA((12,)),
+                pltpu.SemaphoreType.DMA((13,)),
             ],
             compiler_params=params(48),
-        )(arrived, moment_one[0], moment_two[0], first, master[0], second)
+        )(arrived, *first, part, moments, master[0], second)
         returned = exchange(produced.reshape(EXP, 8, WIDE)).reshape(MAIN, WIDE)
 
     with jax.named_scope("combine"):

time: 175 us -> 172 us (0.983)
  starting transfers between devices: 57.8 us -> 55 us
    all_to_all x3, starting transfers between devices: 34.2 us -> 31.4 us  [exchange(): return lax.all_to_all(x, 'expert', split_axis=0, concat_axis=0, tiled=True)]
  transfers between devices with their start and end apart: 11 -> 11, of which waited for: 7 -> 7; matrix products, arithmetic and copies ran while one was open for 0% -> 1% of each run, Pallas kernels for 4% -> 3%
where the time goes in v7:
time: 172 us; the launch traced here: 171 us
  waiting for transfers between devices  71.6 us (42%)
  starting transfers between devices  55 us (32%)
  blocking collectives  24.4 us (14%)
  Pallas kernels  14.4 us (8%)
  local copies, waits for them, and re-layouts  3.22 us (2%)
  other arithmetic  2.26 us (1%)
    all_to_all x3, waiting for transfers between devices, exchange(): return lax.all_to_all(x, 'expert', split_axis=0, concat_axis=0, tiled=True)  61 us
    all_to_all x3, starting transfers between devices, exchange(): return lax.all_to_all(x, 'expert', split_axis=0, concat_axis=0, tiled=True)  31.4 us
    all_to_all x1, blocking collectives, exchange(): return lax.all_to_all(x, 'expert', split_axis=0, concat_axis=0, tiled=True)  24.4 us
    ppermute x8, starting transfers between devices, before(): return lax.ppermute(x, 'tensor', [(i, (i + shift) % 4) for i in range(4)])  23.6 us
    ppermute x8, waiting for transfers between devices, before(): return lax.ppermute(x, 'tensor', [(i, (i + shift) % 4) for i in range(4)])  10.5 us
    pallas_call x1, Pallas kernels, shards(): pl.pallas_call(finish, in_specs=[vmem] * 5 + [hbm] * 4, out_specs=hbm, ou...  6.91 us
  transfers between devices with their start and end apart: 11, of which 7 were waited for; matrix products, arithmetic and copies ran while one was open for 1% of the time, Pallas kernels for 3%

profile of v7, /device:TPU:14, one launch (start us, length us, event | category | flops | bytes accessed | tf_op | source)
XLA Modules:
  0.0 171.1 jit_solution(6120893167497243838)
XLA Ops:
  0.0 1.9 %pad.4 = bf16[1792,128]{1,0:T(8,128)(2,1)} pad(bf16[1728,128]{1,0:T(8,128)(2,1)} %bitcast.44, bf16[]{:T(256)} %constant.5.clone.1), padding=0_64x0_0 | pad | bytes 901122 | tf_op jit(solution)/shard_map/second_hidden_out/jit(_pad)/pad | solution.py:281
  1.9 17.5 %all-to-all-start = ((bf16[128,7,2,128]{3,2,1,0:T(2,128)(2,1)}), bf16[128,7,2,128]{3,2,1,0:T(2,128)(2,1)S(1)}, u32[]{:S(2)}, u32[]{:S(2)}) async-start(bf16[128,7,2,128]{3,2,1,0:T(2,128)(2,1)} %bitcast.8), calls=%async_computation | async-start | bytes 917504 | tf_op jit(solution)/shard_map/second_hidden_out/all_to_all | solution.py:238
  19.4 0.5 second_hidden_in.4.own_hbm
  20.0 2.5 %dispatch.1 = bf16[1024,768]{1,0:T(8,128)(2,1)} custom-call(s32[6,128]{1,0:T(8,128)S(1)} %bitcast.36, f32[6,128]{1,0:T(8,128)S(1)} %bitcast.37, s32[1,128]{1,0:T(1,128)S(1)} %bitcast.40, bf16[128,640]{1,0:T(8,128)(2,1)S(1)} %copy-done.2), custom_call_target="tpu_custom_call" | custom-call | tf_op jit(solution)/shard_map/dispatch/pallas_call | solution.py:285
  22.6 0.2 select_reduce_fusion.3
  22.8 0.2 select_reduce_fusion
  23.0 0.2 select_reduce_fusion.2
  23.2 1.5 pad_maximum_fusion.moments_hbm
  24.8 13.5 %all-to-all-done.in_ref = bf16[128,7,2,128]{3,2,1,0:T(2,128)(2,1)S(1)} async-done(((bf16[128,7,2,128]{3,2,1,0:T(2,128)(2,1)}), bf16[128,7,2,128]{3,2,1,0:T(2,128)(2,1)S(1)}, u32[]{:S(2)}, u32[]{:S(2)}) %all-to-all-start) | async-done | bytes 458784 | tf_op jit(solution)/shard_map/second_hidden_out/all_to_all | solution.py:238
  38.3 0.6 second_hidden_in.3
  38.9 24.4 %all_to_all.20 = bf16[128,7,2,128]{3,2,1,0:T(2,128)(2,1)S(1)} all-to-all(bf16[128,7,2,128]{3,2,1,0:T(2,128)(2,1)S(1)} %second_hidden_in.3), channel_id=1, replica_groups=mesh['expert'=128,'tensor'=4] {'expert'}, dimensions={0} | all-to-all | bytes 917504 | tf_op jit(solution)/shard_map/second_hidden_in/all_to_all | solution.py:238
  63.2 5.7 %all-to-all-start.1 = ((bf16[128,8,768]{2,1,0:T(8,128)(2,1)}), bf16[128,8,768]{2,1,0:T(8,128)(2,1)S(1)}, u32[]{:S(2)}, u32[]{:S(2)}) async-start(bf16[128,8,768]{2,1,0:T(8,128)(2,1)} %bitcast.13), calls=%async_computation.1 | async-start | bytes 3145728 | tf_op jit(solution)/shard_map/dispatch/all_to_all | solution.py:238
  69.0 2.4 %collective-permute-start.4 = (bf16[192,1152]{1,0:T(8,128)(2,1)S(1)}, bf16[192,1152]{1,0:T(8,128)(2,1)S(1)}, u32[]{:S(2)}, u32[]{:S(2)}) collective-permute-start(bf16[192,1152]{1,0:T(8,128)(2,1)S(1)} %bitcast.33), channel_id=1, source_target_pairs={{0,1},{1,2},{2,3},{3,0},{4,5},{5,6},{6,7},{7,4},{8,9},{9,10},{10,1... | collective-permute-start | bytes 1327112 | tf_op jit(solution)/shard_map/second_hidden_in/ppermute | solution.py:242
  71.4 3.5 %collective-permute-start.5 = (bf16[192,1152]{1,0:T(8,128)(2,1)S(1)}, bf16[192,1152]{1,0:T(8,128)(2,1)S(1)}, u32[]{:S(2)}, u32[]{:S(2)}) collective-permute-start(bf16[192,1152]{1,0:T(8,128)(2,1)S(1)} %bitcast.34), channel_id=1, source_target_pairs={{0,3},{1,0},{2,1},{3,2},{4,7},{5,4},{6,5},{7,6},{8,11},{9,8},{10,9... | collective-permute-start | bytes 1327112 | tf_op jit(solution)/shard_map/second_hidden_in/ppermute | solution.py:242
  74.9 3.6 %collective-permute-start = (bf16[192,1152]{1,0:T(8,128)(2,1)S(1)}, bf16[192,1152]{1,0:T(8,128)(2,1)S(1)}, u32[]{:S(2)}, u32[]{:S(2)}) collective-permute-start(bf16[192,1152]{1,0:T(8,128)(2,1)S(1)} %second_hidden_in.4.own_hbm), channel_id=1, source_target_pairs={{0,1},{1,2},{2,3},{3,0},{4,5},{5,6},{6,7},{7,4},{8,9},{9,10},{10,1... | collective-permute-start | bytes 1327112 | tf_op jit(solution)/shard_map/first_hidden/ppermute | solution.py:242
  78.5 2.2 %collective-permute-start.1 = (bf16[192,1152]{1,0:T(8,128)(2,1)S(1)}, bf16[192,1152]{1,0:T(8,128)(2,1)S(1)}, u32[]{:S(2)}, u32[]{:S(2)}) collective-permute-start(bf16[192,1152]{1,0:T(8,128)(2,1)S(1)} %second_hidden_in.4.own_hbm), channel_id=1, source_target_pairs={{0,3},{1,0},{2,1},{3,2},{4,7},{5,4},{6,5},{7,6},{8,11},{9,8},{10,9... | collective-permute-start | bytes 1327112 | tf_op jit(solution)/shard_map/first_hidden/ppermute | solution.py:242
  80.7 3.2 %collective-permute-done.4.one_ref = bf16[192,1152]{1,0:T(8,128)(2,1)S(1)} collective-permute-done((bf16[192,1152]{1,0:T(8,128)(2,1)S(1)}, bf16[192,1152]{1,0:T(8,128)(2,1)S(1)}, u32[]{:S(2)}, u32[]{:S(2)}) %collective-permute-start.4) | collective-permute-done | bytes 442400 | tf_op jit(solution)/shard_map/second_hidden_in/ppermute | solution.py:242
  83.9 3.6 %collective-permute-start.6 = (bf16[96,1152]{1,0:T(8,128)(2,1)S(1)}, bf16[96,1152]{1,0:T(8,128)(2,1)S(1)}, u32[]{:S(2)}, u32[]{:S(2)}) collective-permute-start(bf16[96,1152]{1,0:T(8,128)(2,1)S(1)} %slice.27), channel_id=1, source_target_pairs={{0,1},{1,2},{2,3},{3,0},{4,5},{5,6},{6,7},{7,4},{8,9},{9,10},{10,1... | collective-permute-start | bytes 663560 | tf_op jit(solution)/shard_map/second_hidden_in/ppermute | solution.py:242
  87.6 2.2 %collective-permute-start.7 = (bf16[96,1152]{1,0:T(8,128)(2,1)S(1)}, bf16[96,1152]{1,0:T(8,128)(2,1)S(1)}, u32[]{:S(2)}, u32[]{:S(2)}) collective-permute-start(bf16[96,1152]{1,0:T(8,128)(2,1)S(1)} %slice.28), channel_id=1, source_target_pairs={{0,3},{1,0},{2,1},{3,2},{4,7},{5,4},{6,5},{7,6},{8,11},{9,8},{10,9... | collective-permute-start | bytes 663560 | tf_op jit(solution)/shard_map/second_hidden_in/ppermute | solution.py:242
  89.8 3.6 %collective-permute-done.near_ref = bf16[192,1152]{1,0:T(8,128)(2,1)S(1)} collective-permute-done((bf16[192,1152]{1,0:T(8,128)(2,1)S(1)}, bf16[192,1152]{1,0:T(8,128)(2,1)S(1)}, u32[]{:S(2)}, u32[]{:S(2)}) %collective-permute-start) | collective-permute-done | bytes 442400 | tf_op jit(solution)/shard_map/first_hidden/ppermute | solution.py:242
  93.4 3.6 %collective-permute-start.2 = (bf16[96,1152]{1,0:T(8,128)(2,1)S(1)}, bf16[96,1152]{1,0:T(8,128)(2,1)S(1)}, u32[]{:S(2)}, u32[]{:S(2)}) collective-permute-start(bf16[96,1152]{1,0:T(8,128)(2,1)S(1)} %slice.24), channel_id=1, source_target_pairs={{0,1},{1,2},{2,3},{3,0},{4,5},{5,6},{6,7},{7,4},{8,9},{9,10},{10,1... | collective-permute-start | bytes 663560 | tf_op jit(solution)/shard_map/first_hidden/ppermute | solution.py:242
  97.1 2.4 %collective-permute-start.3 = (bf16[96,1152]{1,0:T(8,128)(2,1)S(1)}, bf16[96,1152]{1,0:T(8,128)(2,1)S(1)}, u32[]{:S(2)}, u32[]{:S(2)}) collective-permute-start(bf16[96,1152]{1,0:T(8,128)(2,1)S(1)} %slice.25), channel_id=1, source_target_pairs={{0,3},{1,0},{2,1},{3,2},{4,7},{5,4},{6,5},{7,6},{8,11},{9,8},{10,9... | collective-permute-start | bytes 663560 | tf_op jit(solution)/shard_map/first_hidden/ppermute | solution.py:242
  99.5 1.2 collective-permute-done.7.two_high_ref
  100.7 1.7 second_hidden_in.5.second_hbm
  102.3 1.2 copy-done
  103.5 2.6 %collective-permute-done.3.high_ref = bf16[96,1152]{1,0:T(8,128)(2,1)S(1)} collective-permute-done((bf16[96,1152]{1,0:T(8,128)(2,1)S(1)}, bf16[96,1152]{1,0:T(8,128)(2,1)S(1)}, u32[]{:S(2)}, u32[]{:S(2)}) %collective-permute-start.3) | collective-permute-done | bytes 221216 | tf_op jit(solution)/shard_map/first_hidden/ppermute | solution.py:242
  106.1 5.6 %all-to-all-done.1 = bf16[128,8,768]{2,1,0:T(8,128)(2,1)S(1)} async-done(((bf16[128,8,768]{2,1,0:T(8,128)(2,1)}), bf16[128,8,768]{2,1,0:T(8,128)(2,1)S(1)}, u32[]{:S(2)}, u32[]{:S(2)}) %all-to-all-start.1) | async-done | bytes 1572896 | tf_op jit(solution)/shard_map/dispatch/all_to_all | solution.py:238
  111.7 6.9 %finish.1 = bf16[1024,768]{1,0:T(8,128)(2,1)} custom-call(bf16[1024,768]{1,0:T(8,128)(2,1)S(1)} %bitcast.31, bf16[192,1152]{1,0:T(8,128)(2,1)S(1)} %collective-permute-done.near_ref, bf16[192,1152]{1,0:T(8,128)(2,1)S(1)} %collective-permute-done.1.far_ref, bf16[96,1152]{1,0:T(8,128)(2,1)S(1)} %collective-permute-done.2.low_ref, ...), custom_call_target="tpu_custom_call" | custom-call | tf_op jit(solution)/shard_map/finish/pallas_call | solution.py:324
  118.6 8.2 %all-to-all-start.3 = ((bf16[128,8,768]{2,1,0:T(8,128)(2,1)}), bf16[128,8,768]{2,1,0:T(8,128)(2,1)S(1)}, u32[]{:S(2)}, u32[]{:S(2)}) async-start(bf16[128,8,768]{2,1,0:T(8,128)(2,1)} %bitcast.22), calls=%async_computation.3 | async-start | bytes 3145728 | tf_op jit(solution)/shard_map/finish/all_to_all | solution.py:238
  126.8 0.7 mixing.1
  127.5 42.0 %all-to-all-done.3 = bf16[128,8,768]{2,1,0:T(8,128)(2,1)S(1)} async-done(((bf16[128,8,768]{2,1,0:T(8,128)(2,1)}), bf16[128,8,768]{2,1,0:T(8,128)(2,1)S(1)}, u32[]{:S(2)}, u32[]{:S(2)}) %all-to-all-start.3) | async-done | bytes 1572896 | tf_op jit(solution)/shard_map/finish/all_to_all | solution.py:238
  169.5 1.6 combine.1
  (34 shorter events, 0.4 us)
Async XLA Ops:
  0.0 19.4 %copy-start.1 = (bf16[1,1152,192]{1,2,0:T(8,128)(2,1)S(1)}, bf16[1,1152,192]{1,2,0:T(8,128)(2,1)}, u32[]{:S(2)}) copy-start(bf16[1,1152,192]{1,2,0:T(8,128)(2,1)} %param.15) | copy-start | bytes 1327108
  0.0 19.9 %copy-start.7 = (s32[128]{0:T(128)S(1)}, s32[128]{0:T(128)}, u32[]{:S(2)}) copy-start(s32[128]{0:T(128)} %param.22) | copy-start | bytes 1540
  0.0 19.9 %copy-start.10 = (s32[128]{0:T(128)S(1)}, s32[128]{0:T(128)}, u32[]{:S(2)}) copy-start(s32[128]{0:T(128)} %param.23) | copy-start | bytes 1540
  0.0 20.0 %copy-start.4 = (f32[128,6]{0,1:T(8,128)S(1)}, f32[128,6]{0,1:T(8,128)}, u32[]{:S(2)}) copy-start(f32[128,6]{0,1:T(8,128)} %param.14) | copy-start | bytes 9220
  0.0 20.0 %copy-start.3 = (s32[128,6]{0,1:T(8,128)S(1)}, s32[128,6]{0,1:T(8,128)}, u32[]{:S(2)}) copy-start(s32[128,6]{0,1:T(8,128)} %param.13) | copy-start | bytes 9220
  0.0 20.0 %copy-start.2 = (bf16[128,640]{1,0:T(8,128)(2,1)S(1)}, bf16[128,640]{1,0:T(8,128)(2,1)}, u32[]{:S(2)}) copy-start(bf16[128,640]{1,0:T(8,128)(2,1)} %tokens_ref.1) | copy-start | bytes 491524
  1.9 21.3 %copy-start.8 = (bf16[1,768,640]{2,1,0:T(8,128)(2,1)S(1)}, bf16[1,768,640]{2,1,0:T(8,128)(2,1)}, u32[]{:S(2)}) copy-start(bf16[1,768,640]{2,1,0:T(8,128)(2,1)} %param.21) | copy-start | bytes 2949124
  1.9 21.3 %copy-start.9 = (bf16[1,768,640]{2,1,0:T(8,128)(2,1)S(1)}, bf16[1,768,640]{2,1,0:T(8,128)(2,1)}, u32[]{:S(2)}) copy-start(bf16[1,768,640]{2,1,0:T(8,128)(2,1)} %param.20) | copy-start | bytes 2949124
  1.9 36.4 %all-to-all-start = ((bf16[128,7,2,128]{3,2,1,0:T(2,128)(2,1)}), bf16[128,7,2,128]{3,2,1,0:T(2,128)(2,1)S(1)}, u32[]{:S(2)}, u32[]{:S(2)}) async-start(bf16[128,7,2,128]{3,2,1,0:T(2,128)(2,1)} %bitcast.8), calls=%async_computation | async-start | bytes 917504 | tf_op jit(solution)/shard_map/second_hidden_out/all_to_all | solution.py:238
  63.2 48.4 %all-to-all-start.1 = ((bf16[128,8,768]{2,1,0:T(8,128)(2,1)}), bf16[128,8,768]{2,1,0:T(8,128)(2,1)S(1)}, u32[]{:S(2)}, u32[]{:S(2)}) async-start(bf16[128,8,768]{2,1,0:T(8,128)(2,1)} %bitcast.13), calls=%async_computation.1 | async-start | bytes 3145728 | tf_op jit(solution)/shard_map/dispatch/all_to_all | solution.py:238
  69.0 14.9 %collective-permute-start.4 = (bf16[192,1152]{1,0:T(8,128)(2,1)S(1)}, bf16[192,1152]{1,0:T(8,128)(2,1)S(1)}, u32[]{:S(2)}, u32[]{:S(2)}) collective-permute-start(bf16[192,1152]{1,0:T(8,128)(2,1)S(1)} %bitcast.33), channel_id=1, source_target_pairs={{0,1},{1,2},{2,3},{3,0},{4,5},{5,6},{6,7},{7,4},{8,9},{9,10},{10,1... | collective-permute-start | bytes 1327112 | tf_op jit(solution)/shard_map/second_hidden_in/ppermute | solution.py:242
  71.4 16.2 %collective-permute-start.5 = (bf16[192,1152]{1,0:T(8,128)(2,1)S(1)}, bf16[192,1152]{1,0:T(8,128)(2,1)S(1)}, u32[]{:S(2)}, u32[]{:S(2)}) collective-permute-start(bf16[192,1152]{1,0:T(8,128)(2,1)S(1)} %bitcast.34), channel_id=1, source_target_pairs={{0,3},{1,0},{2,1},{3,2},{4,7},{5,4},{6,5},{7,6},{8,11},{9,8},{10,9... | collective-permute-start | bytes 1327112 | tf_op jit(solution)/shard_map/second_hidden_in/ppermute | solution.py:242
  74.9 18.5 %collective-permute-start = (bf16[192,1152]{1,0:T(8,128)(2,1)S(1)}, bf16[192,1152]{1,0:T(8,128)(2,1)S(1)}, u32[]{:S(2)}, u32[]{:S(2)}) collective-permute-start(bf16[192,1152]{1,0:T(8,128)(2,1)S(1)} %second_hidden_in.4.own_hbm), channel_id=1, source_target_pairs={{0,1},{1,2},{2,3},{3,0},{4,5},{5,6},{6,7},{7,4},{8,9},{9,10},{10,1... | collective-permute-start | bytes 1327112 | tf_op jit(solution)/shard_map/first_hidden/ppermute | solution.py:242
  78.5 18.6 %collective-permute-start.1 = (bf16[192,1152]{1,0:T(8,128)(2,1)S(1)}, bf16[192,1152]{1,0:T(8,128)(2,1)S(1)}, u32[]{:S(2)}, u32[]{:S(2)}) collective-permute-start(bf16[192,1152]{1,0:T(8,128)(2,1)S(1)} %second_hidden_in.4.own_hbm), channel_id=1, source_target_pairs={{0,3},{1,0},{2,1},{3,2},{4,7},{5,4},{6,5},{7,6},{8,11},{9,8},{10,9... | collective-permute-start | bytes 1327112 | tf_op jit(solution)/shard_map/first_hidden/ppermute | solution.py:242
  83.9 15.6 %collective-permute-start.6 = (bf16[96,1152]{1,0:T(8,128)(2,1)S(1)}, bf16[96,1152]{1,0:T(8,128)(2,1)S(1)}, u32[]{:S(2)}, u32[]{:S(2)}) collective-permute-start(bf16[96,1152]{1,0:T(8,128)(2,1)S(1)} %slice.27), channel_id=1, source_target_pairs={{0,1},{1,2},{2,3},{3,0},{4,5},{5,6},{6,7},{7,4},{8,9},{9,10},{10,1... | collective-permute-start | bytes 663560 | tf_op jit(solution)/shard_map/second_hidden_in/ppermute | solution.py:242
  87.6 13.1 %collective-permute-start.7 = (bf16[96,1152]{1,0:T(8,128)(2,1)S(1)}, bf16[96,1152]{1,0:T(8,128)(2,1)S(1)}, u32[]{:S(2)}, u32[]{:S(2)}) collective-permute-start(bf16[96,1152]{1,0:T(8,128)(2,1)S(1)} %slice.28), channel_id=1, source_target_pairs={{0,3},{1,0},{2,1},{3,2},{4,7},{5,4},{6,5},{7,6},{8,11},{9,8},{10,9... | collective-permute-start | bytes 663560 | tf_op jit(solution)/shard_map/second_hidden_in/ppermute | solution.py:242
  93.4 10.1 %collective-permute-start.2 = (bf16[96,1152]{1,0:T(8,128)(2,1)S(1)}, bf16[96,1152]{1,0:T(8,128)(2,1)S(1)}, u32[]{:S(2)}, u32[]{:S(2)}) collective-permute-start(bf16[96,1152]{1,0:T(8,128)(2,1)S(1)} %slice.24), channel_id=1, source_target_pairs={{0,1},{1,2},{2,3},{3,0},{4,5},{5,6},{6,7},{7,4},{8,9},{9,10},{10,1... | collective-permute-start | bytes 663560 | tf_op jit(solution)/shard_map/first_hidden/ppermute | solution.py:242
  97.1 9.0 %collective-permute-start.3 = (bf16[96,1152]{1,0:T(8,128)(2,1)S(1)}, bf16[96,1152]{1,0:T(8,128)(2,1)S(1)}, u32[]{:S(2)}, u32[]{:S(2)}) collective-permute-start(bf16[96,1152]{1,0:T(8,128)(2,1)S(1)} %slice.25), channel_id=1, source_target_pairs={{0,3},{1,0},{2,1},{3,2},{4,7},{5,4},{6,5},{7,6},{8,11},{9,8},{10,9... | collective-permute-start | bytes 663560 | tf_op jit(solution)/shard_map/first_hidden/ppermute | solution.py:242
  102.3 1.2 copy-start
  118.6 8.2 %copy-start.5 = (s32[128,6]{0,1:T(8,128)S(1)}, s32[128,6]{0,1:T(8,128)}, u32[]{:S(2)}) copy-start(s32[128,6]{0,1:T(8,128)} %param.16) | copy-start | bytes 9220
  118.6 8.2 %copy-start.6 = (f32[128,6]{0,1:T(8,128)S(1)}, f32[128,6]{0,1:T(8,128)}, u32[]{:S(2)}) copy-start(f32[128,6]{0,1:T(8,128)} %param.17) | copy-start | bytes 9220
  118.6 50.9 %all-to-all-start.3 = ((bf16[128,8,768]{2,1,0:T(8,128)(2,1)}), bf16[128,8,768]{2,1,0:T(8,128)(2,1)S(1)}, u32[]{:S(2)}, u32[]{:S(2)}) async-start(bf16[128,8,768]{2,1,0:T(8,128)(2,1)} %bitcast.22), calls=%async_computation.3 | async-start | bytes 3145728 | tf_op jit(solution)/shard_map/finish/all_to_all | solution.py:238

commit v8 on v7

--- a/solution.py
+++ b/solution.py
@@ -139,7 +139,7 @@
 
 
 def finish(
-    payload_ref, near_ref, far_ref, low_ref, high_ref, own_hbm, moments_hbm, master_hbm, second_hbm, out_hbm,
+    payload_ref, near_ref, far_ref, across_ref, own_hbm, moments_hbm, master_hbm, second_hbm, out_hbm,
     own, moments, master, second, weight, gradients, rows, extra, out, sems,
 ):
     me = lax.axis_index("tensor")
@@ -162,7 +162,7 @@
     rows[0:MAIN, :] = payload_ref[:, 0:COLS]
     rows[MAIN:ROWS, :] = last_rows(payload_ref, extra)
     at = 0
-    for ref in (near_ref, far_ref, low_ref, high_ref, own):
+    for ref in (near_ref, far_ref, across_ref, own):
         if ref is own:
             mine.wait()
         to = at + ref.shape[0]
@@ -242,10 +242,12 @@
     return lax.ppermute(x, "tensor", [(i, (i + shift) % 4) for i in range(4)])
 
 
-def gather(x):
+def gather(x, halves):
     half = x.shape[0] // 2
     near, far = before(x, 1), before(x, 3)
-    return [near, far, before(near[:half], 1), before(far[half:], 3)]
+    if halves:
+        return [near, far, before(near[:half], 1), before(far[half:], 3)]
+    return [near, far, before(near, 1)]
 
 
 def shards(
@@ -302,7 +304,7 @@
         kept, rows, part, moments = lax.optimization_barrier((kept, rows, part, moments))
         mine = exchange(kept).reshape(EXP * 14, 128)[:PROWS]
         mine = mine.reshape(24, 9, 8, 128).transpose(0, 2, 1, 3).reshape(HPART, ROWS)
-        second = [*gather(mine), mine]
+        second = [*gather(mine, True), mine]
         second = pl.pallas_call(
             prepare_second, out_shape=shape(ROWS, HID), compiler_params=params(), cost_estimate=pl.CostEstimate(flops=3*1000*1000000, bytes_accessed=0, transcendentals=0)
         )(*second)
@@ -311,7 +313,7 @@
         arrived = exchange(rows.reshape(EXP, 8, WIDE)).reshape(MAIN, WIDE)
 
     with jax.named_scope("first_hidden"):
-        first = gather(part)
+        first = gather(part, False)
 
     with jax.named_scope("mixing"):
         mix, mix_last = pl.pallas_call(
@@ -323,7 +325,7 @@
     with jax.named_scope("finish"):
         produced = pl.pallas_call(
             finish,
-            in_specs=[vmem] * 5 + [hbm] * 4,
+            in_specs=[vmem] * 4 + [hbm] * 4,
             out_specs=hbm,
             out_shape=shape(MAIN, WIDE),
             scratch_shapes=[

time: 172 us -> 174 us (1.012)
  the two profiles are of different devices: /device:TPU:14 before, /device:TPU:8 now
where the time goes in v8:
time: 174 us; the launch traced here: 173 us
  waiting for transfers between devices  72.9 us (42%)
  starting transfers between devices  55.8 us (32%)
  blocking collectives  24.4 us (14%)
  Pallas kernels  14.3 us (8%)
  local copies, waits for them, and re-layouts  3.19 us (2%)
  other arithmetic  2.25 us (1%)
    all_to_all x3, waiting for transfers between devices, exchange(): return lax.all_to_all(x, 'expert', split_axis=0, concat_axis=0, tiled=True)  58.9 us
    all_to_all x3, starting transfers between devices, exchange(): return lax.all_to_all(x, 'expert', split_axis=0, concat_axis=0, tiled=True)  33.6 us
    all_to_all x1, blocking collectives, exchange(): return lax.all_to_all(x, 'expert', split_axis=0, concat_axis=0, tiled=True)  24.4 us
    ppermute x7, starting transfers between devices, before(): return lax.ppermute(x, 'tensor', [(i, (i + shift) % 4) for i in range(4)])  22.2 us
    ppermute x7, waiting for transfers between devices, before(): return lax.ppermute(x, 'tensor', [(i, (i + shift) % 4) for i in range(4)])  14.1 us
    pallas_call x1, Pallas kernels, shards(): pl.pallas_call(finish, in_specs=[vmem] * 4 + [hbm] * 4, out_specs=hbm, ou...  6.81 us
  transfers between devices with their start and end apart: 10, of which 8 were waited for; matrix products, arithmetic and copies ran while one was open for 1% of the time, Pallas kernels for 3%

profile of v8, /device:TPU:8, one launch (start us, length us, event | category | flops | bytes accessed | tf_op | source)
XLA Modules:
  0.0 173.2 jit_solution(76750954902620917)
XLA Ops:
  0.0 1.9 %pad.4 = bf16[1792,128]{1,0:T(8,128)(2,1)} pad(bf16[1728,128]{1,0:T(8,128)(2,1)} %bitcast.44, bf16[]{:T(256)} %constant.5.clone.1), padding=0_64x0_0 | pad | bytes 901122 | tf_op jit(solution)/shard_map/second_hidden_out/jit(_pad)/pad | solution.py:283
  1.9 17.5 %all-to-all-start = ((bf16[128,7,2,128]{3,2,1,0:T(2,128)(2,1)}), bf16[128,7,2,128]{3,2,1,0:T(2,128)(2,1)S(1)}, u32[]{:S(2)}, u32[]{:S(2)}) async-start(bf16[128,7,2,128]{3,2,1,0:T(2,128)(2,1)} %bitcast.8), calls=%async_computation | async-start | bytes 917504 | tf_op jit(solution)/shard_map/second_hidden_out/all_to_all | solution.py:238
  19.4 0.5 second_hidden_in.4.own_hbm
  20.0 2.5 %dispatch.1 = bf16[1024,768]{1,0:T(8,128)(2,1)} custom-call(s32[6,128]{1,0:T(8,128)S(1)} %bitcast.36, f32[6,128]{1,0:T(8,128)S(1)} %bitcast.37, s32[1,128]{1,0:T(1,128)S(1)} %bitcast.40, bf16[128,640]{1,0:T(8,128)(2,1)S(1)} %copy-done.2), custom_call_target="tpu_custom_call" | custom-call | tf_op jit(solution)/shard_map/dispatch/pallas_call | solution.py:287
  22.5 0.1 select_reduce_fusion.1
  22.6 0.2 select_reduce_fusion.3
  22.8 0.2 select_reduce_fusion
  23.0 0.2 select_reduce_fusion.2
  23.2 1.5 pad_maximum_fusion.moments_hbm
  24.8 13.5 %all-to-all-done.in_ref = bf16[128,7,2,128]{3,2,1,0:T(2,128)(2,1)S(1)} async-done(((bf16[128,7,2,128]{3,2,1,0:T(2,128)(2,1)}), bf16[128,7,2,128]{3,2,1,0:T(2,128)(2,1)S(1)}, u32[]{:S(2)}, u32[]{:S(2)}) %all-to-all-start) | async-done | bytes 458784 | tf_op jit(solution)/shard_map/second_hidden_out/all_to_all | solution.py:238
  38.3 0.6 second_hidden_in.3
  38.9 24.4 %all_to_all.20 = bf16[128,7,2,128]{3,2,1,0:T(2,128)(2,1)S(1)} all-to-all(bf16[128,7,2,128]{3,2,1,0:T(2,128)(2,1)S(1)} %second_hidden_in.3), channel_id=1, replica_groups=mesh['expert'=128,'tensor'=4] {'expert'}, dimensions={0} | all-to-all | bytes 917504 | tf_op jit(solution)/shard_map/second_hidden_in/all_to_all | solution.py:238
  63.2 5.7 %all-to-all-start.1 = ((bf16[128,8,768]{2,1,0:T(8,128)(2,1)}), bf16[128,8,768]{2,1,0:T(8,128)(2,1)S(1)}, u32[]{:S(2)}, u32[]{:S(2)}) async-start(bf16[128,8,768]{2,1,0:T(8,128)(2,1)} %bitcast.13), calls=%async_computation.1 | async-start | bytes 3145728 | tf_op jit(solution)/shard_map/dispatch/all_to_all | solution.py:238
  69.0 3.4 %collective-permute-start.3 = (bf16[192,1152]{1,0:T(8,128)(2,1)S(1)}, bf16[192,1152]{1,0:T(8,128)(2,1)S(1)}, u32[]{:S(2)}, u32[]{:S(2)}) collective-permute-start(bf16[192,1152]{1,0:T(8,128)(2,1)S(1)} %bitcast.33), channel_id=1, source_target_pairs={{0,1},{1,2},{2,3},{3,0},{4,5},{5,6},{6,7},{7,4},{8,9},{9,10},{10,1... | collective-permute-start | bytes 1327112 | tf_op jit(solution)/shard_map/second_hidden_in/ppermute | solution.py:242
  72.4 3.7 %collective-permute-start.4 = (bf16[192,1152]{1,0:T(8,128)(2,1)S(1)}, bf16[192,1152]{1,0:T(8,128)(2,1)S(1)}, u32[]{:S(2)}, u32[]{:S(2)}) collective-permute-start(bf16[192,1152]{1,0:T(8,128)(2,1)S(1)} %bitcast.34), channel_id=1, source_target_pairs={{0,3},{1,0},{2,1},{3,2},{4,7},{5,4},{6,5},{7,6},{8,11},{9,8},{10,9... | collective-permute-start | bytes 1327112 | tf_op jit(solution)/shard_map/second_hidden_in/ppermute | solution.py:242
  76.1 2.2 %collective-permute-start = (bf16[192,1152]{1,0:T(8,128)(2,1)S(1)}, bf16[192,1152]{1,0:T(8,128)(2,1)S(1)}, u32[]{:S(2)}, u32[]{:S(2)}) collective-permute-start(bf16[192,1152]{1,0:T(8,128)(2,1)S(1)} %second_hidden_in.4.own_hbm), channel_id=1, source_target_pairs={{0,1},{1,2},{2,3},{3,0},{4,5},{5,6},{6,7},{7,4},{8,9},{9,10},{10,1... | collective-permute-start | bytes 1327112 | tf_op jit(solution)/shard_map/first_hidden/ppermute | solution.py:242
  78.3 6.9 %collective-permute-done.3.one_ref = bf16[192,1152]{1,0:T(8,128)(2,1)S(1)} collective-permute-done((bf16[192,1152]{1,0:T(8,128)(2,1)S(1)}, bf16[192,1152]{1,0:T(8,128)(2,1)S(1)}, u32[]{:S(2)}, u32[]{:S(2)}) %collective-permute-start.3) | collective-permute-done | bytes 442400 | tf_op jit(solution)/shard_map/second_hidden_in/ppermute | solution.py:242
  85.2 2.2 %collective-permute-start.5 = (bf16[96,1152]{1,0:T(8,128)(2,1)S(1)}, bf16[96,1152]{1,0:T(8,128)(2,1)S(1)}, u32[]{:S(2)}, u32[]{:S(2)}) collective-permute-start(bf16[96,1152]{1,0:T(8,128)(2,1)S(1)} %slice.17), channel_id=1, source_target_pairs={{0,1},{1,2},{2,3},{3,0},{4,5},{5,6},{6,7},{7,4},{8,9},{9,10},{10,1... | collective-permute-start | bytes 663560 | tf_op jit(solution)/shard_map/second_hidden_in/ppermute | solution.py:242
  87.4 4.9 %collective-permute-start.6 = (bf16[96,1152]{1,0:T(8,128)(2,1)S(1)}, bf16[96,1152]{1,0:T(8,128)(2,1)S(1)}, u32[]{:S(2)}, u32[]{:S(2)}) collective-permute-start(bf16[96,1152]{1,0:T(8,128)(2,1)S(1)} %slice.18), channel_id=1, source_target_pairs={{0,3},{1,0},{2,1},{3,2},{4,7},{5,4},{6,5},{7,6},{8,11},{9,8},{10,9... | collective-permute-start | bytes 663560 | tf_op jit(solution)/shard_map/second_hidden_in/ppermute | solution.py:242
  92.3 2.2 %collective-permute-start.1 = (bf16[192,1152]{1,0:T(8,128)(2,1)S(1)}, bf16[192,1152]{1,0:T(8,128)(2,1)S(1)}, u32[]{:S(2)}, u32[]{:S(2)}) collective-permute-start(bf16[192,1152]{1,0:T(8,128)(2,1)S(1)} %second_hidden_in.4.own_hbm), channel_id=1, source_target_pairs={{0,3},{1,0},{2,1},{3,2},{4,7},{5,4},{6,5},{7,6},{8,11},{9,8},{10,9... | collective-permute-start | bytes 1327112 | tf_op jit(solution)/shard_map/first_hidden/ppermute | solution.py:242
  94.6 3.7 %collective-permute-start.2 = (bf16[192,1152]{1,0:T(8,128)(2,1)S(1)}, bf16[192,1152]{1,0:T(8,128)(2,1)S(1)}, u32[]{:S(2)}, u32[]{:S(2)}) collective-permute-start(bf16[192,1152]{1,0:T(8,128)(2,1)S(1)} %collective-permute-done.near_ref), channel_id=1, source_target_pairs={{0,1},{1,2},{2,3},{3,0},{4,5},{5,6},{6,7},{7,4},{8,9},{9,10},{10,1... | collective-permute-start | bytes 1327112 | tf_op jit(solution)/shard_map/first_hidden/ppermute | solution.py:242
  98.3 0.3 collective-permute-done.5.two_low_ref
  98.6 1.6 second_hidden_in.5.second_hbm
  100.2 1.2 copy-done
  101.4 3.4 %collective-permute-done.1.far_ref = bf16[192,1152]{1,0:T(8,128)(2,1)S(1)} collective-permute-done((bf16[192,1152]{1,0:T(8,128)(2,1)S(1)}, bf16[192,1152]{1,0:T(8,128)(2,1)S(1)}, u32[]{:S(2)}, u32[]{:S(2)}) %collective-permute-start.1) | collective-permute-done | bytes 442400 | tf_op jit(solution)/shard_map/first_hidden/ppermute | solution.py:242
  104.8 3.5 %collective-permute-done.2.across_ref = bf16[192,1152]{1,0:T(8,128)(2,1)S(1)} collective-permute-done((bf16[192,1152]{1,0:T(8,128)(2,1)S(1)}, bf16[192,1152]{1,0:T(8,128)(2,1)S(1)}, u32[]{:S(2)}, u32[]{:S(2)}) %collective-permute-start.2) | collective-permute-done | bytes 442400 | tf_op jit(solution)/shard_map/first_hidden/ppermute | solution.py:242
  108.3 3.4 %all-to-all-done.1 = bf16[128,8,768]{2,1,0:T(8,128)(2,1)S(1)} async-done(((bf16[128,8,768]{2,1,0:T(8,128)(2,1)}), bf16[128,8,768]{2,1,0:T(8,128)(2,1)S(1)}, u32[]{:S(2)}, u32[]{:S(2)}) %all-to-all-start.1) | async-done | bytes 1572896 | tf_op jit(solution)/shard_map/dispatch/all_to_all | solution.py:238
  111.7 6.8 %finish.1 = bf16[1024,768]{1,0:T(8,128)(2,1)} custom-call(bf16[1024,768]{1,0:T(8,128)(2,1)S(1)} %bitcast.31, bf16[192,1152]{1,0:T(8,128)(2,1)S(1)} %collective-permute-done.near_ref, bf16[192,1152]{1,0:T(8,128)(2,1)S(1)} %collective-permute-done.1.far_ref, bf16[192,1152]{1,0:T(8,128)(2,1)S(1)} %collective-permute-done.2.across_ref, ...), custom_call_target="tpu_custom_call" | custom-call | tf_op jit(solution)/shard_map/finish/pallas_call | solution.py:326
  118.5 10.4 %all-to-all-start.3 = ((bf16[128,8,768]{2,1,0:T(8,128)(2,1)}), bf16[128,8,768]{2,1,0:T(8,128)(2,1)S(1)}, u32[]{:S(2)}, u32[]{:S(2)}) async-start(bf16[128,8,768]{2,1,0:T(8,128)(2,1)} %bitcast.22), calls=%async_computation.3 | async-start | bytes 3145728 | tf_op jit(solution)/shard_map/finish/all_to_all | solution.py:238
  128.9 0.7 mixing.1
  129.6 42.0 %all-to-all-done.3 = bf16[128,8,768]{2,1,0:T(8,128)(2,1)S(1)} async-done(((bf16[128,8,768]{2,1,0:T(8,128)(2,1)}), bf16[128,8,768]{2,1,0:T(8,128)(2,1)S(1)}, u32[]{:S(2)}, u32[]{:S(2)}) %all-to-all-start.3) | async-done | bytes 1572896 | tf_op jit(solution)/shard_map/finish/all_to_all | solution.py:238
  171.6 1.6 combine.1
  (30 shorter events, 0.3 us)
Async XLA Ops:
  0.0 19.4 %copy-start.1 = (bf16[1,1152,192]{1,2,0:T(8,128)(2,1)S(1)}, bf16[1,1152,192]{1,2,0:T(8,128)(2,1)}, u32[]{:S(2)}) copy-start(bf16[1,1152,192]{1,2,0:T(8,128)(2,1)} %param.15) | copy-start | bytes 1327108
  0.0 19.9 %copy-start.7 = (s32[128]{0:T(128)S(1)}, s32[128]{0:T(128)}, u32[]{:S(2)}) copy-start(s32[128]{0:T(128)} %param.22) | copy-start | bytes 1540
  0.0 19.9 %copy-start.10 = (s32[128]{0:T(128)S(1)}, s32[128]{0:T(128)}, u32[]{:S(2)}) copy-start(s32[128]{0:T(128)} %param.23) | copy-start | bytes 1540
  0.0 20.0 %copy-start.4 = (f32[128,6]{0,1:T(8,128)S(1)}, f32[128,6]{0,1:T(8,128)}, u32[]{:S(2)}) copy-start(f32[128,6]{0,1:T(8,128)} %param.14) | copy-start | bytes 9220
  0.0 20.0 %copy-start.3 = (s32[128,6]{0,1:T(8,128)S(1)}, s32[128,6]{0,1:T(8,128)}, u32[]{:S(2)}) copy-start(s32[128,6]{0,1:T(8,128)} %param.13) | copy-start | bytes 9220
  0.0 20.0 %copy-start.2 = (bf16[128,640]{1,0:T(8,128)(2,1)S(1)}, bf16[128,640]{1,0:T(8,128)(2,1)}, u32[]{:S(2)}) copy-start(bf16[128,640]{1,0:T(8,128)(2,1)} %tokens_ref.1) | copy-start | bytes 491524
  1.9 21.3 %copy-start.8 = (bf16[1,768,640]{2,1,0:T(8,128)(2,1)S(1)}, bf16[1,768,640]{2,1,0:T(8,128)(2,1)}, u32[]{:S(2)}) copy-start(bf16[1,768,640]{2,1,0:T(8,128)(2,1)} %param.21) | copy-start | bytes 2949124
  1.9 21.3 %copy-start.9 = (bf16[1,768,640]{2,1,0:T(8,128)(2,1)S(1)}, bf16[1,768,640]{2,1,0:T(8,128)(2,1)}, u32[]{:S(2)}) copy-start(bf16[1,768,640]{2,1,0:T(8,128)(2,1)} %param.20) | copy-start | bytes 2949124
  1.9 36.4 %all-to-all-start = ((bf16[128,7,2,128]{3,2,1,0:T(2,128)(2,1)}), bf16[128,7,2,128]{3,2,1,0:T(2,128)(2,1)S(1)}, u32[]{:S(2)}, u32[]{:S(2)}) async-start(bf16[128,7,2,128]{3,2,1,0:T(2,128)(2,1)} %bitcast.8), calls=%async_computation | async-start | bytes 917504 | tf_op jit(solution)/shard_map/second_hidden_out/all_to_all | solution.py:238
  63.2 48.4 %all-to-all-start.1 = ((bf16[128,8,768]{2,1,0:T(8,128)(2,1)}), bf16[128,8,768]{2,1,0:T(8,128)(2,1)S(1)}, u32[]{:S(2)}, u32[]{:S(2)}) async-start(bf16[128,8,768]{2,1,0:T(8,128)(2,1)} %bitcast.13), calls=%async_computation.1 | async-start | bytes 3145728 | tf_op jit(solution)/shard_map/dispatch/all_to_all | solution.py:238
  69.0 16.1 %collective-permute-start.3 = (bf16[192,1152]{1,0:T(8,128)(2,1)S(1)}, bf16[192,1152]{1,0:T(8,128)(2,1)S(1)}, u32[]{:S(2)}, u32[]{:S(2)}) collective-permute-start(bf16[192,1152]{1,0:T(8,128)(2,1)S(1)} %bitcast.33), channel_id=1, source_target_pairs={{0,1},{1,2},{2,3},{3,0},{4,5},{5,6},{6,7},{7,4},{8,9},{9,10},{10,1... | collective-permute-start | bytes 1327112 | tf_op jit(solution)/shard_map/second_hidden_in/ppermute | solution.py:242
  72.4 14.9 %collective-permute-start.4 = (bf16[192,1152]{1,0:T(8,128)(2,1)S(1)}, bf16[192,1152]{1,0:T(8,128)(2,1)S(1)}, u32[]{:S(2)}, u32[]{:S(2)}) collective-permute-start(bf16[192,1152]{1,0:T(8,128)(2,1)S(1)} %bitcast.34), channel_id=1, source_target_pairs={{0,3},{1,0},{2,1},{3,2},{4,7},{5,4},{6,5},{7,6},{8,11},{9,8},{10,9... | collective-permute-start | bytes 1327112 | tf_op jit(solution)/shard_map/second_hidden_in/ppermute | solution.py:242
  76.1 18.5 %collective-permute-start = (bf16[192,1152]{1,0:T(8,128)(2,1)S(1)}, bf16[192,1152]{1,0:T(8,128)(2,1)S(1)}, u32[]{:S(2)}, u32[]{:S(2)}) collective-permute-start(bf16[192,1152]{1,0:T(8,128)(2,1)S(1)} %second_hidden_in.4.own_hbm), channel_id=1, source_target_pairs={{0,1},{1,2},{2,3},{3,0},{4,5},{5,6},{6,7},{7,4},{8,9},{9,10},{10,1... | collective-permute-start | bytes 1327112 | tf_op jit(solution)/shard_map/first_hidden/ppermute | solution.py:242
  85.2 13.4 %collective-permute-start.5 = (bf16[96,1152]{1,0:T(8,128)(2,1)S(1)}, bf16[96,1152]{1,0:T(8,128)(2,1)S(1)}, u32[]{:S(2)}, u32[]{:S(2)}) collective-permute-start(bf16[96,1152]{1,0:T(8,128)(2,1)S(1)} %slice.17), channel_id=1, source_target_pairs={{0,1},{1,2},{2,3},{3,0},{4,5},{5,6},{6,7},{7,4},{8,9},{9,10},{10,1... | collective-permute-start | bytes 663560 | tf_op jit(solution)/shard_map/second_hidden_in/ppermute | solution.py:242
  87.4 11.2 %collective-permute-start.6 = (bf16[96,1152]{1,0:T(8,128)(2,1)S(1)}, bf16[96,1152]{1,0:T(8,128)(2,1)S(1)}, u32[]{:S(2)}, u32[]{:S(2)}) collective-permute-start(bf16[96,1152]{1,0:T(8,128)(2,1)S(1)} %slice.18), channel_id=1, source_target_pairs={{0,3},{1,0},{2,1},{3,2},{4,7},{5,4},{6,5},{7,6},{8,11},{9,8},{10,9... | collective-permute-start | bytes 663560 | tf_op jit(solution)/shard_map/second_hidden_in/ppermute | solution.py:242
  92.3 12.6 %collective-permute-start.1 = (bf16[192,1152]{1,0:T(8,128)(2,1)S(1)}, bf16[192,1152]{1,0:T(8,128)(2,1)S(1)}, u32[]{:S(2)}, u32[]{:S(2)}) collective-permute-start(bf16[192,1152]{1,0:T(8,128)(2,1)S(1)} %second_hidden_in.4.own_hbm), channel_id=1, source_target_pairs={{0,3},{1,0},{2,1},{3,2},{4,7},{5,4},{6,5},{7,6},{8,11},{9,8},{10,9... | collective-permute-start | bytes 1327112 | tf_op jit(solution)/shard_map/first_hidden/ppermute | solution.py:242
  94.6 13.7 %collective-permute-start.2 = (bf16[192,1152]{1,0:T(8,128)(2,1)S(1)}, bf16[192,1152]{1,0:T(8,128)(2,1)S(1)}, u32[]{:S(2)}, u32[]{:S(2)}) collective-permute-start(bf16[192,1152]{1,0:T(8,128)(2,1)S(1)} %collective-permute-done.near_ref), channel_id=1, source_target_pairs={{0,1},{1,2},{2,3},{3,0},{4,5},{5,6},{6,7},{7,4},{8,9},{9,10},{10,1... | collective-permute-start | bytes 1327112 | tf_op jit(solution)/shard_map/first_hidden/ppermute | solution.py:242
  100.2 1.2 copy-start
  118.5 10.4 %copy-start.5 = (s32[128,6]{0,1:T(8,128)S(1)}, s32[128,6]{0,1:T(8,128)}, u32[]{:S(2)}) copy-start(s32[128,6]{0,1:T(8,128)} %param.16) | copy-start | bytes 9220
  118.5 10.4 %copy-start.6 = (f32[128,6]{0,1:T(8,128)S(1)}, f32[128,6]{0,1:T(8,128)}, u32[]{:S(2)}) copy-start(f32[128,6]{0,1:T(8,128)} %param.17) | copy-start | bytes 9220
  118.5 53.1 %all-to-all-start.3 = ((bf16[128,8,768]{2,1,0:T(8,128)(2,1)}), bf16[128,8,768]{2,1,0:T(8,128)(2,1)S(1)}, u32[]{:S(2)}, u32[]{:S(2)}) async-start(bf16[128,8,768]{2,1,0:T(8,128)(2,1)} %bitcast.22), calls=%async_computation.3 | async-start | bytes 3145728 | tf_op jit(solution)/shard_map/finish/all_to_all | solution.py:238

commit v9 on v7

--- a/solution.py
+++ b/solution.py
@@ -145,6 +145,8 @@
     me = lax.axis_index("tensor")
     mine = pltpu.make_async_copy(own_hbm, own, sems.at[8])
     mine.start()
+    rest = pltpu.make_async_copy(second_hbm, second, sems.at[9])
+    rest.start()
     copies = []
     for n, behind in enumerate((1, 3, 2, 0)):
         place = pl.ds(pl.multiple_of(lax.rem(me + 4 - behind, 4) * HPART, HPART), HPART)
@@ -156,8 +158,6 @@
         copies.append(pair)
         for copy in pair:
             copy.start()
-    rest = pltpu.make_async_copy(second_hbm, second, sems.at[9])
-    rest.start()
 
     rows[0:MAIN, :] = payload_ref[:, 0:COLS]
     rows[MAIN:ROWS, :] = last_rows(payload_ref, extra)

time: 172 us -> 172 us (level)
  no operation moved by 1% of the time
where the time goes in v9:
time: 172 us; the launch traced here: 171 us
  waiting for transfers between devices  71.6 us (42%)
  starting transfers between devices  55 us (32%)
  blocking collectives  24.4 us (14%)
  Pallas kernels  14.2 us (8%)
  local copies, waits for them, and re-layouts  3.22 us (2%)
  other arithmetic  2.26 us (1%)
    all_to_all x3, waiting for transfers between devices, exchange(): return lax.all_to_all(x, 'expert', split_axis=0, concat_axis=0, tiled=True)  61 us
    all_to_all x3, starting transfers between devices, exchange(): return lax.all_to_all(x, 'expert', split_axis=0, concat_axis=0, tiled=True)  31.4 us
    all_to_all x1, blocking collectives, exchange(): return lax.all_to_all(x, 'expert', split_axis=0, concat_axis=0, tiled=True)  24.4 us
    ppermute x8, starting transfers between devices, before(): return lax.ppermute(x, 'tensor', [(i, (i + shift) % 4) for i in range(4)])  23.6 us
    ppermute x8, waiting for transfers between devices, before(): return lax.ppermute(x, 'tensor', [(i, (i + shift) % 4) for i in range(4)])  10.5 us
    pallas_call x1, Pallas kernels, shards(): pl.pallas_call(finish, in_specs=[vmem] * 5 + [hbm] * 4, out_specs=hbm, ou...  6.7 us
  transfers between devices with their start and end apart: 11, of which 7 were waited for; matrix products, arithmetic and copies ran while one was open for 1% of the time, Pallas kernels for 3%

profile of v9, /device:TPU:14, one launch (start us, length us, event | category | flops | bytes accessed | tf_op | source)
XLA Modules:
  0.0 170.9 jit_solution(9072375427468322765)
XLA Ops:
  0.0 1.9 %pad.4 = bf16[1792,128]{1,0:T(8,128)(2,1)} pad(bf16[1728,128]{1,0:T(8,128)(2,1)} %bitcast.44, bf16[]{:T(256)} %constant.5.clone.1), padding=0_64x0_0 | pad | bytes 901122 | tf_op jit(solution)/shard_map/second_hidden_out/jit(_pad)/pad | solution.py:281
  1.9 17.5 %all-to-all-start = ((bf16[128,7,2,128]{3,2,1,0:T(2,128)(2,1)}), bf16[128,7,2,128]{3,2,1,0:T(2,128)(2,1)S(1)}, u32[]{:S(2)}, u32[]{:S(2)}) async-start(bf16[128,7,2,128]{3,2,1,0:T(2,128)(2,1)} %bitcast.8), calls=%async_computation | async-start | bytes 917504 | tf_op jit(solution)/shard_map/second_hidden_out/all_to_all | solution.py:238
  19.4 0.5 second_hidden_in.4.own_hbm
  20.0 2.5 %dispatch.1 = bf16[1024,768]{1,0:T(8,128)(2,1)} custom-call(s32[6,128]{1,0:T(8,128)S(1)} %bitcast.36, f32[6,128]{1,0:T(8,128)S(1)} %bitcast.37, s32[1,128]{1,0:T(1,128)S(1)} %bitcast.40, bf16[128,640]{1,0:T(8,128)(2,1)S(1)} %copy-done.2), custom_call_target="tpu_custom_call" | custom-call | tf_op jit(solution)/shard_map/dispatch/pallas_call | solution.py:285
  22.6 0.2 select_reduce_fusion.3
  22.8 0.2 select_reduce_fusion
  23.0 0.2 select_reduce_fusion.2
  23.2 1.5 pad_maximum_fusion.moments_hbm
  24.8 13.5 %all-to-all-done.in_ref = bf16[128,7,2,128]{3,2,1,0:T(2,128)(2,1)S(1)} async-done(((bf16[128,7,2,128]{3,2,1,0:T(2,128)(2,1)}), bf16[128,7,2,128]{3,2,1,0:T(2,128)(2,1)S(1)}, u32[]{:S(2)}, u32[]{:S(2)}) %all-to-all-start) | async-done | bytes 458784 | tf_op jit(solution)/shard_map/second_hidden_out/all_to_all | solution.py:238
  38.3 0.6 second_hidden_in.3
  38.9 24.4 %all_to_all.20 = bf16[128,7,2,128]{3,2,1,0:T(2,128)(2,1)S(1)} all-to-all(bf16[128,7,2,128]{3,2,1,0:T(2,128)(2,1)S(1)} %second_hidden_in.3), channel_id=1, replica_groups=mesh['expert'=128,'tensor'=4] {'expert'}, dimensions={0} | all-to-all | bytes 917504 | tf_op jit(solution)/shard_map/second_hidden_in/all_to_all | solution.py:238
  63.2 5.7 %all-to-all-start.1 = ((bf16[128,8,768]{2,1,0:T(8,128)(2,1)}), bf16[128,8,768]{2,1,0:T(8,128)(2,1)S(1)}, u32[]{:S(2)}, u32[]{:S(2)}) async-start(bf16[128,8,768]{2,1,0:T(8,128)(2,1)} %bitcast.13), calls=%async_computation.1 | async-start | bytes 3145728 | tf_op jit(solution)/shard_map/dispatch/all_to_all | solution.py:238
  69.0 2.4 %collective-permute-start.4 = (bf16[192,1152]{1,0:T(8,128)(2,1)S(1)}, bf16[192,1152]{1,0:T(8,128)(2,1)S(1)}, u32[]{:S(2)}, u32[]{:S(2)}) collective-permute-start(bf16[192,1152]{1,0:T(8,128)(2,1)S(1)} %bitcast.33), channel_id=1, source_target_pairs={{0,1},{1,2},{2,3},{3,0},{4,5},{5,6},{6,7},{7,4},{8,9},{9,10},{10,1... | collective-permute-start | bytes 1327112 | tf_op jit(solution)/shard_map/second_hidden_in/ppermute | solution.py:242
  71.4 3.5 %collective-permute-start.5 = (bf16[192,1152]{1,0:T(8,128)(2,1)S(1)}, bf16[192,1152]{1,0:T(8,128)(2,1)S(1)}, u32[]{:S(2)}, u32[]{:S(2)}) collective-permute-start(bf16[192,1152]{1,0:T(8,128)(2,1)S(1)} %bitcast.34), channel_id=1, source_target_pairs={{0,3},{1,0},{2,1},{3,2},{4,7},{5,4},{6,5},{7,6},{8,11},{9,8},{10,9... | collective-permute-start | bytes 1327112 | tf_op jit(solution)/shard_map/second_hidden_in/ppermute | solution.py:242
  74.9 3.6 %collective-permute-start = (bf16[192,1152]{1,0:T(8,128)(2,1)S(1)}, bf16[192,1152]{1,0:T(8,128)(2,1)S(1)}, u32[]{:S(2)}, u32[]{:S(2)}) collective-permute-start(bf16[192,1152]{1,0:T(8,128)(2,1)S(1)} %second_hidden_in.4.own_hbm), channel_id=1, source_target_pairs={{0,1},{1,2},{2,3},{3,0},{4,5},{5,6},{6,7},{7,4},{8,9},{9,10},{10,1... | collective-permute-start | bytes 1327112 | tf_op jit(solution)/shard_map/first_hidden/ppermute | solution.py:242
  78.5 2.2 %collective-permute-start.1 = (bf16[192,1152]{1,0:T(8,128)(2,1)S(1)}, bf16[192,1152]{1,0:T(8,128)(2,1)S(1)}, u32[]{:S(2)}, u32[]{:S(2)}) collective-permute-start(bf16[192,1152]{1,0:T(8,128)(2,1)S(1)} %second_hidden_in.4.own_hbm), channel_id=1, source_target_pairs={{0,3},{1,0},{2,1},{3,2},{4,7},{5,4},{6,5},{7,6},{8,11},{9,8},{10,9... | collective-permute-start | bytes 1327112 | tf_op jit(solution)/shard_map/first_hidden/ppermute | solution.py:242
  80.7 3.2 %collective-permute-done.4.one_ref = bf16[192,1152]{1,0:T(8,128)(2,1)S(1)} collective-permute-done((bf16[192,1152]{1,0:T(8,128)(2,1)S(1)}, bf16[192,1152]{1,0:T(8,128)(2,1)S(1)}, u32[]{:S(2)}, u32[]{:S(2)}) %collective-permute-start.4) | collective-permute-done | bytes 442400 | tf_op jit(solution)/shard_map/second_hidden_in/ppermute | solution.py:242
  83.9 3.6 %collective-permute-start.6 = (bf16[96,1152]{1,0:T(8,128)(2,1)S(1)}, bf16[96,1152]{1,0:T(8,128)(2,1)S(1)}, u32[]{:S(2)}, u32[]{:S(2)}) collective-permute-start(bf16[96,1152]{1,0:T(8,128)(2,1)S(1)} %slice.27), channel_id=1, source_target_pairs={{0,1},{1,2},{2,3},{3,0},{4,5},{5,6},{6,7},{7,4},{8,9},{9,10},{10,1... | collective-permute-start | bytes 663560 | tf_op jit(solution)/shard_map/second_hidden_in/ppermute | solution.py:242
  87.6 2.2 %collective-permute-start.7 = (bf16[96,1152]{1,0:T(8,128)(2,1)S(1)}, bf16[96,1152]{1,0:T(8,128)(2,1)S(1)}, u32[]{:S(2)}, u32[]{:S(2)}) collective-permute-start(bf16[96,1152]{1,0:T(8,128)(2,1)S(1)} %slice.28), channel_id=1, source_target_pairs={{0,3},{1,0},{2,1},{3,2},{4,7},{5,4},{6,5},{7,6},{8,11},{9,8},{10,9... | collective-permute-start | bytes 663560 | tf_op jit(solution)/shard_map/second_hidden_in/ppermute | solution.py:242
  89.8 3.6 %collective-permute-done.near_ref = bf16[192,1152]{1,0:T(8,128)(2,1)S(1)} collective-permute-done((bf16[192,1152]{1,0:T(8,128)(2,1)S(1)}, bf16[192,1152]{1,0:T(8,128)(2,1)S(1)}, u32[]{:S(2)}, u32[]{:S(2)}) %collective-permute-start) | collective-permute-done | bytes 442400 | tf_op jit(solution)/shard_map/first_hidden/ppermute | solution.py:242
  93.4 3.6 %collective-permute-start.2 = (bf16[96,1152]{1,0:T(8,128)(2,1)S(1)}, bf16[96,1152]{1,0:T(8,128)(2,1)S(1)}, u32[]{:S(2)}, u32[]{:S(2)}) collective-permute-start(bf16[96,1152]{1,0:T(8,128)(2,1)S(1)} %slice.24), channel_id=1, source_target_pairs={{0,1},{1,2},{2,3},{3,0},{4,5},{5,6},{6,7},{7,4},{8,9},{9,10},{10,1... | collective-permute-start | bytes 663560 | tf_op jit(solution)/shard_map/first_hidden/ppermute | solution.py:242
  97.1 2.4 %collective-permute-start.3 = (bf16[96,1152]{1,0:T(8,128)(2,1)S(1)}, bf16[96,1152]{1,0:T(8,128)(2,1)S(1)}, u32[]{:S(2)}, u32[]{:S(2)}) collective-permute-start(bf16[96,1152]{1,0:T(8,128)(2,1)S(1)} %slice.25), channel_id=1, source_target_pairs={{0,3},{1,0},{2,1},{3,2},{4,7},{5,4},{6,5},{7,6},{8,11},{9,8},{10,9... | collective-permute-start | bytes 663560 | tf_op jit(solution)/shard_map/first_hidden/ppermute | solution.py:242
  99.5 1.2 collective-permute-done.7.two_high_ref
  100.7 1.7 second_hidden_in.5.second_hbm
  102.3 1.2 copy-done
  103.5 2.6 %collective-permute-done.3.high_ref = bf16[96,1152]{1,0:T(8,128)(2,1)S(1)} collective-permute-done((bf16[96,1152]{1,0:T(8,128)(2,1)S(1)}, bf16[96,1152]{1,0:T(8,128)(2,1)S(1)}, u32[]{:S(2)}, u32[]{:S(2)}) %collective-permute-start.3) | collective-permute-done | bytes 221216 | tf_op jit(solution)/shard_map/first_hidden/ppermute | solution.py:242
  106.1 5.6 %all-to-all-done.1 = bf16[128,8,768]{2,1,0:T(8,128)(2,1)S(1)} async-done(((bf16[128,8,768]{2,1,0:T(8,128)(2,1)}), bf16[128,8,768]{2,1,0:T(8,128)(2,1)S(1)}, u32[]{:S(2)}, u32[]{:S(2)}) %all-to-all-start.1) | async-done | bytes 1572896 | tf_op jit(solution)/shard_map/dispatch/all_to_all | solution.py:238
  111.7 6.7 %finish.1 = bf16[1024,768]{1,0:T(8,128)(2,1)} custom-call(bf16[1024,768]{1,0:T(8,128)(2,1)S(1)} %bitcast.31, bf16[192,1152]{1,0:T(8,128)(2,1)S(1)} %collective-permute-done.near_ref, bf16[192,1152]{1,0:T(8,128)(2,1)S(1)} %collective-permute-done.1.far_ref, bf16[96,1152]{1,0:T(8,128)(2,1)S(1)} %collective-permute-done.2.low_ref, ...), custom_call_target="tpu_custom_call" | custom-call | tf_op jit(solution)/shard_map/finish/pallas_call | solution.py:324
  118.4 8.2 %all-to-all-start.3 = ((bf16[128,8,768]{2,1,0:T(8,128)(2,1)}), bf16[128,8,768]{2,1,0:T(8,128)(2,1)S(1)}, u32[]{:S(2)}, u32[]{:S(2)}) async-start(bf16[128,8,768]{2,1,0:T(8,128)(2,1)} %bitcast.22), calls=%async_computation.3 | async-start | bytes 3145728 | tf_op jit(solution)/shard_map/finish/all_to_all | solution.py:238
  126.6 0.7 mixing.1
  127.3 42.0 %all-to-all-done.3 = bf16[128,8,768]{2,1,0:T(8,128)(2,1)S(1)} async-done(((bf16[128,8,768]{2,1,0:T(8,128)(2,1)}), bf16[128,8,768]{2,1,0:T(8,128)(2,1)S(1)}, u32[]{:S(2)}, u32[]{:S(2)}) %all-to-all-start.3) | async-done | bytes 1572896 | tf_op jit(solution)/shard_map/finish/all_to_all | solution.py:238
  169.3 1.6 combine.1
  (34 shorter events, 0.4 us)
Async XLA Ops:
  0.0 19.4 %copy-start.1 = (bf16[1,1152,192]{1,2,0:T(8,128)(2,1)S(1)}, bf16[1,1152,192]{1,2,0:T(8,128)(2,1)}, u32[]{:S(2)}) copy-start(bf16[1,1152,192]{1,2,0:T(8,128)(2,1)} %param.15) | copy-start | bytes 1327108
  0.0 19.9 %copy-start.7 = (s32[128]{0:T(128)S(1)}, s32[128]{0:T(128)}, u32[]{:S(2)}) copy-start(s32[128]{0:T(128)} %param.22) | copy-start | bytes 1540
  0.0 19.9 %copy-start.10 = (s32[128]{0:T(128)S(1)}, s32[128]{0:T(128)}, u32[]{:S(2)}) copy-start(s32[128]{0:T(128)} %param.23) | copy-start | bytes 1540
  0.0 20.0 %copy-start.4 = (f32[128,6]{0,1:T(8,128)S(1)}, f32[128,6]{0,1:T(8,128)}, u32[]{:S(2)}) copy-start(f32[128,6]{0,1:T(8,128)} %param.14) | copy-start | bytes 9220
  0.0 20.0 %copy-start.3 = (s32[128,6]{0,1:T(8,128)S(1)}, s32[128,6]{0,1:T(8,128)}, u32[]{:S(2)}) copy-start(s32[128,6]{0,1:T(8,128)} %param.13) | copy-start | bytes 9220
  0.0 20.0 %copy-start.2 = (bf16[128,640]{1,0:T(8,128)(2,1)S(1)}, bf16[128,640]{1,0:T(8,128)(2,1)}, u32[]{:S(2)}) copy-start(bf16[128,640]{1,0:T(8,128)(2,1)} %tokens_ref.1) | copy-start | bytes 491524
  1.9 21.3 %copy-start.8 = (bf16[1,768,640]{2,1,0:T(8,128)(2,1)S(1)}, bf16[1,768,640]{2,1,0:T(8,128)(2,1)}, u32[]{:S(2)}) copy-start(bf16[1,768,640]{2,1,0:T(8,128)(2,1)} %param.21) | copy-start | bytes 2949124
  1.9 21.3 %copy-start.9 = (bf16[1,768,640]{2,1,0:T(8,128)(2,1)S(1)}, bf16[1,768,640]{2,1,0:T(8,128)(2,1)}, u32[]{:S(2)}) copy-start(bf16[1,768,640]{2,1,0:T(8,128)(2,1)} %param.20) | copy-start | bytes 2949124
  1.9 36.4 %all-to-all-start = ((bf16[128,7,2,128]{3,2,1,0:T(2,128)(2,1)}), bf16[128,7,2,128]{3,2,1,0:T(2,128)(2,1)S(1)}, u32[]{:S(2)}, u32[]{:S(2)}) async-start(bf16[128,7,2,128]{3,2,1,0:T(2,128)(2,1)} %bitcast.8), calls=%async_computation | async-start | bytes 917504 | tf_op jit(solution)/shard_map/second_hidden_out/all_to_all | solution.py:238
  63.2 48.4 %all-to-all-start.1 = ((bf16[128,8,768]{2,1,0:T(8,128)(2,1)}), bf16[128,8,768]{2,1,0:T(8,128)(2,1)S(1)}, u32[]{:S(2)}, u32[]{:S(2)}) async-start(bf16[128,8,768]{2,1,0:T(8,128)(2,1)} %bitcast.13), calls=%async_computation.1 | async-start | bytes 3145728 | tf_op jit(solution)/shard_map/dispatch/all_to_all | solution.py:238
  69.0 14.9 %collective-permute-start.4 = (bf16[192,1152]{1,0:T(8,128)(2,1)S(1)}, bf16[192,1152]{1,0:T(8,128)(2,1)S(1)}, u32[]{:S(2)}, u32[]{:S(2)}) collective-permute-start(bf16[192,1152]{1,0:T(8,128)(2,1)S(1)} %bitcast.33), channel_id=1, source_target_pairs={{0,1},{1,2},{2,3},{3,0},{4,5},{5,6},{6,7},{7,4},{8,9},{9,10},{10,1... | collective-permute-start | bytes 1327112 | tf_op jit(solution)/shard_map/second_hidden_in/ppermute | solution.py:242
  71.4 16.2 %collective-permute-start.5 = (bf16[192,1152]{1,0:T(8,128)(2,1)S(1)}, bf16[192,1152]{1,0:T(8,128)(2,1)S(1)}, u32[]{:S(2)}, u32[]{:S(2)}) collective-permute-start(bf16[192,1152]{1,0:T(8,128)(2,1)S(1)} %bitcast.34), channel_id=1, source_target_pairs={{0,3},{1,0},{2,1},{3,2},{4,7},{5,4},{6,5},{7,6},{8,11},{9,8},{10,9... | collective-permute-start | bytes 1327112 | tf_op jit(solution)/shard_map/second_hidden_in/ppermute | solution.py:242
  74.9 18.5 %collective-permute-start = (bf16[192,1152]{1,0:T(8,128)(2,1)S(1)}, bf16[192,1152]{1,0:T(8,128)(2,1)S(1)}, u32[]{:S(2)}, u32[]{:S(2)}) collective-permute-start(bf16[192,1152]{1,0:T(8,128)(2,1)S(1)} %second_hidden_in.4.own_hbm), channel_id=1, source_target_pairs={{0,1},{1,2},{2,3},{3,0},{4,5},{5,6},{6,7},{7,4},{8,9},{9,10},{10,1... | collective-permute-start | bytes 1327112 | tf_op jit(solution)/shard_map/first_hidden/ppermute | solution.py:242
  78.5 18.6 %collective-permute-start.1 = (bf16[192,1152]{1,0:T(8,128)(2,1)S(1)}, bf16[192,1152]{1,0:T(8,128)(2,1)S(1)}, u32[]{:S(2)}, u32[]{:S(2)}) collective-permute-start(bf16[192,1152]{1,0:T(8,128)(2,1)S(1)} %second_hidden_in.4.own_hbm), channel_id=1, source_target_pairs={{0,3},{1,0},{2,1},{3,2},{4,7},{5,4},{6,5},{7,6},{8,11},{9,8},{10,9... | collective-permute-start | bytes 1327112 | tf_op jit(solution)/shard_map/first_hidden/ppermute | solution.py:242
  83.9 15.6 %collective-permute-start.6 = (bf16[96,1152]{1,0:T(8,128)(2,1)S(1)}, bf16[96,1152]{1,0:T(8,128)(2,1)S(1)}, u32[]{:S(2)}, u32[]{:S(2)}) collective-permute-start(bf16[96,1152]{1,0:T(8,128)(2,1)S(1)} %slice.27), channel_id=1, source_target_pairs={{0,1},{1,2},{2,3},{3,0},{4,5},{5,6},{6,7},{7,4},{8,9},{9,10},{10,1... | collective-permute-start | bytes 663560 | tf_op jit(solution)/shard_map/second_hidden_in/ppermute | solution.py:242
  87.6 13.1 %collective-permute-start.7 = (bf16[96,1152]{1,0:T(8,128)(2,1)S(1)}, bf16[96,1152]{1,0:T(8,128)(2,1)S(1)}, u32[]{:S(2)}, u32[]{:S(2)}) collective-permute-start(bf16[96,1152]{1,0:T(8,128)(2,1)S(1)} %slice.28), channel_id=1, source_target_pairs={{0,3},{1,0},{2,1},{3,2},{4,7},{5,4},{6,5},{7,6},{8,11},{9,8},{10,9... | collective-permute-start | bytes 663560 | tf_op jit(solution)/shard_map/second_hidden_in/ppermute | solution.py:242
  93.4 10.1 %collective-permute-start.2 = (bf16[96,1152]{1,0:T(8,128)(2,1)S(1)}, bf16[96,1152]{1,0:T(8,128)(2,1)S(1)}, u32[]{:S(2)}, u32[]{:S(2)}) collective-permute-start(bf16[96,1152]{1,0:T(8,128)(2,1)S(1)} %slice.24), channel_id=1, source_target_pairs={{0,1},{1,2},{2,3},{3,0},{4,5},{5,6},{6,7},{7,4},{8,9},{9,10},{10,1... | collective-permute-start | bytes 663560 | tf_op jit(solution)/shard_map/first_hidden/ppermute | solution.py:242
  97.1 9.0 %collective-permute-start.3 = (bf16[96,1152]{1,0:T(8,128)(2,1)S(1)}, bf16[96,1152]{1,0:T(8,128)(2,1)S(1)}, u32[]{:S(2)}, u32[]{:S(2)}) collective-permute-start(bf16[96,1152]{1,0:T(8,128)(2,1)S(1)} %slice.25), channel_id=1, source_target_pairs={{0,3},{1,0},{2,1},{3,2},{4,7},{5,4},{6,5},{7,6},{8,11},{9,8},{10,9... | collective-permute-start | bytes 663560 | tf_op jit(solution)/shard_map/first_hidden/ppermute | solution.py:242
  102.3 1.2 copy-start
  118.4 8.2 %copy-start.5 = (s32[128,6]{0,1:T(8,128)S(1)}, s32[128,6]{0,1:T(8,128)}, u32[]{:S(2)}) copy-start(s32[128,6]{0,1:T(8,128)} %param.16) | copy-start | bytes 9220
  118.4 8.2 %copy-start.6 = (f32[128,6]{0,1:T(8,128)S(1)}, f32[128,6]{0,1:T(8,128)}, u32[]{:S(2)}) copy-start(f32[128,6]{0,1:T(8,128)} %param.17) | copy-start | bytes 9220
  118.4 50.9 %all-to-all-start.3 = ((bf16[128,8,768]{2,1,0:T(8,128)(2,1)}), bf16[128,8,768]{2,1,0:T(8,128)(2,1)S(1)}, u32[]{:S(2)}, u32[]{:S(2)}) async-start(bf16[128,8,768]{2,1,0:T(8,128)(2,1)} %bitcast.22), calls=%async_computation.3 | async-start | bytes 3145728 | tf_op jit(solution)/shard_map/finish/all_to_all | solution.py:238
